TPU v7x, 32 devices: a whole 2x2x4 slice. The times are simulated.
32 devices in a mesh: dp: 4 (over y, x), seq: 4 (over z), mp: 2 (over core).
Axes of the slice: x: 2, y: 2, z: 4, core: 2. Of those that a mesh axis runs over, the one named last changes fastest.
Arguments:
- hidden_in: bfloat16 [4, 1024, 1536], P('dp', 'seq'), may hold values from -6 to 6
- positions: int32 [4, 1024], P('dp', 'seq'), may hold values from 0 to 767, as said below
- mixer_gain: bfloat16 [1536], P(('dp', 'seq')), may hold values from 0.5 to 1.5
- mixer_in: bfloat16 [1536, 3, 1536], P(('dp', 'seq'), None, 'mp'), may hold values from -0.15625 to 0.15625
- mixer_taps: bfloat16 [3, 1536], P(None, 'mp'), may hold values from -3 to 3
- mixer_out: bfloat16 [1536, 1536], P(('dp', 'seq'), 'mp'), may hold values from -0.15625 to 0.15625
- first_gain: bfloat16 [1536], P(('dp', 'seq')), may hold values from 0.5 to 1.5
- first_lift: bfloat16 [1536, 2, 6912], P(('dp', 'seq'), None, 'mp'), may hold values from -0.15625 to 0.15625
- first_drop: bfloat16 [1536, 6912], P(('dp', 'seq'), 'mp'), may hold values from -0.078125 to 0.078125
- attend_gain: bfloat16 [1536], P(('dp', 'seq')), may hold values from 0.5 to 1.5
- query_weight: bfloat16 [1536, 1536], P(('dp', 'seq'), 'mp'), may hold values from -0.15625 to 0.15625
- pair_weight: bfloat16 [1536, 2, 512], P(('dp', 'seq'), None, 'mp'), may hold values from -0.15625 to 0.15625
- query_scale: bfloat16 [64], replicated, may hold values from 0.5 to 1.5
- key_scale: bfloat16 [64], replicated, may hold values from 0.5 to 1.5
- attend_out: bfloat16 [1536, 1536], P(('dp', 'seq'), 'mp'), may hold values from -0.625 to 0.625
- second_gain: bfloat16 [1536], P(('dp', 'seq')), may hold values from 0.5 to 1.5
- second_lift: bfloat16 [1536, 2, 6912], P(('dp', 'seq'), None, 'mp'), may hold values from -0.15625 to 0.15625
- second_drop: bfloat16 [1536, 6912], P(('dp', 'seq'), 'mp'), may hold values from -0.078125 to 0.078125
- cotangent: bfloat16 [4, 1024, 1536], P('dp', 'seq'), may hold values from -6 to 6
Outputs:
- result: bfloat16 [4, 1024, 1536], P('dp', 'seq')
- hidden_gradient: float32 [4, 1024, 1536], P('dp', 'seq')
- mixer_gain_gradient: float32 [1536], P(('dp', 'seq'))
- mixer_in_gradient: float32 [1536, 3, 1536], P(('dp', 'seq'), None, 'mp')
- mixer_taps_gradient: float32 [3, 1536], P(None, 'mp')
- mixer_out_gradient: float32 [1536, 1536], P(('dp', 'seq'), 'mp')
- first_gain_gradient: float32 [1536], P(('dp', 'seq'))
- first_lift_gradient: float32 [1536, 2, 6912], P(('dp', 'seq'), None, 'mp')
- first_drop_gradient: float32 [1536, 6912], P(('dp', 'seq'), 'mp')
- attend_gain_gradient: float32 [1536], P(('dp', 'seq'))
- query_weight_gradient: float32 [1536, 1536], P(('dp', 'seq'), 'mp')
- pair_weight_gradient: float32 [1536, 2, 512], P(('dp', 'seq'), None, 'mp')
- query_scale_gradient: float32 [64], replicated
- key_scale_gradient: float32 [64], replicated
- attend_out_gradient: float32 [1536, 1536], P(('dp', 'seq'), 'mp')
- second_gain_gradient: float32 [1536], P(('dp', 'seq'))
- second_lift_gradient: float32 [1536, 2, 6912], P(('dp', 'seq'), None, 'mp')
- second_drop_gradient: float32 [1536, 6912], P(('dp', 'seq'), 'mp')
Inputs may be any that keep to these rules, and one draw needn't show every extreme that they name: In each row three packed documents follow one another, and positions count 0, 1, 2, ... from the start of each: the first and the last have together exactly 256 tokens, each at least one, so the middle one has exactly 768 tokens.
All inputs are finite; a program needn't handle non-finite values.
Results may differ from a plain program's by a relative error of at most 0.035.
Values may be sent and summed in bfloat16 or wider, within the bound.
No kernel may reach another device: no remote copies, remote signals or barrier semaphores. Data moves between devices by JAX's collectives and lax.ppermute only.
A program may use at most 384 MiB of HBM per device.

v0:
```python
import jax
import jax.numpy as jnp
from jax import lax
from jax.sharding import PartitionSpec as P

D = 1536
HD = 64


epsilon = 1e-05
rope_base = 1000000.0


def passed_along(array, axis, by):
    length = lax.axis_size(axis)
    pairs = [(i, i + by) for i in range(length) if 0 <= i + by < length]
    return lax.ppermute(array, axis, pairs)


def rms_scale(values):
    return lax.rsqrt(jnp.mean(values * values, axis=-1, keepdims=True) + epsilon)


def norm_back(back_normed, normed, inverse):
    return inverse * (back_normed - normed * jnp.mean(back_normed * normed, axis=-1, keepdims=True))


def frequencies():
    exponent = jnp.arange(HD // 2, dtype=jnp.float32) * (2.0 / HD)
    return jnp.power(rope_base, -exponent)


def rotate(values, cosines, sine_table):
    middle = values.shape[-1] // 2
    leading = values[..., :middle]
    trailing = values[..., middle:]
    return jnp.concatenate(
        [leading * cosines - trailing * sine_table, trailing * cosines + leading * sine_table],
        axis=-1,
    )


def model_sum(partial_value):
    return lax.psum(partial_value.astype(jnp.bfloat16), "mp").astype(jnp.float32)


def feed_forward(hidden, gain, lift, drop):
    inverse = rms_scale(hidden)
    normed = hidden * inverse
    lowered = (normed * gain.astype(jnp.float32)).astype(jnp.bfloat16)
    gate_up = jnp.einsum("td,dkf->tkf", lowered, lift, preferred_element_type=jnp.float32)
    active = (jax.nn.silu(gate_up[:, 0]) * gate_up[:, 1]).astype(jnp.bfloat16)
    partial_out = jnp.einsum("tf,df->td", active, drop, preferred_element_type=jnp.float32)
    return (hidden + model_sum(partial_out), (inverse, normed, lowered, gate_up, active))


def feed_backward(back_out, stored, gain, lift, drop):
    inverse, normed, lowered, gate_up, active = stored
    back_low = back_out.astype(jnp.bfloat16)
    back_active = jnp.einsum("td,df->tf", back_low, drop, preferred_element_type=jnp.float32)
    drop_term = jnp.einsum("td,tf->df", back_low, active, preferred_element_type=jnp.float32)
    gate_value = gate_up[:, 0]
    up_value = gate_up[:, 1]
    sigmoid_value = jax.nn.sigmoid(gate_value)
    back_gate = back_active * up_value * sigmoid_value * (1.0 + gate_value * (1.0 - sigmoid_value))
    back_up = back_active * gate_value * sigmoid_value
    back_pair = jnp.stack([back_gate, back_up], axis=1).astype(jnp.bfloat16)
    lift_term = jnp.einsum("td,tkf->dkf", lowered, back_pair, preferred_element_type=jnp.float32)
    back_normed = model_sum(
        jnp.einsum("tkf,dkf->td", back_pair, lift, preferred_element_type=jnp.float32)
    )
    gain_term = jnp.sum(back_normed * normed, axis=0)
    back_hidden = back_out + norm_back(back_normed * gain.astype(jnp.float32), normed, inverse)
    return (back_hidden, (gain_term, lift_term, drop_term))


def mixer_forward(hidden, token_order, gain, weight_in, tap_values, weight_out):
    inverse = rms_scale(hidden)
    normed = hidden * inverse
    lowered = (normed * gain.astype(jnp.float32)).astype(jnp.bfloat16)
    gate_parts = jnp.einsum("td,dkc->tkc", lowered, weight_in, preferred_element_type=jnp.float32)
    gated_input = (gate_parts[:, 0] * gate_parts[:, 2]).astype(jnp.bfloat16)
    earlier = passed_along(gated_input[-2:], "seq", 1)
    padded = jnp.concatenate([earlier, gated_input], axis=0).astype(jnp.float32)
    one_back = (token_order >= 1).astype(jnp.float32)[:, None]
    two_back = (token_order >= 2).astype(jnp.float32)[:, None]
    convolved = (
        tap_values[2] * padded[2:]
        + tap_values[1] * padded[1:-1] * one_back
        + tap_values[0] * padded[:-2] * two_back
    )
    gated_output = (gate_parts[:, 1] * convolved).astype(jnp.bfloat16)
    partial_out = jnp.einsum(
        "tc,dc->td", gated_output, weight_out, preferred_element_type=jnp.float32
    )
    stored = (
        inverse,
        normed,
        lowered,
        gate_parts,
        padded,
        convolved,
        gated_output,
        one_back,
        two_back,
    )
    return (hidden + model_sum(partial_out), stored)


def mixer_backward(back_out, stored, gain, weight_in, tap_values, weight_out):
    inverse, normed, lowered, gate_parts, padded, convolved, gated_output, one_back, two_back = (
        stored
    )
    back_low = back_out.astype(jnp.bfloat16)
    back_gated = jnp.einsum("td,dc->tc", back_low, weight_out, preferred_element_type=jnp.float32)
    out_term = jnp.einsum("td,tc->dc", back_low, gated_output, preferred_element_type=jnp.float32)
    back_output_gate = back_gated * convolved
    back_conv = back_gated * gate_parts[:, 1]
    tap_term = jnp.stack(
        [
            jnp.sum(back_conv * padded[:-2] * two_back, axis=0),
            jnp.sum(back_conv * padded[1:-1] * one_back, axis=0),
            jnp.sum(back_conv * padded[2:], axis=0),
        ]
    )
    back_padded = (
        jnp.pad(tap_values[2] * back_conv, ((2, 0), (0, 0)))
        + jnp.pad(tap_values[1] * back_conv * one_back, ((1, 1), (0, 0)))
        + jnp.pad(tap_values[0] * back_conv * two_back, ((0, 2), (0, 0)))
    )
    later = passed_along(back_padded[:2], "seq", -1)
    back_mixed = back_padded[2:] + jnp.pad(later, ((back_conv.shape[0] - 2, 0), (0, 0)))
    back_parts = jnp.stack(
        [back_mixed * gate_parts[:, 2], back_output_gate, back_mixed * gate_parts[:, 0]], axis=1
    ).astype(jnp.bfloat16)
    in_term = jnp.einsum("td,tkc->dkc", lowered, back_parts, preferred_element_type=jnp.float32)
    back_normed = model_sum(
        jnp.einsum("tkc,dkc->td", back_parts, weight_in, preferred_element_type=jnp.float32)
    )
    gain_term = jnp.sum(back_normed * normed, axis=0)
    back_hidden = back_out + norm_back(back_normed * gain.astype(jnp.float32), normed, inverse)
    return (back_hidden, (gain_term, in_term, out_term), tap_term)


def key_slice(key_all, begin_row, key_span, group_count):
    return lax.dynamic_slice_in_dim(key_all, begin_row, key_span, 0).reshape(
        key_span, group_count, HD
    )


def masked_scores(grouped, key_part, begin_row, key_span, row_index, row_first):
    scores = jnp.einsum(
        "grd,kgd->grk", grouped, key_part, preferred_element_type=jnp.float32
    ) * HD ** (-0.5)
    key_index = begin_row + jnp.arange(key_span, dtype=jnp.int32)
    allowed = (key_index[None, :] <= row_index[:, None]) & (
        key_index[None, :] >= row_first[:, None]
    )
    return jnp.where(allowed[None], scores, -1e30)


def attention_core(grouped, key_all, value_all, row_index, row_first, key_span, step_count):
    group_count, row_count = (grouped.shape[0], grouped.shape[1])

    def peak_step(step_index, loop_state):
        running_top, running_total = loop_state
        begin_row = step_index * key_span
        key_part = key_slice(key_all, begin_row, key_span, group_count)
        scores = masked_scores(grouped, key_part, begin_row, key_span, row_index, row_first)
        new_top = jnp.maximum(running_top, jnp.max(scores, axis=-1))
        running_total = running_total * jnp.exp(running_top - new_top) + jnp.sum(
            jnp.exp(scores - new_top[..., None]), axis=-1
        )
        return (new_top, running_total)

    start_state = (
        jnp.full((group_count, row_count), -1e30, jnp.float32),
        jnp.zeros((group_count, row_count), jnp.float32),
    )
    running_top, running_total = lax.fori_loop(0, step_count, peak_step, start_state)
    log_sum = running_top + jnp.log(running_total)

    def value_step(step_index, accumulated):
        begin_row = step_index * key_span
        key_part = key_slice(key_all, begin_row, key_span, group_count)
        value_part = key_slice(value_all, begin_row, key_span, group_count)
        scores = masked_scores(grouped, key_part, begin_row, key_span, row_index, row_first)
        probs_low = jnp.exp(scores - log_sum[..., None]).astype(jnp.bfloat16)
        return accumulated + jnp.einsum(
            "grk,kgd->grd", probs_low, value_part, preferred_element_type=jnp.float32
        )

    attended = lax.fori_loop(
        0, step_count, value_step, jnp.zeros((group_count, row_count, HD), jnp.float32)
    )
    return (attended, log_sum)


def attention_back(
    grouped,
    back_grouped,
    key_all,
    value_all,
    log_sum,
    row_index,
    row_first,
    key_span,
    step_count,
    total_length,
):
    group_count, row_count = (grouped.shape[0], grouped.shape[1])

    def block_terms(step_index):
        begin_row = step_index * key_span
        key_part = key_slice(key_all, begin_row, key_span, group_count)
        value_part = key_slice(value_all, begin_row, key_span, group_count)
        probs = jnp.exp(
            masked_scores(grouped, key_part, begin_row, key_span, row_index, row_first)
            - log_sum[..., None]
        )
        back_probs = jnp.einsum(
            "grd,kgd->grk", back_grouped, value_part, preferred_element_type=jnp.float32
        )
        return (begin_row, key_part, probs, back_probs)

    def dot_step(step_index, row_dot):
        begin_row, key_part, probs, back_probs = block_terms(step_index)
        return row_dot + jnp.sum(probs * back_probs, axis=-1)

    row_dot = lax.fori_loop(
        0, step_count, dot_step, jnp.zeros((group_count, row_count), jnp.float32)
    )

    def back_step(step_index, loop_state):
        back_query, back_keys, back_values = loop_state
        begin_row, key_part, probs, back_probs = block_terms(step_index)
        back_scores = (probs * (back_probs - row_dot[..., None])).astype(jnp.bfloat16)
        back_query = back_query + jnp.einsum(
            "grk,kgd->grd", back_scores, key_part, preferred_element_type=jnp.float32
        ) * HD ** (-0.5)
        key_add = (
            jnp.einsum("grk,grd->kgd", back_scores, grouped, preferred_element_type=jnp.float32)
            * HD ** (-0.5)
        ).reshape(key_span, group_count * HD)
        value_add = jnp.einsum(
            "grk,grd->kgd",
            probs.astype(jnp.bfloat16),
            back_grouped,
            preferred_element_type=jnp.float32,
        ).reshape(key_span, group_count * HD)
        back_keys = lax.dynamic_update_slice_in_dim(
            back_keys,
            lax.dynamic_slice_in_dim(back_keys, begin_row, key_span, 0) + key_add,
            begin_row,
            0,
        )
        back_values = lax.dynamic_update_slice_in_dim(
            back_values,
            lax.dynamic_slice_in_dim(back_values, begin_row, key_span, 0) + value_add,
            begin_row,
            0,
        )
        return (back_query, back_keys, back_values)

    start_state = (
        jnp.zeros((group_count, row_count, HD), jnp.float32),
        jnp.zeros((total_length, group_count * HD), jnp.float32),
        jnp.zeros((total_length, group_count * HD), jnp.float32),
    )
    return lax.fori_loop(0, step_count, back_step, start_state)


def attend_forward(
    hidden, token_order, gain, query_weight, pair_weight, query_gain, key_gain, out_weight
):
    tokens = hidden.shape[0]
    inverse = rms_scale(hidden)
    normed = hidden * inverse
    lowered = (normed * gain.astype(jnp.float32)).astype(jnp.bfloat16)
    query_raw = jnp.einsum("td,dc->tc", lowered, query_weight, preferred_element_type=jnp.float32)
    pair_raw = jnp.einsum("td,dkc->tkc", lowered, pair_weight, preferred_element_type=jnp.float32)
    head_count = query_raw.shape[1] // HD
    group_count = pair_raw.shape[2] // HD
    repeat = head_count // group_count
    query_heads = query_raw.reshape(tokens, head_count, HD)
    key_heads = pair_raw[:, 0].reshape(tokens, group_count, HD)
    angles = token_order.astype(jnp.float32)[:, None] * frequencies()[None, :]
    cosines = jnp.cos(angles)[:, None, :]
    sine_table = jnp.sin(angles)[:, None, :]
    query_inverse = rms_scale(query_heads)
    query_normed = query_heads * query_inverse
    query_rot = rotate(query_normed * query_gain, cosines, sine_table).astype(jnp.bfloat16)
    key_inverse = rms_scale(key_heads)
    key_normed = key_heads * key_inverse
    key_flat = (
        rotate(key_normed * key_gain, cosines, sine_table)
        .astype(jnp.bfloat16)
        .reshape(tokens, group_count * HD)
    )
    value_low = pair_raw[:, 1].astype(jnp.bfloat16)
    key_all, value_all = (
        lax.all_gather(key_flat, "seq", axis=0, tiled=True),
        lax.all_gather(value_low, "seq", axis=0, tiled=True),
    )
    grouped = (
        query_rot.reshape(tokens, group_count, repeat, HD)
        .transpose(1, 2, 0, 3)
        .reshape(group_count, repeat * tokens, HD)
    )
    row_index = jnp.tile(
        lax.axis_index("seq") * tokens + jnp.arange(tokens, dtype=jnp.int32), repeat
    )
    row_first = row_index - jnp.tile(token_order, repeat)
    total_length = tokens * lax.axis_size("seq")
    key_span = min(512, total_length)
    step_count = ((lax.axis_index("seq") + 1) * tokens + key_span - 1) // key_span
    attended, log_sum = attention_core(
        grouped, key_all, value_all, row_index, row_first, key_span, step_count
    )
    attended_low = (
        attended.astype(jnp.bfloat16)
        .reshape(group_count, repeat, tokens, HD)
        .transpose(2, 0, 1, 3)
        .reshape(tokens, head_count * HD)
    )
    partial_out = jnp.einsum(
        "tc,dc->td", attended_low, out_weight, preferred_element_type=jnp.float32
    )
    stored = (
        inverse,
        normed,
        lowered,
        query_inverse,
        query_normed,
        key_inverse,
        key_normed,
        cosines,
        sine_table,
        grouped,
        key_flat,
        value_low,
        key_all,
        value_all,
        log_sum,
        attended_low,
        row_index,
        row_first,
        key_span,
        step_count,
    )
    return (hidden + model_sum(partial_out), stored)


def attend_backward(
    back_out, stored, gain, query_weight, pair_weight, query_gain, key_gain, out_weight
):
    (
        inverse,
        normed,
        lowered,
        query_inverse,
        query_normed,
        key_inverse,
        key_normed,
        cosines,
        sine_table,
        grouped,
        key_flat,
        value_low,
        kept_keys,
        kept_values,
        log_sum,
        attended_low,
        row_index,
        row_first,
        key_span,
        step_count,
    ) = stored
    tokens = back_out.shape[0]
    group_count = grouped.shape[0]
    repeat = grouped.shape[1] // tokens
    head_count = group_count * repeat
    back_low = back_out.astype(jnp.bfloat16)
    back_attended = jnp.einsum(
        "td,dc->tc", back_low, out_weight, preferred_element_type=jnp.float32
    ).astype(jnp.bfloat16)
    out_term = jnp.einsum("td,tc->dc", back_low, attended_low, preferred_element_type=jnp.float32)
    back_grouped = (
        back_attended.reshape(tokens, group_count, repeat, HD)
        .transpose(1, 2, 0, 3)
        .reshape(group_count, repeat * tokens, HD)
    )
    key_all, value_all = (kept_keys, kept_values)
    total_length = tokens * lax.axis_size("seq")
    back_grouped_query, back_key_all, back_value_all = attention_back(
        grouped,
        back_grouped,
        key_all,
        value_all,
        log_sum,
        row_index,
        row_first,
        key_span,
        step_count,
        total_length,
    )
    back_keys_local, back_values_local = (
        lax.psum_scatter(
            back_key_all.astype(jnp.bfloat16), "seq", scatter_dimension=0, tiled=True
        ).astype(jnp.float32),
        lax.psum_scatter(
            back_value_all.astype(jnp.bfloat16), "seq", scatter_dimension=0, tiled=True
        ).astype(jnp.float32),
    )
    back_query_rot = (
        back_grouped_query.reshape(group_count, repeat, tokens, HD)
        .transpose(2, 0, 1, 3)
        .reshape(tokens, head_count, HD)
    )
    back_query_scaled = rotate(back_query_rot, cosines, -sine_table)
    query_scale_term = jnp.sum(back_query_scaled * query_normed, axis=(0, 1))
    back_query = norm_back(back_query_scaled * query_gain, query_normed, query_inverse)
    back_key_scaled = rotate(back_keys_local.reshape(tokens, group_count, HD), cosines, -sine_table)
    key_scale_term = jnp.sum(back_key_scaled * key_normed, axis=(0, 1))
    back_key = norm_back(back_key_scaled * key_gain, key_normed, key_inverse)
    back_query_low = back_query.reshape(tokens, head_count * HD).astype(jnp.bfloat16)
    back_pair = jnp.stack(
        [back_key.reshape(tokens, group_count * HD), back_values_local], axis=1
    ).astype(jnp.bfloat16)
    query_term = jnp.einsum(
        "td,tc->dc", lowered, back_query_low, preferred_element_type=jnp.float32
    )
    pair_term = jnp.einsum("td,tkc->dkc", lowered, back_pair, preferred_element_type=jnp.float32)
    back_partial = jnp.einsum(
        "tc,dc->td", back_query_low, query_weight, preferred_element_type=jnp.float32
    ) + jnp.einsum("tkc,dkc->td", back_pair, pair_weight, preferred_element_type=jnp.float32)
    back_normed = model_sum(back_partial)
    gain_term = jnp.sum(back_normed * normed, axis=0)
    back_hidden = back_out + norm_back(back_normed * gain.astype(jnp.float32), normed, inverse)
    return (
        back_hidden,
        (gain_term, query_term, pair_term, out_term),
        (query_scale_term, key_scale_term),
    )


def body(
    hidden_in,
    positions,
    mixer_gain,
    mixer_in,
    mixer_taps,
    mixer_out,
    first_gain,
    first_lift,
    first_drop,
    attend_gain,
    query_weight,
    pair_weight,
    query_scale,
    key_scale,
    attend_out,
    second_gain,
    second_lift,
    second_drop,
    cotangent,
):
    hidden = hidden_in[0].astype(jnp.float32)
    token_order = positions[0]
    tap_values = mixer_taps.astype(jnp.float32)
    query_gain = query_scale.astype(jnp.float32)
    key_gain = key_scale.astype(jnp.float32)
    mixer_set = (
        lax.all_gather(mixer_gain, ("dp", "seq"), axis=0, tiled=True),
        lax.all_gather(mixer_in, ("dp", "seq"), axis=0, tiled=True),
        lax.all_gather(mixer_out, ("dp", "seq"), axis=0, tiled=True),
        lax.all_gather(first_gain, ("dp", "seq"), axis=0, tiled=True),
        lax.all_gather(first_lift, ("dp", "seq"), axis=0, tiled=True),
        lax.all_gather(first_drop, ("dp", "seq"), axis=0, tiled=True),
    )
    after_mixer, mixer_stored = mixer_forward(
        hidden, token_order, mixer_set[0], mixer_set[1], tap_values, mixer_set[2]
    )
    after_first, first_stored = feed_forward(after_mixer, mixer_set[3], mixer_set[4], mixer_set[5])
    attend_set = (
        lax.all_gather(attend_gain, ("dp", "seq"), axis=0, tiled=True),
        lax.all_gather(query_weight, ("dp", "seq"), axis=0, tiled=True),
        lax.all_gather(pair_weight, ("dp", "seq"), axis=0, tiled=True),
        lax.all_gather(attend_out, ("dp", "seq"), axis=0, tiled=True),
        lax.all_gather(second_gain, ("dp", "seq"), axis=0, tiled=True),
        lax.all_gather(second_lift, ("dp", "seq"), axis=0, tiled=True),
        lax.all_gather(second_drop, ("dp", "seq"), axis=0, tiled=True),
    )
    after_attend, attend_stored = attend_forward(
        after_first,
        token_order,
        attend_set[0],
        attend_set[1],
        attend_set[2],
        query_gain,
        key_gain,
        attend_set[3],
    )
    after_second, second_stored = feed_forward(
        after_attend, attend_set[4], attend_set[5], attend_set[6]
    )
    back_signal = cotangent[0].astype(jnp.float32)
    back_attend, second_terms = feed_backward(
        back_signal, second_stored, attend_set[4], attend_set[5], attend_set[6]
    )
    back_first, attend_terms, scale_terms = attend_backward(
        back_attend,
        attend_stored,
        attend_set[0],
        attend_set[1],
        attend_set[2],
        query_gain,
        key_gain,
        attend_set[3],
    )
    attend_totals = (
        lax.psum_scatter(attend_terms[0], ("dp", "seq"), scatter_dimension=0, tiled=True),
        lax.psum_scatter(attend_terms[1], ("dp", "seq"), scatter_dimension=0, tiled=True),
        lax.psum_scatter(attend_terms[2], ("dp", "seq"), scatter_dimension=0, tiled=True),
        lax.psum_scatter(attend_terms[3], ("dp", "seq"), scatter_dimension=0, tiled=True),
        lax.psum_scatter(second_terms[0], ("dp", "seq"), scatter_dimension=0, tiled=True),
        lax.psum_scatter(second_terms[1], ("dp", "seq"), scatter_dimension=0, tiled=True),
        lax.psum_scatter(second_terms[2], ("dp", "seq"), scatter_dimension=0, tiled=True),
    )
    back_mixer, first_terms = feed_backward(
        back_first, first_stored, mixer_set[3], mixer_set[4], mixer_set[5]
    )
    back_hidden, mixer_terms, tap_term = mixer_backward(
        back_mixer, mixer_stored, mixer_set[0], mixer_set[1], tap_values, mixer_set[2]
    )
    mixer_totals = (
        lax.psum_scatter(mixer_terms[0], ("dp", "seq"), scatter_dimension=0, tiled=True),
        lax.psum_scatter(mixer_terms[1], ("dp", "seq"), scatter_dimension=0, tiled=True),
        lax.psum_scatter(mixer_terms[2], ("dp", "seq"), scatter_dimension=0, tiled=True),
        lax.psum_scatter(first_terms[0], ("dp", "seq"), scatter_dimension=0, tiled=True),
        lax.psum_scatter(first_terms[1], ("dp", "seq"), scatter_dimension=0, tiled=True),
        lax.psum_scatter(first_terms[2], ("dp", "seq"), scatter_dimension=0, tiled=True),
    )
    channel_start = lax.axis_index("mp") * tap_term.shape[1]
    tap_full = lax.dynamic_update_slice_in_dim(
        jnp.zeros((3, D), jnp.float32), tap_term, channel_start, 1
    )
    small_totals = lax.psum((tap_full, scale_terms[0], scale_terms[1]), ("dp", "seq", "mp"))
    tap_gradient = lax.dynamic_slice_in_dim(small_totals[0], channel_start, tap_term.shape[1], 1)
    return (
        after_second.astype(jnp.bfloat16)[None],
        back_hidden[None],
        mixer_totals[0],
        mixer_totals[1],
        tap_gradient,
        mixer_totals[2],
        mixer_totals[3],
        mixer_totals[4],
        mixer_totals[5],
        attend_totals[0],
        attend_totals[1],
        attend_totals[2],
        small_totals[1],
        small_totals[2],
        attend_totals[3],
        attend_totals[4],
        attend_totals[5],
        attend_totals[6],
    )


def solution(mesh):
    return jax.shard_map(
        body,
        mesh=mesh,
        in_specs=(
            P("dp", "seq", None),
            P("dp", "seq"),
            P(("dp", "seq")),
            P(("dp", "seq"), None, "mp"),
            P(None, "mp"),
            P(("dp", "seq"), "mp"),
            P(("dp", "seq")),
            P(("dp", "seq"), None, "mp"),
            P(("dp", "seq"), "mp"),
            P(("dp", "seq")),
            P(("dp", "seq"), "mp"),
            P(("dp", "seq"), None, "mp"),
            P(),
            P(),
            P(("dp", "seq"), "mp"),
            P(("dp", "seq")),
            P(("dp", "seq"), None, "mp"),
            P(("dp", "seq"), "mp"),
            P("dp", "seq", None),
        ),
        out_specs=(
            P("dp", "seq", None),
            P("dp", "seq", None),
            P(("dp", "seq")),
            P(("dp", "seq"), None, "mp"),
            P(None, "mp"),
            P(("dp", "seq"), "mp"),
            P(("dp", "seq")),
            P(("dp", "seq"), None, "mp"),
            P(("dp", "seq"), "mp"),
            P(("dp", "seq")),
            P(("dp", "seq"), "mp"),
            P(("dp", "seq"), None, "mp"),
            P(),
            P(),
            P(("dp", "seq"), "mp"),
            P(("dp", "seq")),
            P(("dp", "seq"), None, "mp"),
            P(("dp", "seq"), "mp"),
        ),
        check_vma=False,
    )
```

profile of v0, /device:TPU:0, one launch (start us, length us, event | category | flops | bytes accessed | tf_op | source)
XLA Modules:
  0.0 4098.7 jit_solution(9082303445352614944)
XLA Ops:
  14.1 80.7 %all-reduce.14 = (bf16[1536]{0:T(1024)(128)(2,1)S(1)}, bf16[1536]{0:T(1024)(128)(2,1)S(1)}, bf16[1536]{0:T(1024)(128)(2,1)S(1)}, bf16[1536]{0:T(1024)(128)(2,1)S(1)}) all-reduce(bf16[1536]{0:T(1024)(128)(2,1)S(1)} %dynamic-update-slice, bf16[1536]{0:T(1024)(128)(2,1)S(1)} %dynamic-update-slice.1, ...), channel_id=1, replica_groups=mesh['dp'=4,'seq'=4,'mp'=2] {'dp','seq'}, use_global_device_ids=true, to_apply=%add.4 | all-reduce | flops 6144 | bytes 24576
  97.6 18.1 all-gather.11.cloned.1.call-done
  127.3 51.8 %all-gather.13.cloned.1.call-done = bf16[1536,768]{1,0:T(8,128)(2,1)} async-done(((bf16[96,768]{1,0:T(8,128)(2,1)}), bf16[1536,768]{1,0:T(8,128)(2,1)}) %all-gather.13.cloned.1.call-update) | async-done | bytes 2359312 | tf_op jit(solution)/shard_map/all_gather | solution.py:476
  184.6 16.2 all-reduce.24.cloned.1.call-done
  202.4 237.3 %all-gather.15.cloned.1.call-done = bf16[1536,2,3456]{2,0,1:T(8,128)(2,1)} async-done(((bf16[96,2,3456]{2,0,1:T(8,128)(2,1)}), bf16[1536,2,3456]{2,0,1:T(8,128)(2,1)}) %all-gather.15.cloned.1.call-update) | async-done | bytes 21233680 | tf_op jit(solution)/shard_map/all_gather | solution.py:478
  453.9 120.5 %all-gather.17.cloned.1.call-done = bf16[1536,3456]{1,0:T(8,128)(2,1)} async-done(((bf16[96,3456]{1,0:T(8,128)(2,1)}), bf16[1536,3456]{1,0:T(8,128)(2,1)}) %all-gather.17.cloned.1.call-update) | async-done | bytes 10616848 | tf_op jit(solution)/shard_map/all_gather | solution.py:479
  602.8 59.5 %all-gather.19.cloned.1.call-done = bf16[1536,2,256]{2,0,1:T(8,128)(2,1)} async-done(((bf16[96,2,256]{2,0,1:T(8,128)(2,1)}), bf16[1536,2,256]{2,0,1:T(8,128)(2,1)}) %all-gather.19.cloned.1.call-update) | async-done | bytes 1572880 | tf_op jit(solution)/shard_map/all_gather | solution.py:488
  665.2 17.1 all_gather.53
  682.3 44.0 %all-gather.21.cloned.1.call-done = bf16[1536,768]{1,0:T(8,128)(2,1)} async-done(((bf16[96,768]{1,0:T(8,128)(2,1)}), bf16[1536,768]{1,0:T(8,128)(2,1)}) %all-gather.21.cloned.1.call-update) | async-done | bytes 2359312 | tf_op jit(solution)/shard_map/all_gather | solution.py:487
  733.2 20.1 all-gather
  760.5 31.4 all-gather.23.cloned.1.call-done
  815.4 237.1 %all-gather.25.cloned.1.call-done = bf16[1536,2,3456]{2,0,1:T(8,128)(2,1)} async-done(((bf16[96,2,3456]{2,0,1:T(8,128)(2,1)}), bf16[1536,2,3456]{2,0,1:T(8,128)(2,1)}) %all-gather.25.cloned.1.call-update) | async-done | bytes 21233680 | tf_op jit(solution)/shard_map/all_gather | solution.py:491
  1052.5 14.9 fusion.131
  1067.4 119.8 %all-gather.27.cloned.1.call-done = bf16[1536,3456]{1,0:T(8,128)(2,1)} async-done(((bf16[96,3456]{1,0:T(8,128)(2,1)}), bf16[1536,3456]{1,0:T(8,128)(2,1)}) %all-gather.27.cloned.1.call-update) | async-done | bytes 10616848 | tf_op jit(solution)/shard_map/all_gather | solution.py:492
  1210.6 17.5 all-reduce.30.cloned.1.call-done
  1245.3 14.9 while.53
  1270.9 38.5 reduce-scatter.14.cloned.1.call-done
  1311.3 20.7 reduce-scatter.16.cloned.1.call-done
  1335.5 17.6 all-reduce.32.cloned.1.call-done
  1421.7 19.8 fusion.62
  1442.2 18.8 fusion.61
  1498.2 20.9 copy.160
  1532.5 41.6 %all-reduce.12 = (f32[3,1536]{1,0:T(4,128)S(1)}, f32[64]{0:T(128)}, f32[64]{0:T(128)}) all-reduce(f32[3,1536]{1,0:T(4,128)S(1)} %maximum_dynamic-update-slice_fusion, f32[64]{0:T(128)S(1)} %reduce_sum.241, f32[64]{0:T(128)S(1)} %reduce_sum.244), channel_id=1, replica_groups=mesh['dp'=4,'seq'=4,'mp'=2] {'dp','seq','mp'}, use_global_device_ids=true, to_apply=%region_39.40 | all-reduce | flops 4736 | bytes 37888 | tf_op jit(solution)/shard_map/psum | solution.py:548
  1576.6 80.5 %all-reduce.13 = (f32[1536]{0:T(1024)S(1)}, f32[1536]{0:T(1024)S(1)}, f32[1536]{0:T(1024)S(1)}, f32[1536]{0:T(1024)S(1)}) all-reduce(f32[1536]{0:T(1024)S(1)} %get-tuple-element.443, f32[1536]{0:T(1024)S(1)} %copy-done.93, f32[1536]{0:T(1024)S(1)} %copy-done.92, ...), channel_id=5, replica_groups=mesh['dp'=4,'seq'=4,'mp'=2] {'dp','seq'}, use_global_device_ids=true, to_apply=%region_34.35.clone | all-reduce | flops 6144 | bytes 49152
  1665.0 524.2 %reduce-scatter.32.cloned.1.call-done = f32[96,2,3456]{2,0,1:T(8,128)} async-done(((f32[1536,2,3456]{2,0,1:T(8,128)}), f32[96,2,3456]{2,0,1:T(8,128)}) %reduce-scatter.32.cloned.1.call-update) | async-done | bytes 2654224 | tf_op jit(solution)/shard_map/reduce_scatter | solution.py:527
  2194.5 604.4 %reduce-scatter.22.cloned.1.call-done = f32[96,2,3456]{2,0,1:T(8,128)} async-done(((f32[1536,2,3456]{2,0,1:T(8,128)}), f32[96,2,3456]{2,0,1:T(8,128)}) %reduce-scatter.22.cloned.1.call-update) | async-done | bytes 2654224 | tf_op jit(solution)/shard_map/reduce_scatter | solution.py:541
  2804.2 137.4 %reduce-scatter.26.cloned.1.call-done = f32[96,768]{1,0:T(8,128)} async-done(((f32[1536,768]{1,0:T(8,128)}), f32[96,768]{1,0:T(8,128)}) %reduce-scatter.26.cloned.1.call-update) | async-done | bytes 294928 | tf_op jit(solution)/shard_map/reduce_scatter | solution.py:523
  2941.6 141.5 %reduce-scatter.30.cloned.1.call-done = f32[96,768]{1,0:T(8,128)} async-done(((f32[1536,768]{1,0:T(8,128)}), f32[96,768]{1,0:T(8,128)}) %reduce-scatter.30.cloned.1.call-update) | async-done | bytes 294928 | tf_op jit(solution)/shard_map/reduce_scatter | solution.py:525
  3083.1 142.3 %reduce-scatter.20.cloned.1.call-done = f32[96,768]{1,0:T(8,128)} async-done(((f32[1536,768]{1,0:T(8,128)}), f32[96,768]{1,0:T(8,128)}) %reduce-scatter.20.cloned.1.call-update) | async-done | bytes 294928 | tf_op jit(solution)/shard_map/reduce_scatter | solution.py:539
  3225.4 226.0 %reduce-scatter.18.cloned.1.call-done = f32[96,3,768]{2,0,1:T(8,128)} async-done(((f32[1536,3,768]{2,0,1:T(8,128)}), f32[96,3,768]{2,0,1:T(8,128)}) %reduce-scatter.18.cloned.1.call-update) | async-done | bytes 884752 | tf_op jit(solution)/shard_map/reduce_scatter | solution.py:538
  3451.4 320.8 %reduce-scatter.34.cloned.1.call-done = f32[96,3456]{1,0:T(8,128)} async-done(((f32[1536,3456]{1,0:T(8,128)}), f32[96,3456]{1,0:T(8,128)}) %reduce-scatter.34.cloned.1.call-update) | async-done | bytes 1327120
  3772.2 319.2 %reduce-scatter.24.cloned.1.call-done = f32[96,3456]{1,0:T(8,128)} async-done(((f32[1536,3456]{1,0:T(8,128)}), f32[96,3456]{1,0:T(8,128)}) %reduce-scatter.24.cloned.1.call-update) | async-done | bytes 1327120 | tf_op jit(solution)/shard_map/reduce_scatter | solution.py:542
  (505 shorter events, 337.4 us)
Async XLA Ops:
  7.2 108.5 %all-gather.11.cloned.1.call-start = ((), (), s32[]{:S(2)}) async-start(), calls=%async_computation.11 | async-start | bytes 7520256 | tf_op jit(solution)/shard_map/all_gather | solution.py:475
  7.9 171.2 %all-gather.13.cloned.1.call-start = ((), (), s32[]{:S(2)}) async-start(), calls=%async_computation.12 | async-start | bytes 2506752 | tf_op jit(solution)/shard_map/all_gather | solution.py:476
  8.7 192.1 %all-reduce.24.cloned.1.call-start = ((), (), s32[]{:S(2)}) async-start(), calls=%async_computation.13 | async-start | bytes 1572864 | tf_op jit(solution)/shard_map/psum | solution.py:44
  121.2 3.9 collective-permute-start
  182.6 257.1 %all-gather.15.cloned.1.call-start = ((), (), s32[]{:S(2)}) async-start(), calls=%async_computation.14 | async-start | bytes 22560768 | tf_op jit(solution)/shard_map/all_gather | solution.py:478
  183.9 390.4 %all-gather.17.cloned.1.call-start = ((), (), s32[]{:S(2)}) async-start(), calls=%async_computation.15 | async-start | bytes 11280384 | tf_op jit(solution)/shard_map/all_gather | solution.py:479
  184.5 415.4 %all-reduce.26.cloned.1.call-start = ((), (), s32[]{:S(2)}) async-start(), calls=%async_computation.16 | async-start | bytes 1572864 | tf_op jit(solution)/shard_map/psum | solution.py:44
  582.3 79.9 %all-gather.19.cloned.1.call-start = ((), (), s32[]{:S(2)}) async-start(), calls=%async_computation.17 | async-start | bytes 1671168 | tf_op jit(solution)/shard_map/all_gather | solution.py:488
  583.1 143.3 %all-gather.21.cloned.1.call-start = ((), (), s32[]{:S(2)}) async-start(), calls=%async_computation.18 | async-start | bytes 2506752 | tf_op jit(solution)/shard_map/all_gather | solution.py:487
  583.8 208.1 %all-gather.23.cloned.1.call-start = ((), (), s32[]{:S(2)}) async-start(), calls=%async_computation.19 | async-start | bytes 2506752 | tf_op jit(solution)/shard_map/all_gather | solution.py:489
  584.5 228.9 %all-reduce.28.cloned.1.call-start = ((), (), s32[]{:S(2)}) async-start(), calls=%async_computation.20 | async-start | bytes 1572864 | tf_op jit(solution)/shard_map/psum | solution.py:44
  795.3 257.2 %all-gather.25.cloned.1.call-start = ((), (), s32[]{:S(2)}) async-start(), calls=%async_computation.21 | async-start | bytes 22560768 | tf_op jit(solution)/shard_map/all_gather | solution.py:491
  797.9 389.3 %all-gather.27.cloned.1.call-start = ((), (), s32[]{:S(2)}) async-start(), calls=%async_computation.22 | async-start | bytes 11280384 | tf_op jit(solution)/shard_map/all_gather | solution.py:492
  798.5 429.7 %all-reduce.30.cloned.1.call-start = ((), (), s32[]{:S(2)}) async-start(), calls=%async_computation.23 | async-start | bytes 1572864 | tf_op jit(solution)/shard_map/psum | solution.py:44
  798.7 431.9 %copy-start.68 = (f32[1536]{0:T(1024)}, f32[1536]{0:T(1024)S(1)}, u32[]{:S(2)}) copy-start(f32[1536]{0:T(1024)S(1)} %convert_element_type.224) | copy-start | bytes 18436
  815.4 415.2 %copy-start.2 = (f32[256,1536]{1,0:T(8,128)}, f32[256,1536]{1,0:T(8,128)S(1)}, u32[]{:S(2)}) copy-start(f32[256,1536]{1,0:T(8,128)S(1)} %get-tuple-element.543) | copy-start | bytes 4718596
  815.4 415.2 %copy-start.82 = (f32[256]{0:T(256)}, f32[256]{0:T(256)S(1)}, u32[]{:S(2)}) copy-start(f32[256]{0:T(256)S(1)} %add_rsqrt_fusion.2) | copy-start | bytes 3076
  1210.6 98.8 %reduce-scatter.14.cloned.1.call-start = ((), (), s32[]{:S(2)}) async-start(), calls=%async_computation.24 | async-start | bytes 655360 | tf_op jit(solution)/shard_map/reduce_scatter | solution.py:408
  1262.4 69.6 %reduce-scatter.16.cloned.1.call-start = ((), (), s32[]{:S(2)}) async-start(), calls=%async_computation.25 | async-start | bytes 655360 | tf_op jit(solution)/shard_map/reduce_scatter | solution.py:411
  1268.5 84.6 %all-reduce.32.cloned.1.call-start = ((), (), s32[]{:S(2)}) async-start(), calls=%async_computation.26 | async-start | bytes 1572864 | tf_op jit(solution)/shard_map/psum | solution.py:44
  1335.5 63.4 %all-reduce.34.cloned.1.call-start = ((), (), s32[]{:S(2)}) async-start(), calls=%async_computation.27 | async-start | bytes 1572864 | tf_op jit(solution)/shard_map/psum | solution.py:44
  1378.3 196.4 %all-reduce.36.cloned.1.call-start = ((), (), s32[]{:S(2)}) async-start(), calls=%async_computation.37 | async-start | bytes 3145728 | tf_op jit(solution)/shard_map/psum | solution.py:44
  1407.1 5.8 collective-permute-start.1
  1416.9 246.3 %reduce-scatter.28.cloned.1.call-start = ((), (), s32[]{:S(2)}) async-start(), calls=%async_computation.33 | async-start | bytes 3342336 | tf_op jit(solution)/shard_map/reduce_scatter | solution.py:524
  1420.3 768.9 %reduce-scatter.32.cloned.1.call-start = ((), (), s32[]{:S(2)}) async-start(), calls=%async_computation.35 | async-start | bytes 45121536 | tf_op jit(solution)/shard_map/reduce_scatter | solution.py:527
  1441.5 1357.3 %reduce-scatter.22.cloned.1.call-start = ((), (), s32[]{:S(2)}) async-start(), calls=%async_computation.30 | async-start | bytes 45121536 | tf_op jit(solution)/shard_map/reduce_scatter | solution.py:541
  1461.0 1480.5 %reduce-scatter.26.cloned.1.call-start = ((), (), s32[]{:S(2)}) async-start(), calls=%async_computation.32 | async-start | bytes 5013504 | tf_op jit(solution)/shard_map/reduce_scatter | solution.py:523
  1465.2 1617.9 %reduce-scatter.30.cloned.1.call-start = ((), (), s32[]{:S(2)}) async-start(), calls=%async_computation.34 | async-start | bytes 5013504 | tf_op jit(solution)/shard_map/reduce_scatter | solution.py:525
  1470.6 1754.8 %reduce-scatter.20.cloned.1.call-start = ((), (), s32[]{:S(2)}) async-start(), calls=%async_computation.29 | async-start | bytes 5013504 | tf_op jit(solution)/shard_map/reduce_scatter | solution.py:539
  1476.1 1975.4 %reduce-scatter.18.cloned.1.call-start = ((), (), s32[]{:S(2)}) async-start(), calls=%async_computation.28 | async-start | bytes 15040512 | tf_op jit(solution)/shard_map/reduce_scatter | solution.py:538
  1484.4 2287.8 %reduce-scatter.34.cloned.1.call-start = ((), (), s32[]{:S(2)}) async-start(), calls=%async_computation.36 | async-start | bytes 22560768
  1519.2 2572.2 %reduce-scatter.24.cloned.1.call-start = ((), (), s32[]{:S(2)}) async-start(), calls=%async_computation.31 | async-start | bytes 22560768 | tf_op jit(solution)/shard_map/reduce_scatter | solution.py:542
  (119 other events, 3165.1 us)
Sparse Core Ops, SparseCore 0:
  10.9 104.7 all-gather.10
  118.5 60.6 all-gather.12
  182.7 18.0 all-reduce.23
  204.5 235.1 all-gather.14
  442.7 131.6 all-gather.16
  582.4 17.3 all-reduce.25
  603.1 59.0 all-gather.18
  665.0 61.2 all-gather.20
  729.1 62.7 all-gather.22
  795.4 18.0 all-reduce.27
  817.3 235.1 all-gather.24
  1055.5 131.6 all-gather.26
  1210.7 17.4 all-reduce.29
  1262.5 46.8 reduce-scatter.13
  1312.1 19.8 reduce-scatter.15
  1335.6 17.4 all-reduce.31
  1378.4 20.3 all-reduce.33
  1417.0 20.7 all-reduce.35
  1443.5 131.9 reduce-scatter.27
  1582.7 606.4 reduce-scatter.31
  2195.4 603.3 reduce-scatter.21
  2805.4 136.1 reduce-scatter.25
  2947.3 135.7 reduce-scatter.29
  3089.5 135.8 reduce-scatter.19
  3231.8 219.6 reduce-scatter.17
  3458.9 313.2 reduce-scatter.33
  3778.6 312.7 reduce-scatter.23
where the time goes:
time: 4110 us; the launch traced here: 4100 us
  waiting for transfers between devices  3490 us (85%)
  blocking collectives  240 us (6%)
  matrix products  223 us (5%)
  local copies, waits for them, and re-layouts  77 us (2%)
    reduce_scatter x1, waiting for transfers between devices, body(): lax.psum_scatter(first_terms[1], ('dp', 'seq'), scatter_dimension=0, tile...  604 us
    reduce_scatter x1, waiting for transfers between devices, body(): lax.psum_scatter(second_terms[1], ('dp', 'seq'), scatter_dimension=0, til...  524 us
    unnamed x28, waiting for transfers between devices  325 us
    reduce_scatter x1, waiting for transfers between devices, body(): lax.psum_scatter(first_terms[2], ('dp', 'seq'), scatter_dimension=0, tile...  319 us
    all_gather x1, waiting for transfers between devices, body(): lax.all_gather(first_lift, ('dp', 'seq'), axis=0, tiled=True)  237 us
    all_gather x1, waiting for transfers between devices, body(): lax.all_gather(second_lift, ('dp', 'seq'), axis=0, tiled=True)  237 us
    reduce_scatter x1, waiting for transfers between devices, body(): lax.psum_scatter(mixer_terms[1], ('dp', 'seq'), scatter_dimension=0, tile...  226 us
    unnamed x2, blocking collectives  161 us
  transfers between devices with their start and end apart: 29, of which 27 were waited for; matrix products, arithmetic and copies ran while one was open for 5% of the time, Pallas kernels for 0%

commit v1 on v0

v1 whole, which is shorter than its diff:
```python
import jax
import jax.numpy as jnp
from jax import lax
from jax.sharding import PartitionSpec as P

HD = 64
GRID = ("dp", "seq")
SEATS = ((0, 0), (0, 1), (1, 0), (1, 1))

epsilon = 1e-05
rope_base = 1000000.0
bf16 = jnp.bfloat16
f32 = jnp.float32


def rms_scale(values):
    return lax.rsqrt(jnp.mean(values * values, axis=-1, keepdims=True) + epsilon)


def norm_back(back_normed, normed, inverse):
    return inverse * (back_normed - normed * jnp.mean(back_normed * normed, axis=-1, keepdims=True))


def frequencies():
    exponent = jnp.arange(HD // 2, dtype=f32) * (2.0 / HD)
    return jnp.power(rope_base, -exponent)


def rotate(values, cosines, sine_table):
    middle = values.shape[-1] // 2
    leading = values[..., :middle]
    trailing = values[..., middle:]
    return jnp.concatenate(
        [leading * cosines - trailing * sine_table, trailing * cosines + leading * sine_table],
        axis=-1,
    )


def dot(pattern, first, second):
    return jnp.einsum(pattern, first, second, preferred_element_type=f32)


class Place:
    def __init__(self):
        dp, seq = lax.axis_index("dp"), lax.axis_index("seq")
        self.core = lax.axis_index("mp")
        self.u, self.v = dp // 2, dp % 2
        self.g, self.w = seq // 2, seq % 2
        self.seat = 2 * self.v + self.w
        self.rank = dp * lax.axis_size("seq") + seq


def far_groups():
    return lax.axis_size("seq") // 2


def swap(array, dp_mask, seq_mask):
    dps, seqs = lax.axis_size("dp"), lax.axis_size("seq")
    pairs = [
        (d * seqs + s, (d ^ dp_mask) * seqs + (s ^ seq_mask)) for d in range(dps) for s in range(seqs)
    ]
    return lax.ppermute(array, GRID, pairs)


def swap_core(array):
    return lax.ppermute(array, "mp", [(0, 1), (1, 0)])


def shift_groups(array, by, cyclic=False):
    seqs = lax.axis_size("seq")
    if cyclic:
        pairs = [(s, (s + 2 * by) % seqs) for s in range(seqs)]
    else:
        pairs = [(s, s + 2 * by) for s in range(seqs) if 0 <= s + 2 * by < seqs]
    return lax.ppermute(array, "seq", pairs)


def flip_if(bit, array, axis):
    return jnp.where(bit == 1, jnp.flip(array, axis), array)


def gather_tokens(own):
    mine = jnp.stack([own] + [swap(own, v, w) for v, w in SEATS[1:]])
    other = swap_core(mine)
    return jnp.stack([mine, other])


def gather_flat(own):
    return gather_tokens(own).reshape(-1, own.shape[-1])


def scatter_tokens(partial_sum):
    rows = partial_sum.shape[0] // 8
    split = partial_sum.reshape(2, 4, rows, partial_sum.shape[-1])
    both = split[0] + swap_core(split[1].astype(bf16)).astype(f32)
    low = both.astype(bf16)
    total = both[0]
    for seat in range(1, 4):
        total = total + swap(low[seat], *SEATS[seat]).astype(f32)
    return total


def in_order(place, flat):
    columns = flat.shape[-1]
    rows = flat.shape[0] // 8
    split = flat.reshape(2, 2, 2, rows, columns)
    split = flip_if(place.w, flip_if(place.core, split, 0), 2)
    return split.transpose(1, 2, 0, 3, 4).reshape(2, 4 * rows, columns)


def own_order(place, ordered):
    columns = ordered.shape[-1]
    rows = ordered.shape[1] // 4
    split = ordered.reshape(2, 2, 2, rows, columns).transpose(2, 0, 1, 3, 4)
    split = flip_if(place.w, flip_if(place.core, split, 0), 2)
    return split.reshape(8 * rows, columns)


def spread_weights(place, packed):
    far = far_groups()
    lead, rows, columns = packed.shape[1:-2], packed.shape[-2], packed.shape[-1]
    plain = (0,) * len(lead)

    def chunk(seat):
        return lax.dynamic_index_in_dim(packed, place.seat ^ seat, 0, keepdims=False)

    near = jnp.zeros(lead + (2, 2, rows, columns), packed.dtype)
    for seat, (v, w) in enumerate(SEATS):
        piece = chunk(seat)
        if seat:
            piece = swap(piece, v, w)
        near = lax.dynamic_update_slice(
            near, piece.reshape(lead + (1, 1, rows, columns)), plain + (place.v ^ v, place.w ^ w, 0, 0)
        )
    whole = jnp.zeros(lead + (2, 2, far, 2, rows, columns), packed.dtype)
    for step in range(far):
        piece = shift_groups(near, step, cyclic=True) if step else near
        opposite = swap(piece, 2, 0)
        group = (place.g - step) % far
        for u, part in ((place.u, piece), (place.u ^ 1, opposite)):
            whole = lax.dynamic_update_slice(
                whole,
                part.reshape(lead + (1, 2, 1, 2, rows, columns)),
                plain + (u, 0, group, 0, 0, 0),
            )
    return whole.reshape(lead + (4 * far * 2 * rows, columns))


def collect_gradient(place, gradient):
    far = far_groups()
    lead, columns = gradient.shape[:-2], gradient.shape[-1]
    rows = gradient.shape[-2] // (8 * far)
    at = len(lead)
    split = gradient.reshape(lead + (2, 2, far, 2, rows, columns))

    def pick(array, index, axis):
        return lax.dynamic_index_in_dim(array, index, axis, keepdims=False)

    send = pick(split, place.u ^ 1, at).astype(bf16)
    half = pick(split, place.u, at).astype(f32) + swap(send, 2, 0).astype(f32)
    part = pick(half, place.g, at + 1)
    for step in range(1, far):
        send = pick(half, (place.g + step) % far, at + 1).astype(bf16)
        part = part + shift_groups(send, step, cyclic=True).astype(f32)
    part = part.astype(bf16)
    pieces = []
    for v, w in SEATS:
        piece = pick(pick(part, place.v ^ v, at), place.w ^ w, at)
        pieces.append(swap(piece, v, w) if v or w else piece)
    seats = jnp.stack(pieces).reshape((2, 2) + lead + (rows, columns))
    seats = flip_if(place.w, flip_if(place.v, seats, 0), 1)
    return seats.reshape((4,) + lead + (rows, columns)).astype(f32)


def per_seat(array):
    split = array.reshape(array.shape[:-1] + (4, array.shape[-1] // 4))
    return jnp.moveaxis(split, -2, 0)


def all_seats(array):
    split = jnp.moveaxis(array, 0, -2)
    return split.reshape(split.shape[:-2] + (-1,))


def pack_mixer(weight_in, weight_out):
    rows = weight_in.shape[0]
    return jnp.concatenate([per_seat(weight_in).reshape(4, rows, -1), per_seat(weight_out)], axis=-1)


def pack_attend(query_weight, pair_weight, out_weight):
    rows = query_weight.shape[0]
    return jnp.concatenate(
        [per_seat(query_weight), per_seat(pair_weight).reshape(4, rows, -1), per_seat(out_weight)], axis=-1
    )


def pack_forward(lift, drop):
    return jnp.concatenate([per_seat(lift).transpose(0, 2, 1, 3), per_seat(drop)[:, None]], axis=1)


def lowered_norm(hidden, gain):
    inverse = rms_scale(hidden)
    normed = hidden * inverse
    return inverse, normed, (normed * gain).astype(bf16)


def feed_forward(hidden, gain, weights):
    inverse, normed, lowered = lowered_norm(hidden, gain)
    tokens = gather_flat(lowered)
    gate = dot("td,df->tf", tokens, weights[0])
    up = dot("td,df->tf", tokens, weights[1])
    active = (jax.nn.silu(gate) * up).astype(bf16)
    out = scatter_tokens(dot("tf,df->td", active, weights[2]))
    return hidden + out, (inverse, normed, tokens, gate, up, active)


def feed_backward(back_out, stored, gain, weights):
    inverse, normed, tokens, gate, up, active = stored
    back_tokens = gather_flat(back_out.astype(bf16))
    back_active = dot("td,df->tf", back_tokens, weights[2])
    sigmoid_value = jax.nn.sigmoid(gate)
    back_gate = (
        back_active * up * sigmoid_value * (1.0 + gate * (1.0 - sigmoid_value))
    ).astype(bf16)
    back_up = (back_active * gate * sigmoid_value).astype(bf16)
    back_normed = scatter_tokens(
        dot("tf,df->td", back_gate, weights[0]) + dot("tf,df->td", back_up, weights[1])
    )
    drop_term = dot("td,tf->df", back_tokens, active)
    lift_terms = (dot("td,tf->df", tokens, back_gate), dot("td,tf->df", tokens, back_up))
    gain_term = jnp.sum(back_normed * normed, axis=0)
    back_hidden = back_out + norm_back(back_normed * gain, normed, inverse)
    return back_hidden, gain_term, jnp.stack(lift_terms + (drop_term,)).astype(bf16)


def mixer_forward(place, hidden, order, gain, weights, taps):
    inverse, normed, lowered = lowered_norm(hidden, gain)
    tokens = gather_flat(lowered)
    channels = taps.shape[1]
    parts = in_order(place, dot("td,dc->tc", tokens, weights[:, : 3 * channels]))
    gate_in, gate_out, value = (parts[..., i * channels : (i + 1) * channels] for i in range(3))
    mixed = (gate_in * value).astype(bf16)
    earlier = shift_groups(mixed[:, -2:], 1)
    padded = jnp.concatenate([earlier, mixed], axis=1).astype(f32)
    one_back = (order >= 1).astype(f32)[..., None]
    two_back = (order >= 2).astype(f32)[..., None]
    convolved = (
        taps[2] * padded[:, 2:] + taps[1] * padded[:, 1:-1] * one_back + taps[0] * padded[:, :-2] * two_back
    )
    gated = own_order(place, (gate_out * convolved).astype(bf16))
    out = scatter_tokens(dot("tc,dc->td", gated, weights[:, 3 * channels :]))
    stored = (inverse, normed, tokens, gate_in, gate_out, value, padded, convolved, gated, one_back, two_back)
    return hidden + out, stored


def mixer_backward(place, back_out, stored, gain, weights, taps):
    inverse, normed, tokens, gate_in, gate_out, value, padded, convolved, gated, one_back, two_back = stored
    channels = taps.shape[1]
    back_tokens = gather_flat(back_out.astype(bf16))
    back_gated = in_order(place, dot("td,dc->tc", back_tokens, weights[:, 3 * channels :]))
    out_term = dot("td,tc->dc", back_tokens, gated)
    back_conv = back_gated * gate_out
    tap_term = jnp.stack(
        [
            jnp.sum(back_conv * padded[:, :-2] * two_back, axis=(0, 1)),
            jnp.sum(back_conv * padded[:, 1:-1] * one_back, axis=(0, 1)),
            jnp.sum(back_conv * padded[:, 2:], axis=(0, 1)),
        ]
    )
    back_padded = (
        jnp.pad(taps[2] * back_conv, ((0, 0), (2, 0), (0, 0)))
        + jnp.pad(taps[1] * back_conv * one_back, ((0, 0), (1, 1), (0, 0)))
        + jnp.pad(taps[0] * back_conv * two_back, ((0, 0), (0, 2), (0, 0)))
    )
    later = shift_groups(back_padded[:, :2], -1)
    back_mixed = back_padded[:, 2:] + jnp.pad(later, ((0, 0), (back_conv.shape[1] - 2, 0), (0, 0)))
    back_parts = own_order(
        place,
        jnp.concatenate([back_mixed * value, back_gated * convolved, back_mixed * gate_in], axis=-1).astype(bf16),
    )
    back_normed = scatter_tokens(dot("tc,dc->td", back_parts, weights[:, : 3 * channels]))
    in_term = dot("td,tc->dc", tokens, back_parts)
    gain_term = jnp.sum(back_normed * normed, axis=0)
    back_hidden = back_out + norm_back(back_normed * gain, normed, inverse)
    return back_hidden, gain_term, jnp.concatenate([in_term, out_term], axis=-1).astype(bf16), tap_term


def attend_forward(place, hidden, order, gain, weights, query_gain, key_gain):
    inverse, normed, lowered = lowered_norm(hidden, gain)
    tokens = gather_flat(lowered)
    heads = weights.shape[1] * 3 // 8 // HD
    groups = weights.shape[1] // 8 // HD
    repeat = heads // groups
    mixed = in_order(place, dot("td,dc->tc", tokens, weights[:, : (heads + 2 * groups) * HD]))
    sequences, count = mixed.shape[:2]
    query_heads = mixed[..., : heads * HD].reshape(sequences, count, heads, HD)
    key_heads = mixed[..., heads * HD : (heads + groups) * HD].reshape(sequences, count, groups, HD)
    value_low = mixed[..., (heads + groups) * HD :].astype(bf16)
    angles = order.astype(f32)[..., None] * frequencies()
    cosines, sines = jnp.cos(angles)[:, :, None, :], jnp.sin(angles)[:, :, None, :]
    query_inverse = rms_scale(query_heads)
    query_normed = query_heads * query_inverse
    query_rot = rotate(query_normed * query_gain, cosines, sines).astype(bf16)
    key_inverse = rms_scale(key_heads)
    key_normed = key_heads * key_inverse
    key_rot = rotate(key_normed * key_gain, cosines, sines).astype(bf16)
    pair = jnp.concatenate([key_rot.reshape(sequences, count, groups * HD), value_low], axis=-1)
    slots = jnp.concatenate([shift_groups(pair, i) if i else pair for i in range(far_groups())], axis=1)
    keys = slots[..., : groups * HD].reshape(sequences, -1, groups, HD)
    values = slots[..., groups * HD :].reshape(sequences, -1, groups, HD)
    grouped = query_rot.reshape(sequences, count, groups, repeat, HD)
    row_index = place.g * count + jnp.arange(count, dtype=jnp.int32)
    row_first = row_index[None] - order
    key_index = jnp.concatenate(
        [(place.g - i) * count + jnp.arange(count, dtype=jnp.int32) for i in range(far_groups())]
    )
    allowed = (key_index[None, None, :] <= row_index[None, :, None]) & (
        key_index[None, None, :] >= row_first[:, :, None]
    )
    scores = dot("vqgrd,vkgd->vgrqk", grouped, keys) * HD**-0.5
    scores = jnp.where(allowed[:, None, None], scores, -1e30)
    probs = jnp.exp(scores - jnp.max(scores, axis=-1, keepdims=True))
    probs = probs / jnp.sum(probs, axis=-1, keepdims=True)
    attended = dot("vgrqk,vkgd->vqgrd", probs.astype(bf16), values).astype(bf16)
    attended = own_order(place, attended.reshape(sequences, count, heads * HD))
    out = scatter_tokens(dot("tc,dc->td", attended, weights[:, (heads + 2 * groups) * HD :]))
    stored = (
        inverse,
        normed,
        tokens,
        query_inverse,
        query_normed,
        key_inverse,
        key_normed,
        cosines,
        sines,
        grouped,
        keys,
        values,
        probs,
        attended,
    )
    return hidden + out, stored


def attend_backward(place, back_out, stored, gain, weights, query_gain, key_gain):
    (
        inverse,
        normed,
        tokens,
        query_inverse,
        query_normed,
        key_inverse,
        key_normed,
        cosines,
        sines,
        grouped,
        keys,
        values,
        probs,
        attended,
    ) = stored
    sequences, count, groups, repeat = grouped.shape[:4]
    heads = groups * repeat
    inner = (heads + 2 * groups) * HD
    back_tokens = gather_flat(back_out.astype(bf16))
    back_attended = in_order(place, dot("td,dc->tc", back_tokens, weights[:, inner:]).astype(bf16))
    back_grouped = back_attended.reshape(sequences, count, groups, repeat, HD)
    out_term = dot("td,tc->dc", back_tokens, attended)
    back_probs = dot("vqgrd,vkgd->vgrqk", back_grouped, values)
    row_dot = jnp.sum(probs * back_probs, axis=-1, keepdims=True)
    back_scores = (probs * (back_probs - row_dot)).astype(bf16)
    back_query_rot = dot("vgrqk,vkgd->vqgrd", back_scores, keys) * HD**-0.5
    back_keys = dot("vgrqk,vqgrd->vkgd", back_scores, grouped) * HD**-0.5
    back_values = dot("vgrqk,vqgrd->vkgd", probs.astype(bf16), back_grouped)
    back_slots = jnp.concatenate(
        [
            back_keys.reshape(sequences, -1, count, groups * HD),
            back_values.reshape(sequences, -1, count, groups * HD),
        ],
        axis=-1,
    )
    back_pair = back_slots[:, 0]
    for i in range(1, far_groups()):
        back_pair = back_pair + shift_groups(back_slots[:, i].astype(bf16), -i).astype(f32)
    back_query_scaled = rotate(back_query_rot.reshape(sequences, count, heads, HD), cosines, -sines)
    query_scale_term = jnp.sum(back_query_scaled * query_normed, axis=(0, 1, 2))
    back_query = norm_back(back_query_scaled * query_gain, query_normed, query_inverse)
    back_key_rot = back_pair[..., : groups * HD].reshape(sequences, count, groups, HD)
    back_key_scaled = rotate(back_key_rot, cosines, -sines)
    key_scale_term = jnp.sum(back_key_scaled * key_normed, axis=(0, 1, 2))
    back_key = norm_back(back_key_scaled * key_gain, key_normed, key_inverse)
    back_mixed = jnp.concatenate(
        [
            back_query.reshape(sequences, count, heads * HD),
            back_key.reshape(sequences, count, groups * HD),
            back_pair[..., groups * HD :],
        ],
        axis=-1,
    ).astype(bf16)
    back_mixed = own_order(place, back_mixed)
    back_normed = scatter_tokens(dot("tc,dc->td", back_mixed, weights[:, :inner]))
    in_term = dot("td,tc->dc", tokens, back_mixed)
    gain_term = jnp.sum(back_normed * normed, axis=0)
    back_hidden = back_out + norm_back(back_normed * gain, normed, inverse)
    return (
        back_hidden,
        gain_term,
        jnp.concatenate([in_term, out_term], axis=-1).astype(bf16),
        (query_scale_term, key_scale_term),
    )


def grid_total(array):
    for mask in (1, 2):
        array = array + swap(array, mask, 0)
    mask = 1
    while mask < lax.axis_size("seq"):
        array = array + swap(array, 0, mask)
        mask *= 2
    return array


def body(
    hidden_in,
    positions,
    mixer_gain,
    mixer_in,
    mixer_taps,
    mixer_out,
    first_gain,
    first_lift,
    first_drop,
    attend_gain,
    query_weight,
    pair_weight,
    query_scale,
    key_scale,
    attend_out,
    second_gain,
    second_lift,
    second_drop,
    cotangent,
):
    place = Place()
    model = hidden_in.shape[-1]
    share = hidden_in.shape[1] // 2
    own_rows = place.core * share
    hidden = lax.dynamic_slice_in_dim(hidden_in[0], own_rows, share).astype(f32)
    signal = lax.dynamic_slice_in_dim(cotangent[0], own_rows, share).astype(f32)
    order = lax.dynamic_slice_in_dim(positions[0], own_rows, share)
    order = in_order(place, gather_flat(order[:, None]))[..., 0]
    gain_rows = mixer_gain.shape[0]
    gains = jnp.stack([mixer_gain, first_gain, attend_gain, second_gain]).astype(f32)
    gains = grid_total(
        lax.dynamic_update_slice_in_dim(jnp.zeros((4, model), f32), gains, place.rank * gain_rows, 1)
    )
    query_gain, key_gain = query_scale.astype(f32), key_scale.astype(f32)
    channels = mixer_taps.shape[1] // 4
    taps = lax.dynamic_slice_in_dim(mixer_taps, place.seat * channels, channels, 1).astype(f32)

    mixer_weights = spread_weights(place, pack_mixer(mixer_in, mixer_out))
    first_weights = spread_weights(place, pack_forward(first_lift, first_drop))
    attend_weights = spread_weights(place, pack_attend(query_weight, pair_weight, attend_out))
    second_weights = spread_weights(place, pack_forward(second_lift, second_drop))

    hidden, mixer_stored = mixer_forward(place, hidden, order, gains[0], mixer_weights, taps)
    hidden, first_stored = feed_forward(hidden, gains[1], first_weights)
    hidden, attend_stored = attend_forward(
        place, hidden, order, gains[2], attend_weights, query_gain, key_gain
    )
    hidden, second_stored = feed_forward(hidden, gains[3], second_weights)

    back, second_gain_term, second_term = feed_backward(signal, second_stored, gains[3], second_weights)
    second_total = collect_gradient(place, second_term)
    back, attend_gain_term, attend_term, scale_terms = attend_backward(
        place, back, attend_stored, gains[2], attend_weights, query_gain, key_gain
    )
    attend_total = collect_gradient(place, attend_term)
    back, first_gain_term, first_term = feed_backward(back, first_stored, gains[1], first_weights)
    first_total = collect_gradient(place, first_term)
    back, mixer_gain_term, mixer_term, tap_term = mixer_backward(
        place, back, mixer_stored, gains[0], mixer_weights, taps
    )
    mixer_total = collect_gradient(place, mixer_term)

    small = jnp.concatenate(
        [mixer_gain_term, first_gain_term, attend_gain_term, second_gain_term, scale_terms[0], scale_terms[1]]
    )
    small = small + swap_core(small)
    tap_full = lax.dynamic_update_slice_in_dim(
        jnp.zeros((3, mixer_taps.shape[1]), f32), tap_term, place.seat * channels, 1
    )
    small = grid_total(jnp.concatenate([small, tap_full.reshape(-1)]))
    gain_totals = lax.dynamic_slice_in_dim(
        small[: 4 * model].reshape(4, model), place.rank * gain_rows, gain_rows, 1
    )
    scale_totals = small[4 * model : 4 * model + 2 * HD].reshape(2, HD)
    tap_total = small[4 * model + 2 * HD :].reshape(tap_full.shape)

    def both_cores(own):
        return flip_if(place.core, jnp.stack([own, swap_core(own)]), 0).reshape(1, 2 * share, model)

    rows = mixer_in.shape[0]
    in_columns = 3 * channels
    inner = attend_total.shape[-1] - query_weight.shape[1] // 4
    queries = query_weight.shape[1] // 4
    return (
        both_cores(hidden.astype(bf16)),
        both_cores(back),
        gain_totals[0],
        all_seats(mixer_total[..., :in_columns].reshape(4, rows, 3, channels)),
        tap_total,
        all_seats(mixer_total[..., in_columns:]),
        gain_totals[1],
        all_seats(first_total[:, :2].transpose(0, 2, 1, 3)),
        all_seats(first_total[:, 2]),
        gain_totals[2],
        all_seats(attend_total[..., :queries]),
        all_seats(attend_total[..., queries:inner].reshape(4, rows, 2, -1)),
        scale_totals[0],
        scale_totals[1],
        all_seats(attend_total[..., inner:]),
        gain_totals[3],
        all_seats(second_total[:, :2].transpose(0, 2, 1, 3)),
        all_seats(second_total[:, 2]),
    )


def solution(mesh):
    grid = ("dp", "seq")
    return jax.shard_map(
        body,
        mesh=mesh,
        in_specs=(
            P("dp", "seq", None),
            P("dp", "seq"),
            P(grid),
            P(grid, None, "mp"),
            P(None, "mp"),
            P(grid, "mp"),
            P(grid),
            P(grid, None, "mp"),
            P(grid, "mp"),
            P(grid),
            P(grid, "mp"),
            P(grid, None, "mp"),
            P(),
            P(),
            P(grid, "mp"),
            P(grid),
            P(grid, None, "mp"),
            P(grid, "mp"),
            P("dp", "seq", None),
        ),
        out_specs=(
            P("dp", "seq", None),
            P("dp", "seq", None),
            P(grid),
            P(grid, None, "mp"),
            P(None, "mp"),
            P(grid, "mp"),
            P(grid),
            P(grid, None, "mp"),
            P(grid, "mp"),
            P(grid),
            P(grid, "mp"),
            P(grid, None, "mp"),
            P(),
            P(),
            P(grid, "mp"),
            P(grid),
            P(grid, None, "mp"),
            P(grid, "mp"),
        ),
        check_vma=False,
    )
```

time: 4110 us -> 1530 us (0.37)
  waiting for transfers between devices: 3490 us -> 841 us
  blocking collectives: 240 us -> 0 us
  local copies, waits for them, and re-layouts: 77 us -> 256 us
  starting transfers between devices: 6.63 us -> 132 us
  other arithmetic: 39.5 us -> 147 us
  matrix products: 223 us -> 136 us
    reduce_scatter x10 -> x0, waiting for transfers between devices: 2150 us -> none  [the longest x1 604 us: body(): lax.psum_scatter(first_terms[1], ('dp', 'seq'), scatter_dimension=0, tile...]
    all_gather x9 -> x0, waiting for transfers between devices: 919 us -> none  [the longest x1 237 us: body(): lax.all_gather(first_lift, ('dp', 'seq'), axis=0, tiled=True)]
    ppermute x2 -> x127, waiting for transfers between devices: 5.11 us -> 841 us  [the longest x95 531 us: swap(): return lax.ppermute(array, GRID, pairs)]
    unnamed x28 -> x0, waiting for transfers between devices: 325 us -> none
    unnamed x2 -> x0, blocking collectives: 161 us -> none
    ppermute x2 -> x127, starting transfers between devices: 4.27 us -> 132 us  [the longest x95 112 us: swap(): return lax.ppermute(array, GRID, pairs)]
    reshape x4 -> x48, local copies, waits for them, and re-layouts: 0.63 us -> 91.9 us  [the longest x8 35.7 us: gather_flat(): return gather_tokens(own).reshape(-1, own.shape[-1])]
    psum x7 -> x0, waiting for transfers between devices: 90.2 us -> none  [model_sum(): lax.psum(partial_value.astype(jnp.bfloat16), 'mp').astype(jnp.float32)]
  transfers between devices with their start and end apart: 29 -> 127, of which waited for: 27 -> 72; matrix products, arithmetic and copies ran while one was open for 5% -> 28% of each run, Pallas kernels for 0% -> 0%
where the time goes in v1:
time: 1530 us; the launch traced here: 1520 us
  waiting for transfers between devices  841 us (55%)
  local copies, waits for them, and re-layouts  256 us (17%)
  other arithmetic  147 us (10%)
  matrix products  136 us (9%)
  starting transfers between devices  132 us (9%)
    ppermute x95, waiting for transfers between devices, swap(): return lax.ppermute(array, GRID, pairs)  531 us
    ppermute x12, waiting for transfers between devices, shift_groups(): return lax.ppermute(array, 'seq', pairs)  310 us
    dot_general x36, matrix products, dot(): return jnp.einsum(pattern, first, second, preferred_element_type=f32)  136 us
    ppermute x95, starting transfers between devices, swap(): return lax.ppermute(array, GRID, pairs)  112 us
    unnamed x389, local copies, waits for them, and re-layouts  55.5 us
    reshape x8, local copies, waits for them, and re-layouts, gather_flat(): return gather_tokens(own).reshape(-1, own.shape[-1])  35.7 us
  transfers between devices with their start and end apart: 127, of which 72 were waited for; matrix products, arithmetic and copies ran while one was open for 28% of the time, Pallas kernels for 0%

profile of v1, /device:TPU:0, one launch (start us, length us, event | category | flops | bytes accessed | tf_op | source)
XLA Modules:
  0.0 1517.0 jit_solution(5918010416030645510)
XLA Ops:
  82.4 11.0 collective-permute-done.5
  99.5 20.4 %collective-permute-done.12 = bf16[2,2,96,768]{3,2,1,0:T(8,128)(2,1)S(1)} collective-permute-done((bf16[2,2,96,768]{3,2,1,0:T(8,128)(2,1)}, bf16[2,2,96,768]{3,2,1,0:T(8,128)(2,1)S(1)}, u32[]{:S(2)}, u32[]{:S(2)}) %collective-permute-start.12) | collective-permute-done | bytes 589856 | tf_op jit(solution)/shard_map/ppermute | solution.py:75
  124.3 9.2 collective-permute-done.13
  165.5 10.3 collective-permute-done.29
  183.0 14.4 collective-permute-done.58
  202.6 111.0 %collective-permute-done.31 = bf16[3,2,2,96,864]{4,3,2,1,0:T(8,128)(2,1)} collective-permute-done((bf16[3,2,2,96,864]{4,3,2,1,0:T(8,128)(2,1)S(1)}, bf16[3,2,2,96,864]{4,3,2,1,0:T(8,128)(2,1)}, u32[]{:S(2)}, u32[]{:S(2)}) %collective-permute-start.31) | collective-permute-done | bytes 1990688 | tf_op jit(solution)/shard_map/ppermute | solution.py:75
  318.0 37.6 %collective-permute-done.60 = bf16[3,2,2,96,864]{4,3,2,1,0:T(8,128)(2,1)} collective-permute-done((bf16[3,2,2,96,864]{4,3,2,1,0:T(8,128)(2,1)}, bf16[3,2,2,96,864]{4,3,2,1,0:T(8,128)(2,1)}, u32[]{:S(2)}, u32[]{:S(2)}) %collective-permute-start.60) | collective-permute-done | bytes 1990688 | tf_op jit(solution)/shard_map/ppermute | solution.py:75
  369.3 7.7 collective-permute-done.23
  382.8 20.9 %collective-permute-done.59 = bf16[3,2,2,96,864]{4,3,2,1,0:T(8,128)(2,1)S(1)} collective-permute-done((bf16[3,2,2,96,864]{4,3,2,1,0:T(8,128)(2,1)}, bf16[3,2,2,96,864]{4,3,2,1,0:T(8,128)(2,1)S(1)}, u32[]{:S(2)}, u32[]{:S(2)}) %collective-permute-start.59) | collective-permute-done | bytes 1990688 | tf_op jit(solution)/shard_map/ppermute | solution.py:62
  405.9 42.0 %collective-permute-done.32 = bf16[3,2,2,96,864]{4,3,2,1,0:T(8,128)(2,1)S(1)} collective-permute-done((bf16[3,2,2,96,864]{4,3,2,1,0:T(8,128)(2,1)}, bf16[3,2,2,96,864]{4,3,2,1,0:T(8,128)(2,1)S(1)}, u32[]{:S(2)}, u32[]{:S(2)}) %collective-permute-start.32) | collective-permute-done | bytes 1990688 | tf_op jit(solution)/shard_map/ppermute | solution.py:62
  447.9 41.0 %collective-permute-done.61 = bf16[3,2,2,96,864]{4,3,2,1,0:T(8,128)(2,1)S(1)} collective-permute-done((bf16[3,2,2,96,864]{4,3,2,1,0:T(8,128)(2,1)}, bf16[3,2,2,96,864]{4,3,2,1,0:T(8,128)(2,1)S(1)}, u32[]{:S(2)}, u32[]{:S(2)}) %collective-permute-start.61) | collective-permute-done | bytes 1990688 | tf_op jit(solution)/shard_map/ppermute | solution.py:62
  533.8 9.1 collective-permute-done.36
  572.1 16.7 %collective-permute-done.45 = bf16[2,2,96,512]{3,2,1,0:T(8,128)(2,1)S(1)} collective-permute-done((bf16[2,2,96,512]{3,2,1,0:T(8,128)(2,1)S(1)}, bf16[2,2,96,512]{3,2,1,0:T(8,128)(2,1)S(1)}, u32[]{:S(2)}, u32[]{:S(2)}) %collective-permute-start.45) | collective-permute-done | bytes 393248 | tf_op jit(solution)/shard_map/ppermute | solution.py:75
  590.4 9.5 collective-permute-done.46
  647.9 10.1 collective-permute-done.69
  664.9 9.0 collective-permute-done.51
  797.9 8.2 collective-permute-done.74
  856.6 11.5 fusion
  931.5 14.8 collective-permute-done.117
  956.9 11.1 collective-permute-done.118
  973.7 8.0 collective-permute-done.83
  984.2 8.3 collective-permute-done.65
  1001.9 29.0 %collective-permute-done.121 = bf16[96,512]{1,0:T(8,128)(2,1)S(1)} collective-permute-done((bf16[96,512]{1,0:T(8,128)(2,1)S(1)}, bf16[96,512]{1,0:T(8,128)(2,1)S(1)}, u32[]{:S(2)}, u32[]{:S(2)}) %collective-permute-start.121) | collective-permute-done | bytes 98336 | tf_op jit(solution)/shard_map/ppermute | solution.py:62
  1041.4 37.8 %collective-permute-done.84 = bf16[128,1536]{1,0:T(8,128)(2,1)} collective-permute-done((bf16[128,1536]{1,0:T(8,128)(2,1)S(1)}, bf16[128,1536]{1,0:T(8,128)(2,1)}, u32[]{:S(2)}, u32[]{:S(2)}) %collective-permute-start.84) | collective-permute-done | bytes 393248 | tf_op jit(solution)/shard_map/ppermute | solution.py:62
  1102.0 9.7 collective-permute-done.125
  1172.9 8.1 collective-permute-done.91
  1270.6 35.2 %collective-permute-done.112 = bf16[3,2,2,2,96,864]{5,4,3,2,1,0:T(8,128)(2,1)} collective-permute-done((bf16[3,2,2,2,96,864]{5,4,3,2,1,0:T(8,128)(2,1)}, bf16[3,2,2,2,96,864]{5,4,3,2,1,0:T(8,128)(2,1)}, u32[]{:S(2)}, u32[]{:S(2)}) %collective-permute-start.112) | collective-permute-done | bytes 3981344 | tf_op jit(solution)/shard_map/ppermute | solution.py:62
  1312.5 17.5 %collective-permute-done.107 = bf16[2,2,2,96,768]{4,3,2,1,0:T(8,128)(2,1)} collective-permute-done((bf16[2,2,2,96,768]{4,3,2,1,0:T(8,128)(2,1)}, bf16[2,2,2,96,768]{4,3,2,1,0:T(8,128)(2,1)}, u32[]{:S(2)}, u32[]{:S(2)}) %collective-permute-start.107) | collective-permute-done | bytes 1179680 | tf_op jit(solution)/shard_map/ppermute | solution.py:62
  1334.4 93.0 %collective-permute-done.108 = bf16[2,2,96,768]{3,2,1,0:T(8,128)(2,1)S(1)} collective-permute-done((bf16[2,2,96,768]{3,2,1,0:T(8,128)(2,1)S(1)}, bf16[2,2,96,768]{3,2,1,0:T(8,128)(2,1)S(1)}, u32[]{:S(2)}, u32[]{:S(2)}) %collective-permute-start.108) | collective-permute-done | bytes 589856 | tf_op jit(solution)/shard_map/ppermute | solution.py:75
  1438.7 7.9 collective-permute-done.98
  1480.8 9.2 collective-permute-done.116
  1490.1 8.5 collective-permute-done.115
  (1016 shorter events, 814.7 us)
Async XLA Ops:
  1.3 58.7 %collective-permute-start.17 = (s32[128,1]{0,1:T(1,128)S(1)}, s32[128,1]{0,1:T(1,128)S(1)}, u32[]{:S(2)}, u32[]{:S(2)}) collective-permute-start(s32[128,1]{0,1:T(1,128)S(1)} %get-tuple-element.261), channel_id=1, source_target_pairs={{0,10},{2,8},{4,14},{6,12},{8,2},{10,0},{12,6},{14,4},{16,26},{18,... | collective-permute-start | bytes 1544 | tf_op jit(solution)/shard_map/ppermute | solution.py:62
  5.3 57.7 %collective-permute-start.16 = (s32[128,1]{0,1:T(1,128)S(1)}, s32[128,1]{0,1:T(1,128)S(1)}, u32[]{:S(2)}, u32[]{:S(2)}) collective-permute-start(s32[128,1]{0,1:T(1,128)S(1)} %get-tuple-element.261), channel_id=1, source_target_pairs={{0,8},{2,10},{4,12},{6,14},{8,0},{10,2},{12,4},{14,6},{16,24},{18,... | collective-permute-start | bytes 1544 | tf_op jit(solution)/shard_map/ppermute | solution.py:62
  5.8 57.7 %collective-permute-start.15 = (s32[128,1]{0,1:T(1,128)S(1)}, s32[128,1]{0,1:T(1,128)S(1)}, u32[]{:S(2)}, u32[]{:S(2)}) collective-permute-start(s32[128,1]{0,1:T(1,128)S(1)} %get-tuple-element.261), channel_id=1, source_target_pairs={{0,2},{2,0},{4,6},{6,4},{8,10},{10,8},{12,14},{14,12},{16,18},{18,... | collective-permute-start | bytes 1544 | tf_op jit(solution)/shard_map/ppermute | solution.py:62
  14.0 58.9 %collective-permute-start.9 = (bf16[96,768]{1,0:T(8,128)(2,1)}, bf16[96,768]{1,0:T(8,128)(2,1)}, u32[]{:S(2)}, u32[]{:S(2)}) collective-permute-start(bf16[96,768]{1,0:T(8,128)(2,1)} %bitcast.17), channel_id=1, source_target_pairs={{0,8},{2,10},{4,12},{6,14},{8,0},{10,2},{12,4},{14,6},{16,24},{18,... | collective-permute-start | bytes 442376 | tf_op jit(solution)/shard_map/ppermute | solution.py:62
  63.0 118.1 %collective-permute-start.57 = (bf16[3,96,864]{2,1,0:T(8,128)(2,1)}, bf16[3,96,864]{2,1,0:T(8,128)(2,1)}, u32[]{:S(2)}, u32[]{:S(2)}) collective-permute-start(bf16[3,96,864]{2,1,0:T(8,128)(2,1)} %bitcast.921), channel_id=1, source_target_pairs={{0,8},{2,10},{4,12},{6,14},{8,0},{10,2},{12,4},{14,6},{16,24},{18,... | collective-permute-start | bytes 1493000 | tf_op jit(solution)/shard_map/ppermute | solution.py:62
  75.2 104.1 %collective-permute-start.56 = (bf16[3,96,864]{2,1,0:T(8,128)(2,1)}, bf16[3,96,864]{2,1,0:T(8,128)(2,1)}, u32[]{:S(2)}, u32[]{:S(2)}) collective-permute-start(bf16[3,96,864]{2,1,0:T(8,128)(2,1)} %bitcast.922), channel_id=1, source_target_pairs={{0,2},{2,0},{4,6},{6,4},{8,10},{10,8},{12,14},{14,12},{16,18},{18,... | collective-permute-start | bytes 1493000 | tf_op jit(solution)/shard_map/ppermute | solution.py:62
  175.9 137.8 %collective-permute-start.31 = (bf16[3,2,2,96,864]{4,3,2,1,0:T(8,128)(2,1)S(1)}, bf16[3,2,2,96,864]{4,3,2,1,0:T(8,128)(2,1)}, u32[]{:S(2)}, u32[]{:S(2)}) collective-permute-start(bf16[3,2,2,96,864]{4,3,2,1,0:T(8,128)(2,1)S(1)} %bitcast_dynamic-update-slice_fusion.17), channel_id=1, source_target_pairs={{0,4},{2,6},{4,0},{6,2},{1,5},{3,7},{5,1},{7,3},{8,12},{10,14},{12... | collective-permute-start | bytes 5971976 | tf_op jit(solution)/shard_map/ppermute | solution.py:75
  198.3 157.3 %collective-permute-start.60 = (bf16[3,2,2,96,864]{4,3,2,1,0:T(8,128)(2,1)}, bf16[3,2,2,96,864]{4,3,2,1,0:T(8,128)(2,1)}, u32[]{:S(2)}, u32[]{:S(2)}) collective-permute-start(bf16[3,2,2,96,864]{4,3,2,1,0:T(8,128)(2,1)} %bitcast_dynamic-update-slice_fusion.14), channel_id=1, source_target_pairs={{0,4},{2,6},{4,0},{6,2},{1,5},{3,7},{5,1},{7,3},{8,12},{10,14},{12... | collective-permute-start | bytes 5971976 | tf_op jit(solution)/shard_map/ppermute | solution.py:75
  198.3 162.6 %collective-permute-start.30 = (bf16[3,2,2,96,864]{4,3,2,1,0:T(8,128)(2,1)S(1)}, bf16[3,2,2,96,864]{4,3,2,1,0:T(8,128)(2,1)}, u32[]{:S(2)}, u32[]{:S(2)}) collective-permute-start(bf16[3,2,2,96,864]{4,3,2,1,0:T(8,128)(2,1)S(1)} %bitcast_dynamic-update-slice_fusion.17), channel_id=1, source_target_pairs={{0,16},{2,18},{4,20},{6,22},{8,24},{10,26},{12,28},{14,30},{16,0},... | collective-permute-start | bytes 5971976 | tf_op jit(solution)/shard_map/ppermute | solution.py:62
  202.5 154.7 %collective-permute-start.20 = (bf16[128,1536]{1,0:T(8,128)(2,1)S(1)}, bf16[128,1536]{1,0:T(8,128)(2,1)S(1)}, u32[]{:S(2)}, u32[]{:S(2)}) collective-permute-start(bf16[128,1536]{1,0:T(8,128)(2,1)S(1)} %get-tuple-element.206), channel_id=1, source_target_pairs={{0,2},{2,0},{4,6},{6,4},{8,10},{10,8},{12,14},{14,12},{16,18},{18,... | collective-permute-start | bytes 1179656 | tf_op jit(solution)/shard_map/ppermute | solution.py:62
  202.6 155.1 %collective-permute-start.22 = (bf16[128,1536]{1,0:T(8,128)(2,1)S(1)}, bf16[128,1536]{1,0:T(8,128)(2,1)S(1)}, u32[]{:S(2)}, u32[]{:S(2)}) collective-permute-start(bf16[128,1536]{1,0:T(8,128)(2,1)S(1)} %get-tuple-element.207), channel_id=1, source_target_pairs={{0,10},{2,8},{4,14},{6,12},{8,2},{10,0},{12,6},{14,4},{16,26},{18,... | collective-permute-start | bytes 1179656 | tf_op jit(solution)/shard_map/ppermute | solution.py:62
  313.7 45.5 %collective-permute-start.21 = (bf16[128,1536]{1,0:T(8,128)(2,1)S(1)}, bf16[128,1536]{1,0:T(8,128)(2,1)S(1)}, u32[]{:S(2)}, u32[]{:S(2)}) collective-permute-start(bf16[128,1536]{1,0:T(8,128)(2,1)S(1)} %get-tuple-element.208), channel_id=1, source_target_pairs={{0,8},{2,10},{4,12},{6,14},{8,0},{10,2},{12,4},{14,6},{16,24},{18,... | collective-permute-start | bytes 1179656 | tf_op jit(solution)/shard_map/ppermute | solution.py:62
  355.6 48.1 %collective-permute-start.59 = (bf16[3,2,2,96,864]{4,3,2,1,0:T(8,128)(2,1)}, bf16[3,2,2,96,864]{4,3,2,1,0:T(8,128)(2,1)S(1)}, u32[]{:S(2)}, u32[]{:S(2)}) collective-permute-start(bf16[3,2,2,96,864]{4,3,2,1,0:T(8,128)(2,1)} %bitcast_dynamic-update-slice_fusion.14), channel_id=1, source_target_pairs={{0,16},{2,18},{4,20},{6,22},{8,24},{10,26},{12,28},{14,30},{16,0},... | collective-permute-start | bytes 5971976 | tf_op jit(solution)/shard_map/ppermute | solution.py:62
  357.1 90.8 %collective-permute-start.32 = (bf16[3,2,2,96,864]{4,3,2,1,0:T(8,128)(2,1)}, bf16[3,2,2,96,864]{4,3,2,1,0:T(8,128)(2,1)S(1)}, u32[]{:S(2)}, u32[]{:S(2)}) collective-permute-start(bf16[3,2,2,96,864]{4,3,2,1,0:T(8,128)(2,1)} %collective-permute-done.31), channel_id=1, source_target_pairs={{0,16},{2,18},{4,20},{6,22},{8,24},{10,26},{12,28},{14,30},{16,0},... | collective-permute-start | bytes 5971976 | tf_op jit(solution)/shard_map/ppermute | solution.py:62
  357.6 131.3 %collective-permute-start.61 = (bf16[3,2,2,96,864]{4,3,2,1,0:T(8,128)(2,1)}, bf16[3,2,2,96,864]{4,3,2,1,0:T(8,128)(2,1)S(1)}, u32[]{:S(2)}, u32[]{:S(2)}) collective-permute-start(bf16[3,2,2,96,864]{4,3,2,1,0:T(8,128)(2,1)} %collective-permute-done.60), channel_id=1, source_target_pairs={{0,16},{2,18},{4,20},{6,22},{8,24},{10,26},{12,28},{14,30},{16,0},... | collective-permute-start | bytes 5971976 | tf_op jit(solution)/shard_map/ppermute | solution.py:62
  382.7 111.8 %collective-permute-start.26 = (bf16[4,128,1536]{2,1,0:T(8,128)(2,1)S(1)}, bf16[4,128,1536]{2,1,0:T(8,128)(2,1)S(1)}, u32[]{:S(2)}, u32[]{:S(2)}) collective-permute-start(bf16[4,128,1536]{2,1,0:T(8,128)(2,1)S(1)} %get-tuple-element.205), channel_id=1, source_target_pairs={{0,1},{1,0},{2,3},{3,2},{4,5},{5,4},{6,7},{7,6},{8,9},{9,8},{10,11... | collective-permute-start | bytes 4718600 | tf_op jit(solution)/shard_map/ppermute | solution.py:66
  516.5 50.7 %collective-permute-start.42 = (bf16[96,512]{1,0:T(8,128)(2,1)}, bf16[96,512]{1,0:T(8,128)(2,1)}, u32[]{:S(2)}, u32[]{:S(2)}) collective-permute-start(bf16[96,512]{1,0:T(8,128)(2,1)} %bitcast.929), channel_id=1, source_target_pairs={{0,8},{2,10},{4,12},{6,14},{8,0},{10,2},{12,4},{14,6},{16,24},{18,... | collective-permute-start | bytes 294920 | tf_op jit(solution)/shard_map/ppermute | solution.py:62
  778.0 59.5 %collective-permute-start.62 = (bf16[4,128,1536]{2,1,0:T(8,128)(2,1)S(1)}, bf16[4,128,1536]{2,1,0:T(8,128)(2,1)S(1)}, u32[]{:S(2)}, u32[]{:S(2)}) collective-permute-start(bf16[4,128,1536]{2,1,0:T(8,128)(2,1)S(1)} %bitcast.1003), channel_id=1, source_target_pairs={{0,1},{1,0},{2,3},{3,2},{4,5},{5,4},{6,7},{7,6},{8,9},{9,8},{10,11... | collective-permute-start | bytes 4718600 | tf_op jit(solution)/shard_map/ppermute | solution.py:66
  835.9 92.2 %collective-permute-start.122 = (bf16[3,2,2,2,96,864]{5,4,3,2,1,0:T(8,128)(2,1)}, bf16[3,2,2,2,96,864]{5,4,3,2,1,0:T(8,128)(2,1)}, u32[]{:S(2)}, u32[]{:S(2)}) collective-permute-start(bf16[3,2,2,2,96,864]{5,4,3,2,1,0:T(8,128)(2,1)} %dynamic-slice_bitcast_fusion), channel_id=1, source_target_pairs={{0,16},{2,18},{4,20},{6,22},{8,24},{10,26},{12,28},{14,30},{16,0},... | collective-permute-start | bytes 11943944 | tf_op jit(solution)/shard_map/ppermute | solution.py:62
  928.1 55.4 %collective-permute-start.63 = (bf16[128,1536]{1,0:T(8,128)(2,1)}, bf16[128,1536]{1,0:T(8,128)(2,1)}, u32[]{:S(2)}, u32[]{:S(2)}) collective-permute-start(bf16[128,1536]{1,0:T(8,128)(2,1)} %get-tuple-element.193), channel_id=1, source_target_pairs={{0,2},{2,0},{4,6},{6,4},{8,10},{10,8},{12,14},{14,12},{16,18},{18,... | collective-permute-start | bytes 1179656 | tf_op jit(solution)/shard_map/ppermute | solution.py:62
  981.6 100.1 %collective-permute-start.123 = (bf16[3,2,2,96,864]{4,3,2,1,0:T(8,128)(2,1)}, bf16[3,2,2,96,864]{4,3,2,1,0:T(8,128)(2,1)}, u32[]{:S(2)}, u32[]{:S(2)}) collective-permute-start(bf16[3,2,2,96,864]{4,3,2,1,0:T(8,128)(2,1)} %fusion.28), channel_id=1, source_target_pairs={{0,4},{2,6},{4,0},{6,2},{1,5},{3,7},{5,1},{7,3},{8,12},{10,14},{12... | collective-permute-start | bytes 5971976 | tf_op jit(solution)/shard_map/ppermute | solution.py:75
  981.6 49.3 %collective-permute-start.121 = (bf16[96,512]{1,0:T(8,128)(2,1)S(1)}, bf16[96,512]{1,0:T(8,128)(2,1)S(1)}, u32[]{:S(2)}, u32[]{:S(2)}) collective-permute-start(bf16[96,512]{1,0:T(8,128)(2,1)S(1)} %get-tuple-element.233), channel_id=1, source_target_pairs={{0,10},{2,8},{4,14},{6,12},{8,2},{10,0},{12,6},{14,4},{16,26},{18,... | collective-permute-start | bytes 294920 | tf_op jit(solution)/shard_map/ppermute | solution.py:62
  983.4 48.9 %collective-permute-start.120 = (bf16[96,512]{1,0:T(8,128)(2,1)S(1)}, bf16[96,512]{1,0:T(8,128)(2,1)S(1)}, u32[]{:S(2)}, u32[]{:S(2)}) collective-permute-start(bf16[96,512]{1,0:T(8,128)(2,1)S(1)} %get-tuple-element.234), channel_id=1, source_target_pairs={{0,8},{2,10},{4,12},{6,14},{8,0},{10,2},{12,4},{14,6},{16,24},{18,... | collective-permute-start | bytes 294920 | tf_op jit(solution)/shard_map/ppermute | solution.py:62
  992.5 43.2 %collective-permute-start.119 = (bf16[96,512]{1,0:T(8,128)(2,1)}, bf16[96,512]{1,0:T(8,128)(2,1)}, u32[]{:S(2)}, u32[]{:S(2)}) collective-permute-start(bf16[96,512]{1,0:T(8,128)(2,1)} %get-tuple-element.235), channel_id=1, source_target_pairs={{0,2},{2,0},{4,6},{6,4},{8,10},{10,8},{12,14},{14,12},{16,18},{18,... | collective-permute-start | bytes 294920 | tf_op jit(solution)/shard_map/ppermute | solution.py:62
  1032.3 46.9 %collective-permute-start.84 = (bf16[128,1536]{1,0:T(8,128)(2,1)S(1)}, bf16[128,1536]{1,0:T(8,128)(2,1)}, u32[]{:S(2)}, u32[]{:S(2)}) collective-permute-start(bf16[128,1536]{1,0:T(8,128)(2,1)S(1)} %get-tuple-element.116), channel_id=1, source_target_pairs={{0,2},{2,0},{4,6},{6,4},{8,10},{10,8},{12,14},{14,12},{16,18},{18,... | collective-permute-start | bytes 1179656 | tf_op jit(solution)/shard_map/ppermute | solution.py:62
  1095.1 56.6 %collective-permute-start.66 = (bf16[128,1536]{1,0:T(8,128)(2,1)S(1)}, bf16[128,1536]{1,0:T(8,128)(2,1)}, u32[]{:S(2)}, u32[]{:S(2)}) collective-permute-start(bf16[128,1536]{1,0:T(8,128)(2,1)S(1)} %copy-done.87), channel_id=1, source_target_pairs={{0,1},{1,0},{2,3},{3,2},{4,5},{5,4},{6,7},{7,6},{8,9},{9,8},{10,11... | collective-permute-start | bytes 1179656 | tf_op jit(solution)/shard_map/ppermute | solution.py:66
  1213.5 92.4 %collective-permute-start.112 = (bf16[3,2,2,2,96,864]{5,4,3,2,1,0:T(8,128)(2,1)}, bf16[3,2,2,2,96,864]{5,4,3,2,1,0:T(8,128)(2,1)}, u32[]{:S(2)}, u32[]{:S(2)}) collective-permute-start(bf16[3,2,2,2,96,864]{5,4,3,2,1,0:T(8,128)(2,1)} %dynamic-slice_bitcast_fusion.1), channel_id=1, source_target_pairs={{0,16},{2,18},{4,20},{6,22},{8,24},{10,26},{12,28},{14,30},{16,0},... | collective-permute-start | bytes 11943944 | tf_op jit(solution)/shard_map/ppermute | solution.py:62
  1261.6 68.4 %collective-permute-start.107 = (bf16[2,2,2,96,768]{4,3,2,1,0:T(8,128)(2,1)}, bf16[2,2,2,96,768]{4,3,2,1,0:T(8,128)(2,1)}, u32[]{:S(2)}, u32[]{:S(2)}) collective-permute-start(bf16[2,2,2,96,768]{4,3,2,1,0:T(8,128)(2,1)} %fusion.53), channel_id=1, source_target_pairs={{0,16},{2,18},{4,20},{6,22},{8,24},{10,26},{12,28},{14,30},{16,0},... | collective-permute-start | bytes 3538952 | tf_op jit(solution)/shard_map/ppermute | solution.py:62
  1269.3 63.0 %collective-permute-start.97 = (bf16[4,128,1536]{2,1,0:T(8,128)(2,1)}, bf16[4,128,1536]{2,1,0:T(8,128)(2,1)}, u32[]{:S(2)}, u32[]{:S(2)}) collective-permute-start(bf16[4,128,1536]{2,1,0:T(8,128)(2,1)} %bitcast.244), channel_id=1, source_target_pairs={{0,1},{1,0},{2,3},{3,2},{4,5},{5,4},{6,7},{7,6},{8,9},{9,8},{10,11... | collective-permute-start | bytes 4718600 | tf_op jit(solution)/shard_map/ppermute | solution.py:66
  1312.2 158.3 %collective-permute-start.113 = (bf16[3,2,2,96,864]{4,3,2,1,0:T(8,128)(2,1)}, bf16[3,2,2,96,864]{4,3,2,1,0:T(8,128)(2,1)}, u32[]{:S(2)}, u32[]{:S(2)}) collective-permute-start(bf16[3,2,2,96,864]{4,3,2,1,0:T(8,128)(2,1)} %fusion.27), channel_id=1, source_target_pairs={{0,4},{2,6},{4,0},{6,2},{1,5},{3,7},{5,1},{7,3},{8,12},{10,14},{12... | collective-permute-start | bytes 5971976 | tf_op jit(solution)/shard_map/ppermute | solution.py:75
  1331.7 95.7 %collective-permute-start.108 = (bf16[2,2,96,768]{3,2,1,0:T(8,128)(2,1)S(1)}, bf16[2,2,96,768]{3,2,1,0:T(8,128)(2,1)S(1)}, u32[]{:S(2)}, u32[]{:S(2)}) collective-permute-start(bf16[2,2,96,768]{3,2,1,0:T(8,128)(2,1)S(1)} %fusion.130), channel_id=1, source_target_pairs={{0,4},{2,6},{4,0},{6,2},{1,5},{3,7},{5,1},{7,3},{8,12},{10,14},{12... | collective-permute-start | bytes 1769480 | tf_op jit(solution)/shard_map/ppermute | solution.py:75
  1467.7 46.6 %collective-permute-start.101 = (f32[128,1536]{1,0:T(8,128)S(1)}, f32[128,1536]{1,0:T(8,128)}, u32[]{:S(2)}, u32[]{:S(2)}) collective-permute-start(f32[128,1536]{1,0:T(8,128)S(1)} %fusion.81), channel_id=1, source_target_pairs={{0,1},{1,0},{2,3},{3,2},{4,5},{5,4},{6,7},{7,6},{8,9},{9,8},{10,11... | collective-permute-start | bytes 2359304 | tf_op jit(solution)/shard_map/ppermute | solution.py:66
  (288 other events, 4035.1 us)

commit v2 on v1

v2 whole, which is shorter than its diff:
```python
import jax
import jax.numpy as jnp
from jax import lax
from jax.sharding import PartitionSpec as P

HD = 64
FIRST_AXIS, SECOND_AXIS = "dp", "dp"

epsilon = 1e-05
rope_base = 1000000.0
bf16 = jnp.bfloat16
f32 = jnp.float32


def rms_scale(values):
    return lax.rsqrt(jnp.mean(values * values, axis=-1, keepdims=True) + epsilon)


def norm_back(back_normed, normed, inverse):
    return inverse * (back_normed - normed * jnp.mean(back_normed * normed, axis=-1, keepdims=True))


def frequencies():
    exponent = jnp.arange(HD // 2, dtype=f32) * (2.0 / HD)
    return jnp.power(rope_base, -exponent)


def rotate(values, cosines, sine_table):
    middle = values.shape[-1] // 2
    leading = values[..., :middle]
    trailing = values[..., middle:]
    return jnp.concatenate(
        [leading * cosines - trailing * sine_table, trailing * cosines + leading * sine_table],
        axis=-1,
    )


def dot(pattern, first, second):
    return jnp.einsum(pattern, first, second, preferred_element_type=f32)


class Team:
    def __init__(self, axis):
        self.axis = axis
        self.across = "seq" if axis == "dp" else "dp"
        self.size = lax.axis_size(axis)
        self.seat = lax.axis_index(axis)


def swap(array, axis, mask):
    return lax.ppermute(array, axis, [(i, i ^ mask) for i in range(lax.axis_size(axis))])


def swap_core(array):
    return swap(array, "mp", 1)


def shift(array, by):
    count = lax.axis_size("seq")
    return lax.ppermute(array, "seq", [(i, i + by) for i in range(count) if 0 <= i + by < count])


def zero(token):
    element = token[(0,) * token.ndim].astype(f32)
    return (element * 0.0).astype(jnp.int32)


def take(array, index, axis):
    return lax.dynamic_index_in_dim(array, index, axis, keepdims=False)


def gather_tokens(team, own):
    mine = jnp.concatenate([own] + [swap(own, team.axis, mask) for mask in range(1, team.size)], axis=0)
    return mine, swap_core(mine)


def scatter_tokens(team, mine, other):
    received = swap_core(other.astype(bf16)).astype(f32)
    rows = mine.shape[0] // team.size
    both = mine + received
    total = both[:rows]
    sends = [(mask, both[mask * rows : (mask + 1) * rows].astype(bf16)) for mask in range(team.size - 1, 0, -1)]
    for mask, send in sends:
        total = total + swap(send, team.axis, mask).astype(f32)
    return total, sends[-1][1]


def true_order(core, sequences, halves):
    mine, other = (half.reshape(sequences, -1, half.shape[-1]) for half in halves)
    return jnp.where(
        core == 0, jnp.concatenate([mine, other], axis=1), jnp.concatenate([other, mine], axis=1)
    )


def own_halves(core, ordered):
    rows = ordered.shape[1] // 2
    return [
        lax.dynamic_slice_in_dim(ordered, at * rows, rows, 1).reshape(-1, ordered.shape[-1])
        for at in (core, 1 - core)
    ]


def team_rows(team, piece_of):
    return [
        swap(piece_of(team.seat ^ mask), team.axis, mask) if mask else piece_of(team.seat)
        for mask in range(team.size)
    ]


def all_rows(team, pieces, late=0):
    lead, (rows, columns) = pieces[0].shape[:-2], pieces[0].shape[-2:]
    plain = (0,) * len(lead)
    near = jnp.zeros(lead + (team.size, rows, columns), pieces[0].dtype)
    for mask, piece in enumerate(pieces):
        near = lax.dynamic_update_slice(
            near, jnp.expand_dims(piece, len(lead)), plain + ((team.seat ^ mask) + late, 0, 0)
        )
    if team.axis == "dp":
        whole = lax.all_gather(near, team.across, axis=len(lead) + 1, tiled=True)
    else:
        near = near.reshape(lead + (team.size * rows, columns))
        whole = lax.all_gather(near, team.across, axis=len(lead), tiled=True)
    return whole.reshape(lead + (-1, columns))


def summed_rows(team, gradient):
    columns = gradient.shape[-1]
    teams = lax.axis_size(team.across)
    if team.axis == "dp":
        split = gradient.reshape(team.size, teams, -1, columns).swapaxes(0, 1)
    else:
        split = gradient.reshape(teams, team.size, -1, columns)
    rows = split.shape[2]
    part = lax.psum_scatter(split.reshape(-1, columns), team.across, scatter_dimension=0, tiled=True)
    return part.reshape(team.size, rows, columns)


def every_seat(team, part, late=0):
    axis = part.ndim - 3
    pieces = []
    for mask in range(team.size):
        piece = take(part, (team.seat ^ mask) + late, axis)
        pieces.append(swap(piece, team.axis, mask) if mask else piece)
    seats = jnp.stack(pieces)
    shape, bits = seats.shape, team.size.bit_length() - 1
    seats = seats.reshape((2,) * bits + shape[1:])
    for bit in range(bits):
        seats = jnp.where((team.seat >> bit) & 1 == 1, jnp.flip(seats, bits - 1 - bit), seats)
    return seats.reshape(shape).astype(f32)


def hidden_width(units, seats):
    tiles = -(-units // (128 * seats))
    return tiles * 128 if units % 128 == 0 else units // seats


def hidden_start(units, seats, seat):
    width = hidden_width(units, seats)
    return jnp.minimum(seat * width, units - width)


def hidden_mask(units, seats, seat):
    width = hidden_width(units, seats)
    doubled = seat * width - hidden_start(units, seats, seat)
    return (lax.broadcasted_iota(jnp.int32, (1, width), 1) >= doubled).astype(f32)


def joined_hidden(units, pieces):
    seats = len(pieces)
    width = hidden_width(units, seats)
    parts = []
    for seat in range(seats):
        low, start = seat * width, min(seat * width, units - width)
        if low < units:
            parts.append(pieces[seat][..., low - start : min(low + width, units) - start])
    return jnp.concatenate(parts, axis=-1)


def quarter(array, seat):
    width = array.shape[-1] // 4
    return array[..., seat * width : (seat + 1) * width]


def all_seats(array):
    return jnp.concatenate([array[i] for i in range(4)], axis=-1)


def pack_mixer(weight_in, weight_out):
    seats = [
        jnp.concatenate([quarter(weight_in[:, k], i) for k in range(3)] + [quarter(weight_out, i)], axis=-1)
        for i in range(4)
    ]
    return jnp.stack(seats)


def pack_attend(query_weight, pair_weight, out_weight):
    seats = [
        jnp.concatenate(
            [quarter(query_weight, i)]
            + [quarter(pair_weight[:, k], i) for k in range(2)]
            + [quarter(out_weight, i)],
            axis=-1,
        )
        for i in range(4)
    ]
    return jnp.stack(seats)


def lowered_norm(hidden, gain):
    inverse = rms_scale(hidden)
    normed = hidden * inverse
    return inverse, normed, (normed * gain).astype(bf16)


def after_norm(back_out, back_normed, normed, inverse, gain):
    gain_term = jnp.sum(back_normed * normed, axis=0)
    return back_out + norm_back(back_normed * gain, normed, inverse), gain_term


def project(pattern, halves, weights):
    return [dot(pattern, half, weights) for half in halves]


def project_out(team, pattern, halves, weights):
    other = dot(pattern, halves[1], weights)
    mine = dot(pattern, halves[0], weights)
    return scatter_tokens(team, mine, other)


def outer(first, second):
    return (dot("td,tf->df", first[0], second[0]) + dot("td,tf->df", first[1], second[1])).astype(bf16)


def feed_active(tokens, lift, mask):
    gate = dot("td,df->tf", tokens, lift[0])
    up = dot("td,df->tf", tokens, lift[1])
    return gate, up, (jax.nn.silu(gate) * up * mask).astype(bf16)


def feed_back(back_tokens, gate, up, drop, mask):
    back_active = dot("td,df->tf", back_tokens, drop) * mask
    sigmoid_value = jax.nn.sigmoid(gate)
    back_gate = back_active * up * sigmoid_value * (1.0 + gate * (1.0 - sigmoid_value))
    return back_gate.astype(bf16), (back_active * gate * sigmoid_value).astype(bf16)


def feed_forward(team, hidden, gain, lift, mask):
    inverse, normed, lowered = lowered_norm(hidden, gain)
    tokens = gather_tokens(team, lowered)
    gate, up, active = zip(*[feed_active(half, lift, mask) for half in tokens])
    return inverse, normed, tokens, gate, up, active


def feed_backward(team, back_out, back_tokens, stored, gain, lift, drop, mask):
    inverse, normed, tokens, gate, up, active = stored
    back_gate, back_up = zip(
        *[feed_back(back_tokens[i], gate[i], up[i], drop, mask) for i in range(2)]
    )
    terms = [
        dot("tf,df->td", back_gate[i], lift[0]) + dot("tf,df->td", back_up[i], lift[1]) for i in (1, 0)
    ]
    back_normed, sent = scatter_tokens(team, terms[1], terms[0])
    drop_term = outer(back_tokens, active)
    lift_terms = [outer(tokens, back_gate), outer(tokens, back_up)]
    back_hidden, gain_term = after_norm(back_out, back_normed, normed, inverse, gain)
    return back_hidden, gain_term, lift_terms + [drop_term]


def mixer_forward(team, core, hidden, token_halves, order, gain, weights, taps):
    inverse = rms_scale(hidden)
    normed = hidden * inverse
    tokens = [lowered_norm(half.astype(f32), gain)[2] for half in token_halves]
    channels = taps.shape[1]
    parts = true_order(core, team.size, project("td,dc->tc", tokens, weights[:, : 3 * channels]))
    gate_in, gate_out, value = (parts[..., i * channels : (i + 1) * channels] for i in range(3))
    mixed = (gate_in * value).astype(bf16)
    earlier = shift(mixed[:, -2:], 1)
    padded = jnp.concatenate([earlier, mixed], axis=1).astype(f32)
    one_back = (order >= 1).astype(f32)[..., None]
    two_back = (order >= 2).astype(f32)[..., None]
    convolved = (
        taps[2] * padded[:, 2:] + taps[1] * padded[:, 1:-1] * one_back + taps[0] * padded[:, :-2] * two_back
    )
    gated = own_halves(core, (gate_out * convolved).astype(bf16))
    out, sent = project_out(team, "tc,dc->td", gated, weights[:, 3 * channels :])
    stored = (inverse, normed, tokens, gate_in, gate_out, value, padded, convolved, gated, one_back, two_back)
    return hidden + out, stored, parts


def mixer_backward(team, core, back_out, stored, gain, weights, taps):
    inverse, normed, tokens, gate_in, gate_out, value, padded, convolved, gated, one_back, two_back = stored
    channels = taps.shape[1]
    back_tokens = gather_tokens(team, back_out.astype(bf16))
    back_gated = true_order(core, team.size, project("td,dc->tc", back_tokens, weights[:, 3 * channels :]))
    back_conv = back_gated * gate_out
    back_padded = (
        jnp.pad(taps[2] * back_conv, ((0, 0), (2, 0), (0, 0)))
        + jnp.pad(taps[1] * back_conv * one_back, ((0, 0), (1, 1), (0, 0)))
        + jnp.pad(taps[0] * back_conv * two_back, ((0, 0), (0, 2), (0, 0)))
    )
    later = shift(back_padded[:, :2], -1)
    back_mixed = back_padded[:, 2:] + jnp.pad(later, ((0, 0), (back_conv.shape[1] - 2, 0), (0, 0)))
    back_parts = own_halves(
        core,
        jnp.concatenate(
            [back_mixed * value, back_gated * convolved, back_mixed * gate_in], axis=-1
        ).astype(bf16),
    )
    back_normed, sent = project_out(team, "tc,dc->td", back_parts, weights[:, : 3 * channels])
    tap_term = jnp.stack(
        [
            jnp.sum(back_conv * padded[:, :-2] * two_back, axis=(0, 1)),
            jnp.sum(back_conv * padded[:, 1:-1] * one_back, axis=(0, 1)),
            jnp.sum(back_conv * padded[:, 2:], axis=(0, 1)),
        ]
    )
    term = jnp.concatenate([outer(tokens, back_parts), outer(back_tokens, gated)], axis=-1)
    back_hidden, gain_term = after_norm(back_out, back_normed, normed, inverse, gain)
    return back_hidden, gain_term, term, tap_term, back_gated


def attend_forward(team, core, hidden, order, gain, weights, query_gain, key_gain):
    inverse, normed, lowered = lowered_norm(hidden, gain)
    tokens = gather_tokens(team, lowered)
    heads = weights.shape[1] * 3 // 8 // HD
    groups = weights.shape[1] // 8 // HD
    repeat = heads // groups
    inner = (heads + 2 * groups) * HD
    mixed = true_order(core, team.size, project("td,dc->tc", tokens, weights[:, :inner]))
    sequences, count = mixed.shape[:2]
    query_heads = mixed[..., : heads * HD].reshape(sequences, count, heads, HD)
    key_heads = mixed[..., heads * HD : (heads + groups) * HD].reshape(sequences, count, groups, HD)
    value_low = mixed[..., (heads + groups) * HD :].astype(bf16)
    angles = order.astype(f32)[..., None] * frequencies()
    cosines, sines = jnp.cos(angles)[:, :, None, :], jnp.sin(angles)[:, :, None, :]
    query_inverse = rms_scale(query_heads)
    query_normed = query_heads * query_inverse
    query_rot = rotate(query_normed * query_gain, cosines, sines).astype(bf16)
    key_inverse = rms_scale(key_heads)
    key_normed = key_heads * key_inverse
    key_rot = rotate(key_normed * key_gain, cosines, sines).astype(bf16)
    pair = jnp.concatenate([key_rot.reshape(sequences, count, groups * HD), value_low], axis=-1)
    blocks = lax.axis_size("seq")
    here = lax.axis_index("seq")
    slots = jnp.concatenate([shift(pair, i) if i else pair for i in range(blocks)], axis=1)
    keys = slots[..., : groups * HD].reshape(sequences, -1, groups, HD)
    values = slots[..., groups * HD :].reshape(sequences, -1, groups, HD)
    grouped = query_rot.reshape(sequences, count, groups, repeat, HD)
    row_index = here * count + jnp.arange(count, dtype=jnp.int32)
    row_first = row_index[None] - order
    key_index = jnp.concatenate(
        [(here - i) * count + jnp.arange(count, dtype=jnp.int32) for i in range(blocks)]
    )
    allowed = (key_index[None, None, :] <= row_index[None, :, None]) & (
        key_index[None, None, :] >= row_first[:, :, None]
    )
    scores = dot("vqgrd,vkgd->vgrqk", grouped, keys) * HD**-0.5
    scores = jnp.where(allowed[:, None, None], scores, -1e30)
    probs = jnp.exp(scores - jnp.max(scores, axis=-1, keepdims=True))
    probs = probs / jnp.sum(probs, axis=-1, keepdims=True)
    attended = dot("vgrqk,vkgd->vqgrd", probs.astype(bf16), values).astype(bf16)
    attended = own_halves(core, attended.reshape(sequences, count, heads * HD))
    out, sent = project_out(team, "tc,dc->td", attended, weights[:, inner:])
    stored = (
        inverse,
        normed,
        tokens,
        query_inverse,
        query_normed,
        key_inverse,
        key_normed,
        cosines,
        sines,
        grouped,
        keys,
        values,
        probs,
        attended,
    )
    return hidden + out, stored, mixed


def attend_backward(team, core, back_out, stored, gain, weights, query_gain, key_gain):
    (
        inverse,
        normed,
        tokens,
        query_inverse,
        query_normed,
        key_inverse,
        key_normed,
        cosines,
        sines,
        grouped,
        keys,
        values,
        probs,
        attended,
    ) = stored
    sequences, count, groups, repeat = grouped.shape[:4]
    heads = groups * repeat
    inner = (heads + 2 * groups) * HD
    back_tokens = gather_tokens(team, back_out.astype(bf16))
    back_attended = true_order(core, team.size, project("td,dc->tc", back_tokens, weights[:, inner:])).astype(bf16)
    back_grouped = back_attended.reshape(sequences, count, groups, repeat, HD)
    back_probs = dot("vqgrd,vkgd->vgrqk", back_grouped, values)
    row_dot = jnp.sum(probs * back_probs, axis=-1, keepdims=True)
    back_scores = (probs * (back_probs - row_dot)).astype(bf16)
    back_query_rot = dot("vgrqk,vkgd->vqgrd", back_scores, keys) * HD**-0.5
    back_keys = dot("vgrqk,vqgrd->vkgd", back_scores, grouped) * HD**-0.5
    back_values = dot("vgrqk,vqgrd->vkgd", probs.astype(bf16), back_grouped)
    back_slots = jnp.concatenate(
        [
            back_keys.reshape(sequences, -1, count, groups * HD),
            back_values.reshape(sequences, -1, count, groups * HD),
        ],
        axis=-1,
    )
    back_pair = back_slots[:, 0]
    for i in range(1, back_slots.shape[1]):
        back_pair = back_pair + shift(back_slots[:, i].astype(bf16), -i).astype(f32)
    back_query_scaled = rotate(back_query_rot.reshape(sequences, count, heads, HD), cosines, -sines)
    query_scale_term = jnp.sum(back_query_scaled * query_normed, axis=(0, 1, 2))
    back_query = norm_back(back_query_scaled * query_gain, query_normed, query_inverse)
    back_key_rot = back_pair[..., : groups * HD].reshape(sequences, count, groups, HD)
    back_key_scaled = rotate(back_key_rot, cosines, -sines)
    key_scale_term = jnp.sum(back_key_scaled * key_normed, axis=(0, 1, 2))
    back_key = norm_back(back_key_scaled * key_gain, key_normed, key_inverse)
    back_mixed = jnp.concatenate(
        [
            back_query.reshape(sequences, count, heads * HD),
            back_key.reshape(sequences, count, groups * HD),
            back_pair[..., groups * HD :],
        ],
        axis=-1,
    ).astype(bf16)
    back_mixed = own_halves(core, back_mixed)
    back_normed, sent = project_out(team, "tc,dc->td", back_mixed, weights[:, :inner])
    term = jnp.concatenate([outer(tokens, back_mixed), outer(back_tokens, attended)], axis=-1)
    back_hidden, gain_term = after_norm(back_out, back_normed, normed, inverse, gain)
    return back_hidden, gain_term, term, (query_scale_term, key_scale_term), back_attended


def grid_total(array):
    for axis in ("dp", "seq"):
        mask = 1
        while mask < lax.axis_size(axis):
            array = array + swap(array, axis, mask)
            mask *= 2
    return array


def body(
    hidden_in,
    positions,
    mixer_gain,
    mixer_in,
    mixer_taps,
    mixer_out,
    first_gain,
    first_lift,
    first_drop,
    attend_gain,
    query_weight,
    pair_weight,
    query_scale,
    key_scale,
    attend_out,
    second_gain,
    second_lift,
    second_drop,
    cotangent,
):
    core = lax.axis_index("mp")
    team = Team("dp")
    first_team, second_team = Team(FIRST_AXIS), Team(SECOND_AXIS)
    rank = lax.axis_index("dp") * lax.axis_size("seq") + lax.axis_index("seq")
    model = hidden_in.shape[-1]
    share = hidden_in.shape[1] // 2
    own_tokens = lax.dynamic_slice_in_dim(hidden_in[0], core * share, share)
    hidden = own_tokens.astype(f32)
    signal_low = lax.dynamic_slice_in_dim(cotangent[0], core * share, share)
    signal = signal_low.astype(f32)
    query_gain, key_gain = query_scale.astype(f32), key_scale.astype(f32)
    channels = mixer_taps.shape[1] // team.size
    taps = lax.dynamic_slice_in_dim(mixer_taps, team.seat * channels, channels, 1).astype(f32)
    units = first_drop.shape[1]
    first_mask = hidden_mask(units, first_team.size, first_team.seat)
    second_mask = hidden_mask(units, second_team.size, second_team.seat)

    def feed_piece(on, lift, drop, late):
        both = jnp.concatenate([lift.transpose(1, 0, 2), drop[None]], axis=0)
        width = hidden_width(units, on.size)
        return lambda seat: lax.dynamic_slice_in_dim(both, hidden_start(units, on.size, seat) + late, width, 2)

    token_halves = gather_tokens(team, own_tokens)
    packed = pack_mixer(mixer_in, mixer_out)
    got = team_rows(team, lambda seat: take(packed, seat, 0))
    mixer_weights = all_rows(team, got)
    near_done = zero(got[-1])

    got_first = team_rows(first_team, feed_piece(first_team, first_lift, first_drop, near_done))
    first_lift_all = all_rows(first_team, [piece[:2] for piece in got_first])
    first_drop_all = all_rows(first_team, [piece[2] for piece in got_first])
    near_done = zero(got_first[-1])

    gain_rows = mixer_gain.shape[0]
    gains = jnp.stack([mixer_gain, first_gain, attend_gain, second_gain]).astype(f32)
    gains = grid_total(
        lax.dynamic_update_slice_in_dim(jnp.zeros((4, model), f32), gains, rank * gain_rows + near_done, 1)
    )
    own_places = positions[0] + near_done
    order = jnp.stack([own_places] + [swap(own_places, team.axis, mask) for mask in range(1, team.size)])

    packed_attend = pack_attend(query_weight, pair_weight, attend_out)
    got_attend = team_rows(team, lambda seat: take(packed_attend, seat + near_done, 0))
    got_second = team_rows(second_team, feed_piece(second_team, second_lift, second_drop, near_done))

    after_mixer, mixer_stored, parts = mixer_forward(
        team, core, hidden, token_halves, order, gains[0], mixer_weights, taps
    )
    mixed_done = zero(parts)
    attend_weights = all_rows(team, got_attend, mixed_done)
    second_lift_all = all_rows(second_team, [piece[:2] for piece in got_second], mixed_done)
    second_drop_all = all_rows(second_team, [piece[2] for piece in got_second], mixed_done)

    first_stored = feed_forward(first_team, after_mixer, gains[1], first_lift_all, first_mask)
    out, sent = project_out(first_team, "tf,df->td", first_stored[-1], first_drop_all)
    after_first = after_mixer + out
    after_attend, attend_stored, mixed = attend_forward(
        team, core, after_first, order, gains[2], attend_weights, query_gain, key_gain
    )
    signal_low = signal_low + zero(mixed).astype(bf16)
    signal_tokens = gather_tokens(second_team, signal_low)
    second_stored = feed_forward(second_team, after_attend, gains[3], second_lift_all, second_mask)

    back, second_gain_term, second_terms = feed_backward(
        second_team, signal, signal_tokens, second_stored, gains[3], second_lift_all, second_drop_all, second_mask
    )
    second_part = [summed_rows(second_team, term) for term in second_terms]
    back, attend_gain_term, attend_term, scale_terms, back_attended = attend_backward(
        team, core, back, attend_stored, gains[2], attend_weights, query_gain, key_gain
    )
    attend_part = summed_rows(team, attend_term)
    late = zero(back_attended).astype(bf16)
    out, sent = project_out(second_team, "tf,df->td", [half + late for half in second_stored[-1]], second_drop_all)
    result = after_attend + out

    first_back_tokens = gather_tokens(first_team, back.astype(bf16))
    back, first_gain_term, first_terms = feed_backward(
        first_team, back, first_back_tokens, first_stored, gains[1], first_lift_all, first_drop_all, first_mask
    )
    first_part = [summed_rows(first_team, term) for term in first_terms]
    back, mixer_gain_term, mixer_term, tap_term, back_gated = mixer_backward(
        team, core, back, mixer_stored, gains[0], mixer_weights, taps
    )
    mixer_part = summed_rows(team, mixer_term)
    gated_done = zero(back_gated)
    second_total = every_seat(second_team, jnp.stack(second_part), gated_done)
    attend_total = every_seat(team, attend_part, gated_done)
    first_total = every_seat(first_team, jnp.stack(first_part))
    mixer_total = every_seat(team, mixer_part)

    small = jnp.concatenate(
        [mixer_gain_term, first_gain_term, attend_gain_term, second_gain_term, scale_terms[0], scale_terms[1]]
    )
    small = small + swap_core(small)
    tap_full = lax.dynamic_update_slice_in_dim(
        jnp.zeros((3, mixer_taps.shape[1]), f32), tap_term, team.seat * channels, 1
    )
    small = grid_total(jnp.concatenate([small, tap_full.reshape(-1)]))
    gain_totals = lax.dynamic_slice_in_dim(
        small[: 4 * model].reshape(4, model), rank * gain_rows, gain_rows, 1
    )
    scale_totals = small[4 * model : 4 * model + 2 * HD].reshape(2, HD)
    tap_total = small[4 * model + 2 * HD :].reshape(tap_full.shape)

    def both_cores(own):
        return true_order(core, 1, [own, swap_core(own)])

    rows = mixer_in.shape[0]
    in_columns = 3 * channels
    inner = attend_total.shape[-1] - query_weight.shape[1] // 4
    queries = query_weight.shape[1] // 4
    return (
        both_cores(result.astype(bf16)),
        both_cores(back),
        gain_totals[0],
        all_seats(mixer_total[..., :in_columns].reshape(4, rows, 3, channels)),
        tap_total,
        all_seats(mixer_total[..., in_columns:]),
        gain_totals[1],
        joined_hidden(units, first_total[:, :2]).transpose(1, 0, 2),
        joined_hidden(units, first_total[:, 2]),
        gain_totals[2],
        all_seats(attend_total[..., :queries]),
        all_seats(attend_total[..., queries:inner].reshape(4, rows, 2, -1)),
        scale_totals[0],
        scale_totals[1],
        all_seats(attend_total[..., inner:]),
        gain_totals[3],
        joined_hidden(units, second_total[:, :2]).transpose(1, 0, 2),
        joined_hidden(units, second_total[:, 2]),
    )


def solution(mesh):
    grid = ("dp", "seq")
    return jax.shard_map(
        body,
        mesh=mesh,
        in_specs=(
            P("dp", "seq", None),
            P("dp", "seq"),
            P(grid),
            P(grid, None, "mp"),
            P(None, "mp"),
            P(grid, "mp"),
            P(grid),
            P(grid, None, "mp"),
            P(grid, "mp"),
            P(grid),
            P(grid, "mp"),
            P(grid, None, "mp"),
            P(),
            P(),
            P(grid, "mp"),
            P(grid),
            P(grid, None, "mp"),
            P(grid, "mp"),
            P("dp", "seq", None),
        ),
        out_specs=(
            P("dp", "seq", None),
            P("dp", "seq", None),
            P(grid),
            P(grid, None, "mp"),
            P(None, "mp"),
            P(grid, "mp"),
            P(grid),
            P(grid, None, "mp"),
            P(grid, "mp"),
            P(grid),
            P(grid, "mp"),
            P(grid, None, "mp"),
            P(),
            P(),
            P(grid, "mp"),
            P(grid),
            P(grid, None, "mp"),
            P(grid, "mp"),
        ),
        check_vma=False,
    )
```

time: 1530 us -> 1070 us (0.70)
  waiting for transfers between devices: 841 us -> 511 us
  local copies, waits for them, and re-layouts: 256 us -> 118 us
  matrix products: 136 us -> 207 us
  other arithmetic: 147 us -> 80 us
  between operations: 4.73 us -> 23.5 us
    ppermute x127 -> x110, waiting for transfers between devices: 841 us -> 399 us  [the longest x102 307 us: swap(): lax.ppermute(array, axis, [(i, i ^ mask) for i in range(lax.axis_size(axi...]
    all_gather x0 -> x6, waiting for transfers between devices: none -> 105 us  [all_rows(): whole = lax.all_gather(near, team.across, axis=len(lead) + 1, tiled=True)]
    reshape x42 -> x16, local copies, waits for them, and re-layouts: 89.4 us -> 11.7 us  [the longest x6 10.7 us: summed_rows(): split = gradient.reshape(team.size, teams, -1, columns).swapaxes(0, 1)]
    dot_general x36 -> x66, matrix products: 136 us -> 207 us  [dot(): return jnp.einsum(pattern, first, second, preferred_element_type=f32)]
    another operation x33 -> x18, other arithmetic: 46.6 us -> 17.6 us  [the longest x17 25.6 us: gather_tokens(): return jnp.stack([mine, other])]
    convert_element_type x21 -> x10, other arithmetic: 31.3 us -> 7.13 us  [the longest x1 1.55 us: body(): first_back_tokens = gather_tokens(first_team, back.astype(bf16))]
    unnamed x389 -> x494, local copies, waits for them, and re-layouts: 55.5 us -> 39.6 us
    ppermute x127 -> x110, starting transfers between devices: 132 us -> 123 us  [the longest x102 107 us: swap(): lax.ppermute(array, axis, [(i, i ^ mask) for i in range(lax.axis_size(axi...]
  transfers between devices with their start and end apart: 127 -> 124, of which waited for: 72 -> 70; matrix products, arithmetic and copies ran while one was open for 28% -> 33% of each run, Pallas kernels for 0% -> 0%
where the time goes in v2:
time: 1070 us
  waiting for transfers between devices  511 us (48%)
  matrix products  207 us (19%)
  starting transfers between devices  125 us (12%)
  local copies, waits for them, and re-layouts  118 us (11%)
  other arithmetic  80 us (7%)
  between operations  23.5 us (2%)
    ppermute x102, waiting for transfers between devices, swap(): lax.ppermute(array, axis, [(i, i ^ mask) for i in range(lax.axis_size(axi...  307 us
    dot_general x66, matrix products, dot(): return jnp.einsum(pattern, first, second, preferred_element_type=f32)  207 us
    ppermute x102, starting transfers between devices, swap(): lax.ppermute(array, axis, [(i, i ^ mask) for i in range(lax.axis_size(axi...  107 us
    all_gather x6, waiting for transfers between devices, all_rows(): whole = lax.all_gather(near, team.across, axis=len(lead) + 1, tiled=True)  105 us
    ppermute x8, waiting for transfers between devices, shift(): lax.ppermute(array, 'seq', [(i, i + by) for i in range(count) if 0 <= i +...  92 us
    unnamed x494, local copies, waits for them, and re-layouts  39.6 us
  transfers between devices with their start and end apart: 124, of which 70 were waited for; matrix products, arithmetic and copies ran while one was open for 33% of the time, Pallas kernels for 0%

profile of v2, /device:TPU:0, one launch (start us, length us, event | category | flops | bytes accessed | tf_op | source)
XLA Modules:
  0.0 1065.4 jit_solution(12796875786256877658)
XLA Ops:
  47.7 8.2 collective-permute-done.23
  57.6 8.3 collective-permute-done.4
  146.7 7.6 collective-permute-done.21
  160.0 17.6 %all-gather.9.cloned.1.call-done = bf16[2,4,384,896]{3,2,1,0:T(8,128)(2,1)} async-done(((bf16[2,4,96,896]{3,2,1,0:T(8,128)(2,1)}), bf16[2,4,384,896]{3,2,1,0:T(8,128)(2,1)}) %all-gather.9.cloned.1.call-update) | async-done | bytes 5505040 | tf_op jit(solution)/shard_map/all_gather | solution.py:119
  199.1 39.8 %all-gather.11.cloned.1.call-done = bf16[4,384,896]{2,1,0:T(8,128)(2,1)} async-done(((bf16[4,96,896]{2,1,0:T(8,128)(2,1)}), bf16[4,384,896]{2,1,0:T(8,128)(2,1)}) %all-gather.11.cloned.1.call-update) | async-done | bytes 2752528 | tf_op jit(solution)/shard_map/all_gather | solution.py:119
  270.1 15.3 %collective-permute-done.34 = bf16[96,512]{1,0:T(8,128)(2,1)} collective-permute-done((bf16[96,512]{1,0:T(8,128)(2,1)}, bf16[96,512]{1,0:T(8,128)(2,1)}, u32[]{:S(2)}, u32[]{:S(2)}) %collective-permute-start.34) | collective-permute-done | bytes 98336 | tf_op jit(solution)/shard_map/ppermute | solution.py:51
  303.0 9.3 collective-permute-done.32
  321.0 9.1 collective-permute-done.48
  351.3 7.1 collective-permute-done.39
  358.5 11.2 %collective-permute-done.38 = bf16[4,256,128]{1,2,0:T(8,128)(2,1)S(1)} collective-permute-done((bf16[4,256,128]{1,2,0:T(8,128)(2,1)S(1)}, bf16[4,256,128]{1,2,0:T(8,128)(2,1)S(1)}, u32[]{:S(2)}, u32[]{:S(2)}) %collective-permute-start.38) | collective-permute-done | bytes 262176 | tf_op jit(solution)/shard_map/ppermute | solution.py:60
  369.7 10.7 %collective-permute-done.37 = bf16[4,256,128]{1,2,0:T(8,128)(2,1)S(1)} collective-permute-done((bf16[4,256,128]{1,2,0:T(8,128)(2,1)S(1)}, bf16[4,256,128]{1,2,0:T(8,128)(2,1)S(1)}, u32[]{:S(2)}, u32[]{:S(2)}) %collective-permute-start.37) | collective-permute-done | bytes 262176 | tf_op jit(solution)/shard_map/ppermute | solution.py:60
  433.3 7.5 collective-permute-done.51
  442.2 7.1 collective-permute-done.46
  449.3 7.9 collective-permute-done.45
  464.3 48.1 %all-gather.17.cloned.1.call-done = bf16[4,384,896]{2,1,0:T(8,128)(2,1)} async-done(((bf16[4,96,896]{2,1,0:T(8,128)(2,1)}), bf16[4,384,896]{2,1,0:T(8,128)(2,1)}) %all-gather.17.cloned.1.call-update) | async-done | bytes 2752528 | tf_op jit(solution)/shard_map/all_gather | solution.py:119
  568.0 9.4 collective-permute-done.56
  577.3 7.8 collective-permute-done.58
  590.9 9.4 collective-permute-done.61
  600.3 7.5 collective-permute-done.60
  624.9 9.8 fusion.23
  634.7 11.6 %fusion = (f32[4,3,256]{2,1,0:T(4,128)S(1)}, f32[4,1024,256,3]{2,1,3,0:T(8,128)}) fusion(f32[4,3,256]{2,1,0:T(4,128)S(1)} %copy-done.162, f32[4,3,256]{2,1,0:T(4,128)S(1)} %copy-done.160, f32[4,1024,256,3]{2,1,3,0:T(8,128)} %copy-done, pred[4,256,1024]{1,2,0:T(8,128)(4,1)S(1)} %copy-done.22, bf16[4,128,3,64]{1,3,2,0:T(8,128)(2,1)S(1)} %copy.232, ...), kind=kOutput, calls=%fused_computation.3 | convolution fusion | flops 423293952 | bytes 27176960 | tf_op jit(solution)/shard_map/vqgrd,vkgd->vgrqk/dot_general | solution.py:39
  646.3 7.1 fusion.6
  678.0 22.4 %collective-permute-done.68 = bf16[4,256,128]{1,2,0:T(8,128)(2,1)S(1)} collective-permute-done((bf16[4,256,128]{1,2,0:T(8,128)(2,1)S(1)}, bf16[4,256,128]{1,2,0:T(8,128)(2,1)S(1)}, u32[]{:S(2)}, u32[]{:S(2)}) %collective-permute-start.68) | collective-permute-done | bytes 262176 | tf_op jit(solution)/shard_map/ppermute | solution.py:60
  701.1 24.3 %collective-permute-done.69 = bf16[4,256,128]{1,2,0:T(8,128)(2,1)S(1)} collective-permute-done((bf16[4,256,128]{1,2,0:T(8,128)(2,1)S(1)}, bf16[4,256,128]{1,2,0:T(8,128)(2,1)S(1)}, u32[]{:S(2)}, u32[]{:S(2)}) %collective-permute-start.69) | collective-permute-done | bytes 262176 | tf_op jit(solution)/shard_map/ppermute | solution.py:60
  762.1 7.4 collective-permute-done.64
  769.5 7.8 collective-permute-done.66
  791.9 7.4 collective-permute-done.76
  849.6 9.4 collective-permute-done.80
  859.0 7.5 collective-permute-done.82
  881.7 7.6 collective-permute-done.84
  930.0 8.4 collective-permute-done.87
  1002.9 22.2 %collective-permute-done.94 = f32[8576]{0:T(1024)S(1)} collective-permute-done((f32[8576]{0:T(1024)S(1)}, f32[8576]{0:T(1024)S(1)}, u32[]{:S(2)}, u32[]{:S(2)}) %collective-permute-start.94) | collective-permute-done | bytes 34336 | tf_op jit(solution)/shard_map/ppermute | solution.py:51
  (1053 shorter events, 640.1 us)
Async XLA Ops:
  7.2 80.4 %all-gather.7.cloned.1.call-start = ((), (), s32[]{:S(2)}) async-start(), calls=%async_computation.8 | async-start | bytes 2949120 | tf_op jit(solution)/shard_map/all_gather | solution.py:119
  23.7 153.9 %all-gather.9.cloned.1.call-start = ((), (), s32[]{:S(2)}) async-start(), calls=%async_computation.9 | async-start | bytes 6881280 | tf_op jit(solution)/shard_map/all_gather | solution.py:119
  47.6 39.5 %collective-permute-start.11 = (bf16[512,1536]{1,0:T(8,128)(2,1)}, bf16[512,1536]{1,0:T(8,128)(2,1)S(1)}, u32[]{:S(2)}, u32[]{:S(2)}) collective-permute-start(bf16[512,1536]{1,0:T(8,128)(2,1)} %get-tuple-element.132), channel_id=1, source_target_pairs={{0,1},{1,0},{2,3},{3,2},{4,5},{5,4},{6,7},{7,6},{8,9},{9,8},{10,11... | collective-permute-start | bytes 4718600 | tf_op jit(solution)/shard_map/ppermute | solution.py:51
  66.8 172.1 %all-gather.11.cloned.1.call-start = ((), (), s32[]{:S(2)}) async-start(), calls=%async_computation.10 | async-start | bytes 3440640 | tf_op jit(solution)/shard_map/all_gather | solution.py:119
  140.4 196.6 %all-gather.13.cloned.1.call-start = ((), (), s32[]{:S(2)}) async-start(), calls=%async_computation.11 | async-start | bytes 1966080 | tf_op jit(solution)/shard_map/all_gather | solution.py:119
  257.6 73.3 %collective-permute-start.49 = (bf16[3,96,896]{2,1,0:T(8,128)(2,1)}, bf16[3,96,896]{2,1,0:T(8,128)(2,1)}, u32[]{:S(2)}, u32[]{:S(2)}) collective-permute-start(bf16[3,96,896]{2,1,0:T(8,128)(2,1)} %get-tuple-element.173), channel_id=1, source_target_pairs={{0,24},{8,16},{16,8},{24,0},{1,25},{9,17},{17,9},{25,1},{2,26},{10... | collective-permute-start | bytes 1548296 | tf_op jit(solution)/shard_map/ppermute | solution.py:51
  287.7 32.2 %collective-permute-start.47 = (bf16[3,96,896]{2,1,0:T(8,128)(2,1)}, bf16[3,96,896]{2,1,0:T(8,128)(2,1)}, u32[]{:S(2)}, u32[]{:S(2)}) collective-permute-start(bf16[3,96,896]{2,1,0:T(8,128)(2,1)} %get-tuple-element.175), channel_id=1, source_target_pairs={{0,8},{8,0},{16,24},{24,16},{1,9},{9,1},{17,25},{25,17},{2,10},{10... | collective-permute-start | bytes 1548296 | tf_op jit(solution)/shard_map/ppermute | solution.py:51
  289.1 169.6 %all-gather.15.cloned.1.call-start = ((), (), s32[]{:S(2)}) async-start(), calls=%async_computation.12 | async-start | bytes 6881280 | tf_op jit(solution)/shard_map/all_gather | solution.py:119
  333.0 179.3 %all-gather.17.cloned.1.call-start = ((), (), s32[]{:S(2)}) async-start(), calls=%async_computation.13 | async-start | bytes 3440640 | tf_op jit(solution)/shard_map/all_gather | solution.py:119
  347.6 32.9 %collective-permute-start.37 = (bf16[4,256,128]{1,2,0:T(8,128)(2,1)S(1)}, bf16[4,256,128]{1,2,0:T(8,128)(2,1)S(1)}, u32[]{:S(2)}, u32[]{:S(2)}) collective-permute-start(bf16[4,256,128]{1,2,0:T(8,128)(2,1)S(1)} %pad_maximum_fusion.29), channel_id=1, source_target_pairs={{0,2},{2,4},{4,6},{1,3},{3,5},{5,7},{8,10},{10,12},{12,14},{9,11},... | collective-permute-start | bytes 786440 | tf_op jit(solution)/shard_map/ppermute | solution.py:60
  399.8 498.7 %reduce-scatter.23.cloned.1.call-start = ((), (), s32[]{:S(2)}) async-start(), calls=%async_computation.21 | async-start | bytes 3440640 | tf_op jit(solution)/shard_map/reduce_scatter | solution.py:134
  408.8 32.0 %collective-permute-start.51 = (bf16[128,1536]{1,0:T(8,128)(2,1)S(1)}, bf16[128,1536]{1,0:T(8,128)(2,1)S(1)}, u32[]{:S(2)}, u32[]{:S(2)}) collective-permute-start(bf16[128,1536]{1,0:T(8,128)(2,1)S(1)} %add_bitcast_fusion), channel_id=1, source_target_pairs={{0,16},{8,24},{16,0},{24,8},{1,17},{9,25},{17,1},{25,9},{2,18},{10... | collective-permute-start | bytes 1179656 | tf_op jit(solution)/shard_map/ppermute | solution.py:51
  426.0 31.2 %collective-permute-start.45 = (bf16[128,1536]{1,0:T(8,128)(2,1)S(1)}, bf16[128,1536]{1,0:T(8,128)(2,1)S(1)}, u32[]{:S(2)}, u32[]{:S(2)}) collective-permute-start(bf16[128,1536]{1,0:T(8,128)(2,1)S(1)} %multiply_convert_fusion.15), channel_id=1, source_target_pairs={{0,16},{8,24},{16,0},{24,8},{1,17},{9,25},{17,1},{25,9},{2,18},{10... | collective-permute-start | bytes 1179656 | tf_op jit(solution)/shard_map/ppermute | solution.py:51
  442.2 74.4 %collective-permute-start.53 = (bf16[512,1536]{1,0:T(8,128)(2,1)}, bf16[512,1536]{1,0:T(8,128)(2,1)}, u32[]{:S(2)}, u32[]{:S(2)}) collective-permute-start(bf16[512,1536]{1,0:T(8,128)(2,1)} %pad_maximum_fusion.9), channel_id=1, source_target_pairs={{0,1},{1,0},{2,3},{3,2},{4,5},{5,4},{6,7},{7,6},{8,9},{9,8},{10,11... | collective-permute-start | bytes 4718600 | tf_op jit(solution)/shard_map/ppermute | solution.py:51
  458.7 63.1 %collective-permute-start.54 = (bf16[512,1536]{1,0:T(8,128)(2,1)}, bf16[512,1536]{1,0:T(8,128)(2,1)}, u32[]{:S(2)}, u32[]{:S(2)}) collective-permute-start(bf16[512,1536]{1,0:T(8,128)(2,1)} %pad_maximum_fusion.8), channel_id=1, source_target_pairs={{0,1},{1,0},{2,3},{3,2},{4,5},{5,4},{6,7},{7,6},{8,9},{9,8},{10,11... | collective-permute-start | bytes 4718600 | tf_op jit(solution)/shard_map/ppermute | solution.py:51
  542.0 356.4 %reduce-scatter.21.cloned.1.call-start = ((), (), s32[]{:S(2)}) async-start(), calls=%async_computation.20 | async-start | bytes 3440640 | tf_op jit(solution)/shard_map/reduce_scatter | solution.py:134
  556.4 342.1 %reduce-scatter.19.cloned.1.call-start = ((), (), s32[]{:S(2)}) async-start(), calls=%async_computation.19 | async-start | bytes 3440640 | tf_op jit(solution)/shard_map/reduce_scatter | solution.py:134
  617.5 296.6 %reduce-scatter.17.cloned.1.call-start = ((), (), s32[]{:S(2)}) async-start(), calls=%async_computation.18 | async-start | bytes 1966080 | tf_op jit(solution)/shard_map/reduce_scatter | solution.py:134
  667.2 66.8 %collective-permute-start.63 = (bf16[512,1536]{1,0:T(8,128)(2,1)}, bf16[512,1536]{1,0:T(8,128)(2,1)}, u32[]{:S(2)}, u32[]{:S(2)}) collective-permute-start(bf16[512,1536]{1,0:T(8,128)(2,1)} %convolution_convert_fusion.2), channel_id=1, source_target_pairs={{0,1},{1,0},{2,3},{3,2},{4,5},{5,4},{6,7},{7,6},{8,9},{9,8},{10,11... | collective-permute-start | bytes 4718600 | tf_op jit(solution)/shard_map/ppermute | solution.py:51
  674.9 50.6 %collective-permute-start.69 = (bf16[4,256,128]{1,2,0:T(8,128)(2,1)S(1)}, bf16[4,256,128]{1,2,0:T(8,128)(2,1)S(1)}, u32[]{:S(2)}, u32[]{:S(2)}) collective-permute-start(bf16[4,256,128]{1,2,0:T(8,128)(2,1)S(1)} %get-tuple-element.233), channel_id=1, source_target_pairs={{4,0},{6,2},{5,1},{7,3},{12,8},{14,10},{13,9},{15,11},{20,16},{22,... | collective-permute-start | bytes 786440 | tf_op jit(solution)/shard_map/ppermute | solution.py:60
  745.3 32.1 %collective-permute-start.66 = (bf16[128,1536]{1,0:T(8,128)(2,1)S(1)}, bf16[128,1536]{1,0:T(8,128)(2,1)S(1)}, u32[]{:S(2)}, u32[]{:S(2)}) collective-permute-start(bf16[128,1536]{1,0:T(8,128)(2,1)S(1)} %get-tuple-element.199), channel_id=1, source_target_pairs={{0,8},{8,0},{16,24},{24,16},{1,9},{9,1},{17,25},{25,17},{2,10},{10... | collective-permute-start | bytes 1179656 | tf_op jit(solution)/shard_map/ppermute | solution.py:51
  786.8 199.7 %reduce-scatter.15.cloned.1.call-start = ((), (), s32[]{:S(2)}) async-start(), calls=%async_computation.17 | async-start | bytes 3440640 | tf_op jit(solution)/shard_map/reduce_scatter | solution.py:134
  811.8 174.7 %reduce-scatter.13.cloned.1.call-start = ((), (), s32[]{:S(2)}) async-start(), calls=%async_computation.16 | async-start | bytes 3440640 | tf_op jit(solution)/shard_map/reduce_scatter | solution.py:134
  834.7 158.1 %reduce-scatter.11.cloned.1.call-start = ((), (), s32[]{:S(2)}) async-start(), calls=%async_computation.15 | async-start | bytes 3440640 | tf_op jit(solution)/shard_map/reduce_scatter | solution.py:134
  895.8 149.1 %reduce-scatter.9.cloned.1.call-start = ((), (), s32[]{:S(2)}) async-start(), calls=%async_computation.14 | async-start | bytes 2949120 | tf_op jit(solution)/shard_map/reduce_scatter | solution.py:134
  915.9 38.8 %collective-permute-start.106 = (bf16[96,512]{1,0:T(8,128)(2,1)}, bf16[96,512]{1,0:T(8,128)(2,1)}, u32[]{:S(2)}, u32[]{:S(2)}) collective-permute-start(bf16[96,512]{1,0:T(8,128)(2,1)} %get-tuple-element.256), channel_id=1, source_target_pairs={{0,24},{8,16},{16,8},{24,0},{1,25},{9,17},{17,9},{25,1},{2,26},{10... | collective-permute-start | bytes 294920 | tf_op jit(solution)/shard_map/ppermute | solution.py:51
  917.6 39.5 %collective-permute-start.105 = (bf16[96,512]{1,0:T(8,128)(2,1)}, bf16[96,512]{1,0:T(8,128)(2,1)}, u32[]{:S(2)}, u32[]{:S(2)}) collective-permute-start(bf16[96,512]{1,0:T(8,128)(2,1)} %get-tuple-element.257), channel_id=1, source_target_pairs={{0,16},{8,24},{16,0},{24,8},{1,17},{9,25},{17,1},{25,9},{2,18},{10... | collective-permute-start | bytes 294920 | tf_op jit(solution)/shard_map/ppermute | solution.py:51
  918.9 38.3 %collective-permute-start.104 = (bf16[96,512]{1,0:T(8,128)(2,1)}, bf16[96,512]{1,0:T(8,128)(2,1)}, u32[]{:S(2)}, u32[]{:S(2)}) collective-permute-start(bf16[96,512]{1,0:T(8,128)(2,1)} %get-tuple-element.258), channel_id=1, source_target_pairs={{0,8},{8,0},{16,24},{24,16},{1,9},{9,1},{17,25},{25,17},{2,10},{10... | collective-permute-start | bytes 294920 | tf_op jit(solution)/shard_map/ppermute | solution.py:51
  922.4 39.2 %collective-permute-start.109 = (bf16[3,96,896]{2,1,0:T(8,128)(2,1)}, bf16[3,96,896]{2,1,0:T(8,128)(2,1)}, u32[]{:S(2)}, u32[]{:S(2)}) collective-permute-start(bf16[3,96,896]{2,1,0:T(8,128)(2,1)} %get-tuple-element.166), channel_id=1, source_target_pairs={{0,24},{8,16},{16,8},{24,0},{1,25},{9,17},{17,9},{25,1},{2,26},{10... | collective-permute-start | bytes 1548296 | tf_op jit(solution)/shard_map/ppermute | solution.py:51
  998.8 33.8 %collective-permute-start.103 = (bf16[3,96,896]{2,1,0:T(8,128)(2,1)S(1)}, bf16[3,96,896]{2,1,0:T(8,128)(2,1)S(1)}, u32[]{:S(2)}, u32[]{:S(2)}) collective-permute-start(bf16[3,96,896]{2,1,0:T(8,128)(2,1)S(1)} %get-tuple-element.170), channel_id=1, source_target_pairs={{0,24},{8,16},{16,8},{24,0},{1,25},{9,17},{17,9},{25,1},{2,26},{10... | collective-permute-start | bytes 1548296 | tf_op jit(solution)/shard_map/ppermute | solution.py:51
  999.8 32.8 %collective-permute-start.102 = (bf16[3,96,896]{2,1,0:T(8,128)(2,1)S(1)}, bf16[3,96,896]{2,1,0:T(8,128)(2,1)S(1)}, u32[]{:S(2)}, u32[]{:S(2)}) collective-permute-start(bf16[3,96,896]{2,1,0:T(8,128)(2,1)S(1)} %get-tuple-element.171), channel_id=1, source_target_pairs={{0,16},{8,24},{16,0},{24,8},{1,17},{9,25},{17,1},{25,9},{2,18},{10... | collective-permute-start | bytes 1548296 | tf_op jit(solution)/shard_map/ppermute | solution.py:51
  1000.8 31.8 %collective-permute-start.101 = (bf16[3,96,896]{2,1,0:T(8,128)(2,1)S(1)}, bf16[3,96,896]{2,1,0:T(8,128)(2,1)S(1)}, u32[]{:S(2)}, u32[]{:S(2)}) collective-permute-start(bf16[3,96,896]{2,1,0:T(8,128)(2,1)S(1)} %get-tuple-element.172), channel_id=1, source_target_pairs={{0,8},{8,0},{16,24},{24,16},{1,9},{9,1},{17,25},{25,17},{2,10},{10... | collective-permute-start | bytes 1548296 | tf_op jit(solution)/shard_map/ppermute | solution.py:51
  (331 other events, 4238.3 us)
Sparse Core Ops, SparseCore 0:
  23.9 50.7 all-gather.6
  76.2 101.3 all-gather.8
  179.7 59.1 all-gather.10
  289.3 34.9 all-gather.12
  333.1 112.9 all-gather.14
  447.5 64.7 all-gather.16
  542.2 52.9 reduce-scatter.22
  597.4 53.8 reduce-scatter.20
  653.7 70.5 reduce-scatter.18
  786.9 32.8 reduce-scatter.16
  822.1 53.1 reduce-scatter.14
  877.5 56.0 reduce-scatter.12
  935.9 56.8 reduce-scatter.10
  994.9 49.3 reduce-scatter.8

commit v3 on v2

--- a/solution.py
+++ b/solution.py
@@ -232,8 +232,9 @@
 
 
 def feed_active(tokens, lift, mask):
-    gate = dot("td,df->tf", tokens, lift[0])
-    up = dot("td,df->tf", tokens, lift[1])
+    both = dot("td,df->tf", tokens, lift)
+    width = both.shape[1] // 2
+    gate, up = both[:, :width], both[:, width:]
     return gate, up, (jax.nn.silu(gate) * up * mask).astype(bf16)
 
 
@@ -241,7 +242,7 @@
     back_active = dot("td,df->tf", back_tokens, drop) * mask
     sigmoid_value = jax.nn.sigmoid(gate)
     back_gate = back_active * up * sigmoid_value * (1.0 + gate * (1.0 - sigmoid_value))
-    return back_gate.astype(bf16), (back_active * gate * sigmoid_value).astype(bf16)
+    return jnp.concatenate([back_gate, back_active * gate * sigmoid_value], axis=1).astype(bf16)
 
 
 def feed_forward(team, hidden, gain, lift, mask):
@@ -251,19 +252,20 @@
     return inverse, normed, tokens, gate, up, active
 
 
-def feed_backward(team, back_out, back_tokens, stored, gain, lift, drop, mask):
+def held(array, token):
+    return array + zero(token).astype(array.dtype)
+
+
+def feed_backward(team, back_out, back_tokens, stored, gain, lift, drop, mask, hold):
     inverse, normed, tokens, gate, up, active = stored
-    back_gate, back_up = zip(
-        *[feed_back(back_tokens[i], gate[i], up[i], drop, mask) for i in range(2)]
-    )
-    terms = [
-        dot("tf,df->td", back_gate[i], lift[0]) + dot("tf,df->td", back_up[i], lift[1]) for i in (1, 0)
-    ]
-    back_normed, sent = scatter_tokens(team, terms[1], terms[0])
-    drop_term = outer(back_tokens, active)
-    lift_terms = [outer(tokens, back_gate), outer(tokens, back_up)]
+    back_pair = [feed_back(back_tokens[i], gate[i], up[i], drop, mask) for i in range(2)]
+    back_normed, sent = project_out(team, "tf,df->td", back_pair, lift)
+    drop_part = summed_rows(team, outer(back_tokens, active))
+    lift_part = summed_rows(team, outer(tokens, back_pair))
+    if hold:
+        gain = held(gain, drop_part)
     back_hidden, gain_term = after_norm(back_out, back_normed, normed, inverse, gain)
-    return back_hidden, gain_term, lift_terms + [drop_term]
+    return back_hidden, gain_term, drop_part, lift_part
 
 
 def mixer_forward(team, core, hidden, token_halves, order, gain, weights, taps):
@@ -380,7 +382,7 @@
     return hidden + out, stored, mixed
 
 
-def attend_backward(team, core, back_out, stored, gain, weights, query_gain, key_gain):
+def attend_backward(team, core, back_out, stored, gain, weights, query_gain, key_gain, before):
     (
         inverse,
         normed,
@@ -401,7 +403,7 @@
     heads = groups * repeat
     inner = (heads + 2 * groups) * HD
     back_tokens = gather_tokens(team, back_out.astype(bf16))
-    back_attended = true_order(core, team.size, project("td,dc->tc", back_tokens, weights[:, inner:])).astype(bf16)
+    back_attended = true_order(core, team.size, project("td,dc->tc", back_tokens, held(weights[:, inner:], before[0]))).astype(bf16)
     back_grouped = back_attended.reshape(sequences, count, groups, repeat, HD)
     back_probs = dot("vqgrd,vkgd->vgrqk", back_grouped, values)
     row_dot = jnp.sum(probs * back_probs, axis=-1, keepdims=True)
@@ -435,7 +437,7 @@
         axis=-1,
     ).astype(bf16)
     back_mixed = own_halves(core, back_mixed)
-    back_normed, sent = project_out(team, "tc,dc->td", back_mixed, weights[:, :inner])
+    back_normed, sent = project_out(team, "tc,dc->td", back_mixed, held(weights[:, :inner], before[1]))
     term = jnp.concatenate([outer(tokens, back_mixed), outer(back_tokens, attended)], axis=-1)
     back_hidden, gain_term = after_norm(back_out, back_normed, normed, inverse, gain)
     return back_hidden, gain_term, term, (query_scale_term, key_scale_term), back_attended
@@ -489,9 +491,20 @@
     second_mask = hidden_mask(units, second_team.size, second_team.seat)
 
     def feed_piece(on, lift, drop, late):
-        both = jnp.concatenate([lift.transpose(1, 0, 2), drop[None]], axis=0)
         width = hidden_width(units, on.size)
-        return lambda seat: lax.dynamic_slice_in_dim(both, hidden_start(units, on.size, seat) + late, width, 2)
+
+        def piece(seat):
+            start = hidden_start(units, on.size, seat) + late
+            parts = [lift[:, 0], lift[:, 1], drop]
+            return jnp.concatenate([lax.dynamic_slice_in_dim(part, start, width, 1) for part in parts], axis=1)
+
+        return piece
+
+    def lift_of(pieces):
+        return [piece[:, : 2 * piece.shape[1] // 3] for piece in pieces]
+
+    def drop_of(pieces):
+        return [piece[:, 2 * piece.shape[1] // 3 :] for piece in pieces]
 
     token_halves = gather_tokens(team, own_tokens)
     packed = pack_mixer(mixer_in, mixer_out)
@@ -500,8 +513,8 @@
     near_done = zero(got[-1])
 
     got_first = team_rows(first_team, feed_piece(first_team, first_lift, first_drop, near_done))
-    first_lift_all = all_rows(first_team, [piece[:2] for piece in got_first])
-    first_drop_all = all_rows(first_team, [piece[2] for piece in got_first])
+    first_lift_all = all_rows(first_team, lift_of(got_first))
+    first_drop_all = all_rows(first_team, drop_of(got_first))
     near_done = zero(got_first[-1])
 
     gain_rows = mixer_gain.shape[0]
@@ -521,8 +534,8 @@
     )
     mixed_done = zero(parts)
     attend_weights = all_rows(team, got_attend, mixed_done)
-    second_lift_all = all_rows(second_team, [piece[:2] for piece in got_second], mixed_done)
-    second_drop_all = all_rows(second_team, [piece[2] for piece in got_second], mixed_done)
+    second_lift_all = all_rows(second_team, lift_of(got_second), mixed_done)
+    second_drop_all = all_rows(second_team, drop_of(got_second), mixed_done)
 
     first_stored = feed_forward(first_team, after_mixer, gains[1], first_lift_all, first_mask)
     out, sent = project_out(first_team, "tf,df->td", first_stored[-1], first_drop_all)
@@ -534,12 +547,11 @@
     signal_tokens = gather_tokens(second_team, signal_low)
     second_stored = feed_forward(second_team, after_attend, gains[3], second_lift_all, second_mask)
 
-    back, second_gain_term, second_terms = feed_backward(
-        second_team, signal, signal_tokens, second_stored, gains[3], second_lift_all, second_drop_all, second_mask
-    )
-    second_part = [summed_rows(second_team, term) for term in second_terms]
+    back, second_gain_term, *second_part = feed_backward(
+        second_team, signal, signal_tokens, second_stored, gains[3], second_lift_all, second_drop_all, second_mask, False
+    )
     back, attend_gain_term, attend_term, scale_terms, back_attended = attend_backward(
-        team, core, back, attend_stored, gains[2], attend_weights, query_gain, key_gain
+        team, core, back, attend_stored, gains[2], attend_weights, query_gain, key_gain, second_part
     )
     attend_part = summed_rows(team, attend_term)
     late = zero(back_attended).astype(bf16)
@@ -547,18 +559,17 @@
     result = after_attend + out
 
     first_back_tokens = gather_tokens(first_team, back.astype(bf16))
-    back, first_gain_term, first_terms = feed_backward(
-        first_team, back, first_back_tokens, first_stored, gains[1], first_lift_all, first_drop_all, first_mask
-    )
-    first_part = [summed_rows(first_team, term) for term in first_terms]
+    back, first_gain_term, *first_part = feed_backward(
+        first_team, back, first_back_tokens, first_stored, gains[1], first_lift_all, first_drop_all, held(first_mask, attend_part), True
+    )
     back, mixer_gain_term, mixer_term, tap_term, back_gated = mixer_backward(
         team, core, back, mixer_stored, gains[0], mixer_weights, taps
     )
     mixer_part = summed_rows(team, mixer_term)
     gated_done = zero(back_gated)
-    second_total = every_seat(second_team, jnp.stack(second_part), gated_done)
+    second_total = every_seat(second_team, jnp.concatenate(second_part[::-1], axis=-1), gated_done)
     attend_total = every_seat(team, attend_part, gated_done)
-    first_total = every_seat(first_team, jnp.stack(first_part))
+    first_total = every_seat(first_team, jnp.concatenate(first_part[::-1], axis=-1))
     mixer_total = every_seat(team, mixer_part)
 
     small = jnp.concatenate(
@@ -577,6 +588,13 @@
 
     def both_cores(own):
         return true_order(core, 1, [own, swap_core(own)])
+
+    def joined_lift(total):
+        width = total.shape[-1] // 3
+        return jnp.stack([joined_hidden(units, total[..., k * width : (k + 1) * width]) for k in range(2)], axis=1)
+
+    def joined_drop(total):
+        return joined_hidden(units, total[..., 2 * total.shape[-1] // 3 :])
 
     rows = mixer_in.shape[0]
     in_columns = 3 * channels
@@ -590,8 +608,8 @@
         tap_total,
         all_seats(mixer_total[..., in_columns:]),
         gain_totals[1],
-        joined_hidden(units, first_total[:, :2]).transpose(1, 0, 2),
-        joined_hidden(units, first_total[:, 2]),
+        joined_lift(first_total),
+        joined_drop(first_total),
         gain_totals[2],
         all_seats(attend_total[..., :queries]),
         all_seats(attend_total[..., queries:inner].reshape(4, rows, 2, -1)),
@@ -599,8 +617,8 @@
         scale_totals[1],
         all_seats(attend_total[..., inner:]),
         gain_totals[3],
-        joined_hidden(units, second_total[:, :2]).transpose(1, 0, 2),
-        joined_hidden(units, second_total[:, 2]),
+        joined_lift(second_total),
+        joined_drop(second_total),
     )
 
 

time: 1070 us -> 1050 us (0.981)
  waiting for transfers between devices: 511 us -> 466 us
  local copies, waits for them, and re-layouts: 118 us -> 145 us
    all_gather x6, waiting for transfers between devices: 105 us -> 32.8 us  [all_rows(): whole = lax.all_gather(near, team.across, axis=len(lead) + 1, tiled=True)]
    dynamic_slice x0 -> x6, local copies, waits for them, and re-layouts: none -> 19.1 us  [piece(): lax.dynamic_slice_in_dim(part, start, width, 1)]
    ppermute x102, waiting for transfers between devices: 307 us -> 324 us  [swap(): lax.ppermute(array, axis, [(i, i ^ mask) for i in range(lax.axis_size(axi...]
    reduce_scatter x8 -> x6, waiting for transfers between devices: 6.28 us -> 20.8 us  [summed_rows(): lax.psum_scatter(split.reshape(-1, columns), team.across, scatter_dimensi...]
    unnamed x494 -> x518, local copies, waits for them, and re-layouts: 39.6 us -> 47.6 us
    dot_general x66 -> x54, matrix products: 207 us -> 200 us  [dot(): return jnp.einsum(pattern, first, second, preferred_element_type=f32)]
  transfers between devices with their start and end apart: 124 -> 122, of which waited for: 70 -> 68; matrix products, arithmetic and copies ran while one was open for 33% -> 36% of each run, Pallas kernels for 0% -> 0%
where the time goes in v3:
time: 1050 us; the launch traced here: 1040 us
  waiting for transfers between devices  466 us (44%)
  matrix products  200 us (19%)
  local copies, waits for them, and re-layouts  145 us (14%)
  starting transfers between devices  121 us (12%)
  other arithmetic  82.3 us (8%)
  between operations  26.1 us (2%)
    ppermute x102, waiting for transfers between devices, swap(): lax.ppermute(array, axis, [(i, i ^ mask) for i in range(lax.axis_size(axi...  324 us
    dot_general x54, matrix products, dot(): return jnp.einsum(pattern, first, second, preferred_element_type=f32)  200 us
    ppermute x102, starting transfers between devices, swap(): lax.ppermute(array, axis, [(i, i ^ mask) for i in range(lax.axis_size(axi...  104 us
    ppermute x8, waiting for transfers between devices, shift(): lax.ppermute(array, 'seq', [(i, i + by) for i in range(count) if 0 <= i +...  88.9 us
    unnamed x518, local copies, waits for them, and re-layouts  47.6 us
    all_gather x6, waiting for transfers between devices, all_rows(): whole = lax.all_gather(near, team.across, axis=len(lead) + 1, tiled=True)  32.8 us
  transfers between devices with their start and end apart: 122, of which 68 were waited for; matrix products, arithmetic and copies ran while one was open for 36% of the time, Pallas kernels for 0%

profile of v3, /device:TPU:0, one launch (start us, length us, event | category | flops | bytes accessed | tf_op | source)
XLA Modules:
  0.0 1041.3 jit_solution(18123649489265724924)
XLA Ops:
  42.1 19.6 %collective-permute-done.23 = bf16[96,2688]{1,0:T(8,128)(2,1)S(1)} collective-permute-done((bf16[96,2688]{1,0:T(8,128)(2,1)S(1)}, bf16[96,2688]{1,0:T(8,128)(2,1)S(1)}, u32[]{:S(2)}, u32[]{:S(2)}) %collective-permute-start.23) | collective-permute-done | bytes 516128 | tf_op jit(solution)/shard_map/ppermute | solution.py:51
  79.4 7.6 collective-permute-done.1
  128.8 8.0 collective-permute-done.12
  165.7 7.6 collective-permute-done.19
  224.9 15.0 %all-gather.11.cloned.1.call-done = bf16[4,384,896]{2,1,0:T(8,128)(2,1)} async-done(((bf16[4,96,896]{2,1,0:T(8,128)(2,1)}), bf16[4,384,896]{2,1,0:T(8,128)(2,1)}) %all-gather.11.cloned.1.call-update) | async-done | bytes 2752528 | tf_op jit(solution)/shard_map/all_gather | solution.py:119
  250.8 8.8 collective-permute-done.47
  259.6 12.0 %collective-permute-done.48 = bf16[96,2688]{1,0:T(8,128)(2,1)S(1)} collective-permute-done((bf16[96,2688]{1,0:T(8,128)(2,1)S(1)}, bf16[96,2688]{1,0:T(8,128)(2,1)S(1)}, u32[]{:S(2)}, u32[]{:S(2)}) %collective-permute-start.48) | collective-permute-done | bytes 516128 | tf_op jit(solution)/shard_map/ppermute | solution.py:51
  304.7 8.1 collective-permute-done.32
  379.2 7.7 collective-permute-done.51
  406.9 9.4 collective-permute-done.46
  430.8 17.8 %all-gather.15.cloned.1.call-done = bf16[4,384,1792]{2,1,0:T(8,128)(2,1)} async-done(((bf16[4,96,1792]{2,1,0:T(8,128)(2,1)}), bf16[4,384,1792]{2,1,0:T(8,128)(2,1)}) %all-gather.15.cloned.1.call-update) | async-done | bytes 5505040 | tf_op jit(solution)/shard_map/all_gather | solution.py:119
  486.2 9.4 collective-permute-done.56
  495.6 8.0 collective-permute-done.58
  509.4 9.3 collective-permute-done.61
  529.5 7.8 fusion.39
  562.6 7.9 fusion.21
  579.0 10.0 fusion
  615.1 21.5 %collective-permute-done.68 = bf16[4,256,128]{1,2,0:T(8,128)(2,1)S(1)} collective-permute-done((bf16[4,256,128]{1,2,0:T(8,128)(2,1)S(1)}, bf16[4,256,128]{1,2,0:T(8,128)(2,1)S(1)}, u32[]{:S(2)}, u32[]{:S(2)}) %collective-permute-start.68) | collective-permute-done | bytes 262176 | tf_op jit(solution)/shard_map/ppermute | solution.py:60
  636.6 23.0 %collective-permute-done.69 = bf16[4,256,128]{1,2,0:T(8,128)(2,1)S(1)} collective-permute-done((bf16[4,256,128]{1,2,0:T(8,128)(2,1)S(1)}, bf16[4,256,128]{1,2,0:T(8,128)(2,1)S(1)}, u32[]{:S(2)}, u32[]{:S(2)}) %collective-permute-start.69) | collective-permute-done | bytes 262176 | tf_op jit(solution)/shard_map/ppermute | solution.py:60
  708.5 8.0 collective-permute-done.66
  751.1 11.5 %reduce-scatter.11.cloned.1.call-done = bf16[384,512]{1,0:T(8,128)(2,1)} async-done(((bf16[1536,512]{1,0:T(8,128)(2,1)}), bf16[384,512]{1,0:T(8,128)(2,1)}) %reduce-scatter.11.cloned.1.call-update) | async-done | bytes 393232 | tf_op jit(solution)/shard_map/reduce_scatter | solution.py:134
  777.7 7.6 fusion.37
  785.4 7.7 add_convert_fusion
  796.4 7.9 fusion.265
  808.6 9.2 reduce-scatter.13.cloned.1.call-done
  833.7 9.4 collective-permute-done.85
  843.1 7.6 collective-permute-done.84
  886.3 24.1 %collective-permute-done.87 = f32[4,2,192]{1,2,0:T(8,128)S(1)} collective-permute-done((f32[4,2,192]{1,2,0:T(8,128)S(1)}, f32[4,2,192]{1,2,0:T(8,128)S(1)}, u32[]{:S(2)}, u32[]{:S(2)}) %collective-permute-start.87) | collective-permute-done | bytes 6176 | tf_op jit(solution)/shard_map/ppermute | solution.py:60
  933.3 8.4 collective-permute-done.109
  953.7 9.3 collective-permute-done.89
  998.4 8.5 collective-permute-done.101
  1006.9 8.2 collective-permute-done.102
  (1076 shorter events, 669.5 us)
Async XLA Ops:
  7.2 110.3 %all-gather.7.cloned.1.call-start = ((), (), s32[]{:S(2)}) async-start(), calls=%async_computation.6 | async-start | bytes 2949120 | tf_op jit(solution)/shard_map/all_gather | solution.py:119
  23.7 186.4 %all-gather.9.cloned.1.call-start = ((), (), s32[]{:S(2)}) async-start(), calls=%async_computation.7 | async-start | bytes 6881280 | tf_op jit(solution)/shard_map/all_gather | solution.py:119
  38.2 24.7 %collective-permute-start.4 = (bf16[96,2688]{1,0:T(8,128)(2,1)S(1)}, bf16[96,2688]{1,0:T(8,128)(2,1)S(1)}, u32[]{:S(2)}, u32[]{:S(2)}) collective-permute-start(bf16[96,2688]{1,0:T(8,128)(2,1)S(1)} %pad_maximum_fusion.39), channel_id=1, source_target_pairs={{0,24},{8,16},{16,8},{24,0},{1,25},{9,17},{17,9},{25,1},{2,26},{10... | collective-permute-start | bytes 1548296 | tf_op jit(solution)/shard_map/ppermute | solution.py:51
  65.6 174.3 %all-gather.11.cloned.1.call-start = ((), (), s32[]{:S(2)}) async-start(), calls=%async_computation.8 | async-start | bytes 3440640 | tf_op jit(solution)/shard_map/all_gather | solution.py:119
  88.5 28.6 %collective-permute-start.11 = (bf16[512,1536]{1,0:T(8,128)(2,1)}, bf16[512,1536]{1,0:T(8,128)(2,1)S(1)}, u32[]{:S(2)}, u32[]{:S(2)}) collective-permute-start(bf16[512,1536]{1,0:T(8,128)(2,1)} %get-tuple-element.112), channel_id=1, source_target_pairs={{0,1},{1,0},{2,3},{3,2},{4,5},{5,4},{6,7},{7,6},{8,9},{9,8},{10,11... | collective-permute-start | bytes 4718600 | tf_op jit(solution)/shard_map/ppermute | solution.py:51
  148.5 174.1 %all-gather.13.cloned.1.call-start = ((), (), s32[]{:S(2)}) async-start(), calls=%async_computation.9 | async-start | bytes 1966080 | tf_op jit(solution)/shard_map/all_gather | solution.py:119
  209.9 215.6 %all-gather.17.cloned.1.call-start = ((), (), s32[]{:S(2)}) async-start(), calls=%async_computation.11 | async-start | bytes 3440640 | tf_op jit(solution)/shard_map/all_gather | solution.py:119
  244.8 29.4 %collective-permute-start.26 = (bf16[512,1536]{1,0:T(8,128)(2,1)}, bf16[512,1536]{1,0:T(8,128)(2,1)}, u32[]{:S(2)}, u32[]{:S(2)}) collective-permute-start(bf16[512,1536]{1,0:T(8,128)(2,1)} %convolution_convert_fusion.6), channel_id=1, source_target_pairs={{0,1},{1,0},{2,3},{3,2},{4,5},{5,4},{6,7},{7,6},{8,9},{9,8},{10,11... | collective-permute-start | bytes 4718600 | tf_op jit(solution)/shard_map/ppermute | solution.py:51
  246.6 25.0 %collective-permute-start.48 = (bf16[96,2688]{1,0:T(8,128)(2,1)S(1)}, bf16[96,2688]{1,0:T(8,128)(2,1)S(1)}, u32[]{:S(2)}, u32[]{:S(2)}) collective-permute-start(bf16[96,2688]{1,0:T(8,128)(2,1)S(1)} %pad_maximum_fusion.43), channel_id=1, source_target_pairs={{0,16},{8,24},{16,0},{24,8},{1,17},{9,25},{17,1},{25,9},{2,18},{10... | collective-permute-start | bytes 1548296 | tf_op jit(solution)/shard_map/ppermute | solution.py:51
  274.1 174.4 %all-gather.15.cloned.1.call-start = ((), (), s32[]{:S(2)}) async-start(), calls=%async_computation.10 | async-start | bytes 6881280 | tf_op jit(solution)/shard_map/all_gather | solution.py:119
  322.3 224.0 %reduce-scatter.7.cloned.1.call-start = ((), (), s32[]{:S(2)}) async-start(), calls=%async_computation.12 | async-start | bytes 3440640 | tf_op jit(solution)/shard_map/reduce_scatter | solution.py:134
  370.0 25.3 %collective-permute-start.41 = (bf16[128,1536]{1,0:T(8,128)(2,1)S(1)}, bf16[128,1536]{1,0:T(8,128)(2,1)S(1)}, u32[]{:S(2)}, u32[]{:S(2)}) collective-permute-start(bf16[128,1536]{1,0:T(8,128)(2,1)S(1)} %get-tuple-element.180), channel_id=1, source_target_pairs={{0,24},{8,16},{16,8},{24,0},{1,25},{9,17},{17,9},{25,1},{2,26},{10... | collective-permute-start | bytes 1179656 | tf_op jit(solution)/shard_map/ppermute | solution.py:51
  371.3 30.9 %collective-permute-start.43 = (bf16[128,1536]{1,0:T(8,128)(2,1)S(1)}, bf16[128,1536]{1,0:T(8,128)(2,1)S(1)}, u32[]{:S(2)}, u32[]{:S(2)}) collective-permute-start(bf16[128,1536]{1,0:T(8,128)(2,1)S(1)} %get-tuple-element.181), channel_id=1, source_target_pairs={{0,8},{8,0},{16,24},{24,16},{1,9},{9,1},{17,25},{25,17},{2,10},{10... | collective-permute-start | bytes 1179656 | tf_op jit(solution)/shard_map/ppermute | solution.py:51
  388.3 37.3 %collective-permute-start.53 = (bf16[512,1536]{1,0:T(8,128)(2,1)}, bf16[512,1536]{1,0:T(8,128)(2,1)}, u32[]{:S(2)}, u32[]{:S(2)}) collective-permute-start(bf16[512,1536]{1,0:T(8,128)(2,1)} %pad_maximum_fusion.13), channel_id=1, source_target_pairs={{0,1},{1,0},{2,3},{3,2},{4,5},{5,4},{6,7},{7,6},{8,9},{9,8},{10,11... | collective-permute-start | bytes 4718600 | tf_op jit(solution)/shard_map/ppermute | solution.py:51
  425.4 29.3 %collective-permute-start.54 = (bf16[512,1536]{1,0:T(8,128)(2,1)}, bf16[512,1536]{1,0:T(8,128)(2,1)}, u32[]{:S(2)}, u32[]{:S(2)}) collective-permute-start(bf16[512,1536]{1,0:T(8,128)(2,1)} %pad_maximum_fusion.12), channel_id=1, source_target_pairs={{0,1},{1,0},{2,3},{3,2},{4,5},{5,4},{6,7},{7,6},{8,9},{9,8},{10,11... | collective-permute-start | bytes 4718600 | tf_op jit(solution)/shard_map/ppermute | solution.py:51
  475.9 186.1 %reduce-scatter.9.cloned.1.call-start = ((), (), s32[]{:S(2)}) async-start(), calls=%async_computation.13 | async-start | bytes 6881280 | tf_op jit(solution)/shard_map/reduce_scatter | solution.py:134
  546.0 216.5 %reduce-scatter.11.cloned.1.call-start = ((), (), s32[]{:S(2)}) async-start(), calls=%async_computation.14 | async-start | bytes 1966080 | tf_op jit(solution)/shard_map/reduce_scatter | solution.py:134
  578.4 94.5 %collective-permute-start.63 = (bf16[512,1536]{1,0:T(8,128)(2,1)}, bf16[512,1536]{1,0:T(8,128)(2,1)}, u32[]{:S(2)}, u32[]{:S(2)}) collective-permute-start(bf16[512,1536]{1,0:T(8,128)(2,1)} %convolution_convert_fusion.3), channel_id=1, source_target_pairs={{0,1},{1,0},{2,3},{3,2},{4,5},{5,4},{6,7},{7,6},{8,9},{9,8},{10,11... | collective-permute-start | bytes 4718600 | tf_op jit(solution)/shard_map/ppermute | solution.py:51
  606.6 29.9 %collective-permute-start.68 = (bf16[4,256,128]{1,2,0:T(8,128)(2,1)S(1)}, bf16[4,256,128]{1,2,0:T(8,128)(2,1)S(1)}, u32[]{:S(2)}, u32[]{:S(2)}) collective-permute-start(bf16[4,256,128]{1,2,0:T(8,128)(2,1)S(1)} %get-tuple-element.227), channel_id=1, source_target_pairs={{2,0},{4,2},{6,4},{3,1},{5,3},{7,5},{10,8},{12,10},{14,12},{11,9},... | collective-permute-start | bytes 786440 | tf_op jit(solution)/shard_map/ppermute | solution.py:60
  608.2 28.4 %collective-permute-start.70 = (bf16[4,256,128]{1,2,0:T(8,128)(2,1)S(1)}, bf16[4,256,128]{1,2,0:T(8,128)(2,1)S(1)}, u32[]{:S(2)}, u32[]{:S(2)}) collective-permute-start(bf16[4,256,128]{1,2,0:T(8,128)(2,1)S(1)} %get-tuple-element.228), channel_id=1, source_target_pairs={{6,0},{7,1},{14,8},{15,9},{22,16},{23,17},{30,24},{31,25}} | collective-permute-start | bytes 786440 | tf_op jit(solution)/shard_map/ppermute | solution.py:60
  609.5 50.1 %collective-permute-start.69 = (bf16[4,256,128]{1,2,0:T(8,128)(2,1)S(1)}, bf16[4,256,128]{1,2,0:T(8,128)(2,1)S(1)}, u32[]{:S(2)}, u32[]{:S(2)}) collective-permute-start(bf16[4,256,128]{1,2,0:T(8,128)(2,1)S(1)} %get-tuple-element.229), channel_id=1, source_target_pairs={{4,0},{6,2},{5,1},{7,3},{12,8},{14,10},{13,9},{15,11},{20,16},{22,... | collective-permute-start | bytes 786440 | tf_op jit(solution)/shard_map/ppermute | solution.py:60
  682.3 26.1 %collective-permute-start.64 = (bf16[128,1536]{1,0:T(8,128)(2,1)S(1)}, bf16[128,1536]{1,0:T(8,128)(2,1)S(1)}, u32[]{:S(2)}, u32[]{:S(2)}) collective-permute-start(bf16[128,1536]{1,0:T(8,128)(2,1)S(1)} %get-tuple-element.174), channel_id=1, source_target_pairs={{0,24},{8,16},{16,8},{24,0},{1,25},{9,17},{17,9},{25,1},{2,26},{10... | collective-permute-start | bytes 1179656 | tf_op jit(solution)/shard_map/ppermute | solution.py:51
  684.3 32.1 %collective-permute-start.66 = (bf16[128,1536]{1,0:T(8,128)(2,1)S(1)}, bf16[128,1536]{1,0:T(8,128)(2,1)S(1)}, u32[]{:S(2)}, u32[]{:S(2)}) collective-permute-start(bf16[128,1536]{1,0:T(8,128)(2,1)S(1)} %get-tuple-element.175), channel_id=1, source_target_pairs={{0,8},{8,0},{16,24},{24,16},{1,9},{9,1},{17,25},{25,17},{2,10},{10... | collective-permute-start | bytes 1179656 | tf_op jit(solution)/shard_map/ppermute | solution.py:51
  691.6 24.9 %collective-permute-start.65 = (bf16[128,1536]{1,0:T(8,128)(2,1)S(1)}, bf16[128,1536]{1,0:T(8,128)(2,1)S(1)}, u32[]{:S(2)}, u32[]{:S(2)}) collective-permute-start(bf16[128,1536]{1,0:T(8,128)(2,1)S(1)} %get-tuple-element.176), channel_id=1, source_target_pairs={{0,16},{8,24},{16,0},{24,8},{1,17},{9,25},{17,1},{25,9},{2,18},{10... | collective-permute-start | bytes 1179656 | tf_op jit(solution)/shard_map/ppermute | solution.py:51
  725.9 91.9 %reduce-scatter.13.cloned.1.call-start = ((), (), s32[]{:S(2)}) async-start(), calls=%async_computation.15 | async-start | bytes 3440640 | tf_op jit(solution)/shard_map/reduce_scatter | solution.py:134
  751.0 238.5 %reduce-scatter.17.cloned.1.call-start = ((), (), s32[]{:S(2)}) async-start(), calls=%async_computation.17 | async-start | bytes 6881280 | tf_op jit(solution)/shard_map/reduce_scatter | solution.py:134
  795.9 224.3 %reduce-scatter.15.cloned.1.call-start = ((), (), s32[]{:S(2)}) async-start(), calls=%async_computation.16 | async-start | bytes 2949120 | tf_op jit(solution)/shard_map/reduce_scatter | solution.py:134
  872.3 54.2 %collective-permute-start.106 = (bf16[96,512]{1,0:T(8,128)(2,1)}, bf16[96,512]{1,0:T(8,128)(2,1)}, u32[]{:S(2)}, u32[]{:S(2)}) collective-permute-start(bf16[96,512]{1,0:T(8,128)(2,1)} %get-tuple-element.258), channel_id=1, source_target_pairs={{0,24},{8,16},{16,8},{24,0},{1,25},{9,17},{17,9},{25,1},{2,26},{10... | collective-permute-start | bytes 294920 | tf_op jit(solution)/shard_map/ppermute | solution.py:51
  873.9 55.1 %collective-permute-start.105 = (bf16[96,512]{1,0:T(8,128)(2,1)}, bf16[96,512]{1,0:T(8,128)(2,1)}, u32[]{:S(2)}, u32[]{:S(2)}) collective-permute-start(bf16[96,512]{1,0:T(8,128)(2,1)} %get-tuple-element.259), channel_id=1, source_target_pairs={{0,16},{8,24},{16,0},{24,8},{1,17},{9,25},{17,1},{25,9},{2,18},{10... | collective-permute-start | bytes 294920 | tf_op jit(solution)/shard_map/ppermute | solution.py:51
  875.4 53.6 %collective-permute-start.104 = (bf16[96,512]{1,0:T(8,128)(2,1)}, bf16[96,512]{1,0:T(8,128)(2,1)}, u32[]{:S(2)}, u32[]{:S(2)}) collective-permute-start(bf16[96,512]{1,0:T(8,128)(2,1)} %get-tuple-element.260), channel_id=1, source_target_pairs={{0,8},{8,0},{16,24},{24,16},{1,9},{9,1},{17,25},{25,17},{2,10},{10... | collective-permute-start | bytes 294920 | tf_op jit(solution)/shard_map/ppermute | solution.py:51
  878.7 54.6 %collective-permute-start.107 = (bf16[96,2688]{1,0:T(8,128)(2,1)}, bf16[96,2688]{1,0:T(8,128)(2,1)}, u32[]{:S(2)}, u32[]{:S(2)}) collective-permute-start(bf16[96,2688]{1,0:T(8,128)(2,1)} %get-tuple-element.150), channel_id=1, source_target_pairs={{0,8},{8,0},{16,24},{24,16},{1,9},{9,1},{17,25},{25,17},{2,10},{10... | collective-permute-start | bytes 1548296 | tf_op jit(solution)/shard_map/ppermute | solution.py:51
  880.8 29.6 %collective-permute-start.87 = (f32[4,2,192]{1,2,0:T(8,128)S(1)}, f32[4,2,192]{1,2,0:T(8,128)S(1)}, u32[]{:S(2)}, u32[]{:S(2)}) collective-permute-start(f32[4,2,192]{1,2,0:T(8,128)S(1)} %pad_add_fusion.1), channel_id=1, source_target_pairs={{2,0},{4,2},{6,4},{3,1},{5,3},{7,5},{10,8},{12,10},{14,12},{11,9},... | collective-permute-start | bytes 18440 | tf_op jit(solution)/shard_map/ppermute | solution.py:60
  (334 other events, 3920.5 us)
Sparse Core Ops, SparseCore 0:
  23.8 50.7 all-gather.6
  76.2 102.3 all-gather.8
  180.7 59.1 all-gather.10
  241.3 35.8 all-gather.12
  278.6 55.8 all-gather.16
  335.9 112.6 all-gather.14
  476.1 52.5 reduce-scatter.6
  546.1 111.3 reduce-scatter.8
  726.0 36.4 reduce-scatter.10
  764.7 53.1 reduce-scatter.12
  820.2 106.1 reduce-scatter.16
  929.1 48.5 reduce-scatter.14

commit v4 on v3

--- a/solution.py
+++ b/solution.py
@@ -1,10 +1,11 @@
 import jax
 import jax.numpy as jnp
 from jax import lax
+from jax.experimental import pallas as pl
+from jax.experimental.pallas import tpu as pltpu
 from jax.sharding import PartitionSpec as P
 
 HD = 64
-FIRST_AXIS, SECOND_AXIS = "dp", "dp"
 
 epsilon = 1e-05
 rope_base = 1000000.0
@@ -74,15 +75,24 @@
     return mine, swap_core(mine)
 
 
-def scatter_tokens(team, mine, other):
+def scatter_begin(team, mine, other):
     received = swap_core(other.astype(bf16)).astype(f32)
     rows = mine.shape[0] // team.size
     both = mine + received
-    total = both[:rows]
     sends = [(mask, both[mask * rows : (mask + 1) * rows].astype(bf16)) for mask in range(team.size - 1, 0, -1)]
-    for mask, send in sends:
-        total = total + swap(send, team.axis, mask).astype(f32)
-    return total, sends[-1][1]
+    return both[:rows], sends
+
+
+def scatter_end(team, total, sends):
+    received = [swap(send, team.axis, mask) for mask, send in sends]
+    for array in received:
+        total = total + array.astype(f32)
+    return total
+
+
+def scatter_tokens(team, mine, other):
+    total, sends = scatter_begin(team, mine, other)
+    return scatter_end(team, total, sends), sends[-1][1]
 
 
 def true_order(core, sequences, halves):
@@ -262,8 +272,8 @@
     back_normed, sent = project_out(team, "tf,df->td", back_pair, lift)
     drop_part = summed_rows(team, outer(back_tokens, active))
     lift_part = summed_rows(team, outer(tokens, back_pair))
-    if hold:
-        gain = held(gain, drop_part)
+    if hold is not None:
+        gain = held(held(gain, drop_part), hold)
     back_hidden, gain_term = after_norm(back_out, back_normed, normed, inverse, gain)
     return back_hidden, gain_term, drop_part, lift_part
 
@@ -319,6 +329,88 @@
     term = jnp.concatenate([outer(tokens, back_parts), outer(back_tokens, gated)], axis=-1)
     back_hidden, gain_term = after_norm(back_out, back_normed, normed, inverse, gain)
     return back_hidden, gain_term, term, tap_term, back_gated
+
+
+def turned(first, second):
+    return lax.dot_general(first, second, (((1,), (1,)), ((), ())), preferred_element_type=f32)
+
+
+def summed(first, second):
+    return lax.dot_general(first, second, (((0,), (0,)), ((), ())), preferred_element_type=f32)
+
+
+def allowed_keys(base_ref, order_ref, keys, count):
+    base = base_ref[0]
+    slot_row = lax.broadcasted_iota(jnp.int32, (keys, 1), 0)
+    slot = lax.div(slot_row, count)
+    key_index = base + slot_row - 2 * slot * count
+    query_index = base + lax.broadcasted_iota(jnp.int32, (1, count), 1)
+    return (key_index <= query_index) & (key_index >= query_index - order_ref[0])
+
+
+def key_probs(query, keys, allowed):
+    scores = jnp.where(allowed, turned(keys, query) * HD**-0.5, -1e30)
+    weights = jnp.exp(scores - jnp.max(scores, axis=0, keepdims=True))
+    return weights * (1.0 / jnp.sum(weights, axis=0, keepdims=True))
+
+
+def attend_kernel(base_ref, order_ref, query_ref, slots_ref, out_ref):
+    count, keys = query_ref.shape[1], slots_ref.shape[1]
+    allowed = allowed_keys(base_ref, order_ref, keys, count)
+    key, value = slots_ref[0, :, :HD], slots_ref[0, :, HD:]
+    parts = []
+    for head in range(query_ref.shape[2] // HD):
+        query = query_ref[0, :, head * HD : (head + 1) * HD]
+        probs = key_probs(query, key, allowed)
+        parts.append(summed(probs.astype(bf16), value))
+    out_ref[0] = jnp.concatenate(parts, axis=1).astype(bf16)
+
+
+def attend_back_kernel(base_ref, order_ref, query_ref, back_ref, slots_ref, back_query_ref, own_ref, rest_ref):
+    count, keys = query_ref.shape[1], slots_ref.shape[1]
+    allowed = allowed_keys(base_ref, order_ref, keys, count)
+    key, value = slots_ref[0, :, :HD], slots_ref[0, :, HD:]
+    back_queries = []
+    back_key = jnp.zeros((keys, HD), f32)
+    back_value = jnp.zeros((keys, HD), f32)
+    for head in range(query_ref.shape[2] // HD):
+        query = query_ref[0, :, head * HD : (head + 1) * HD]
+        back = back_ref[0, :, head * HD : (head + 1) * HD]
+        probs = key_probs(query, key, allowed)
+        back_probs = turned(value, back)
+        row_dot = jnp.sum(probs * back_probs, axis=0, keepdims=True)
+        back_scores = (probs * (back_probs - row_dot)).astype(bf16)
+        back_queries.append(summed(back_scores, key) * HD**-0.5)
+        back_key += jnp.dot(back_scores, query, preferred_element_type=f32)
+        back_value += jnp.dot(probs.astype(bf16), back, preferred_element_type=f32)
+    back_query_ref[0] = jnp.concatenate(back_queries, axis=1)
+    back_pair = jnp.concatenate([back_key * HD**-0.5, back_value], axis=1)
+    own_ref[0] = back_pair[:count]
+    rest_ref[0] = back_pair[count:].astype(bf16)
+
+
+def attend_call(kernel, base, order, arrays, outs):
+    sequences, count = order.shape
+
+    def block(shape):
+        return pl.BlockSpec((1,) + tuple(shape[1:]), lambda i: (i, 0, 0))
+
+    keys = arrays[-1].shape[1]
+    heads = arrays[0].shape[2] // HD
+    return pl.pallas_call(
+        kernel,
+        grid=(sequences,),
+        in_specs=[pl.BlockSpec(memory_space=pltpu.SMEM), block((sequences, 1, count))]
+        + [block(array.shape) for array in arrays],
+        out_specs=[block(out.shape) for out in outs],
+        out_shape=outs,
+        compiler_params=pltpu.CompilerParams(vmem_limit_bytes=56 * 1024 * 1024),
+        cost_estimate=pl.CostEstimate(
+            flops=10 * sequences * heads * count * keys * HD,
+            bytes_accessed=sum(2 * array.size for array in arrays),
+            transcendentals=sequences * heads * count * keys,
+        ),
+    )(base.reshape(1), order.reshape(sequences, 1, count), *arrays)
 
 
 def attend_forward(team, core, hidden, order, gain, weights, query_gain, key_gain):
@@ -345,23 +437,12 @@
     blocks = lax.axis_size("seq")
     here = lax.axis_index("seq")
     slots = jnp.concatenate([shift(pair, i) if i else pair for i in range(blocks)], axis=1)
-    keys = slots[..., : groups * HD].reshape(sequences, -1, groups, HD)
-    values = slots[..., groups * HD :].reshape(sequences, -1, groups, HD)
-    grouped = query_rot.reshape(sequences, count, groups, repeat, HD)
-    row_index = here * count + jnp.arange(count, dtype=jnp.int32)
-    row_first = row_index[None] - order
-    key_index = jnp.concatenate(
-        [(here - i) * count + jnp.arange(count, dtype=jnp.int32) for i in range(blocks)]
-    )
-    allowed = (key_index[None, None, :] <= row_index[None, :, None]) & (
-        key_index[None, None, :] >= row_first[:, :, None]
-    )
-    scores = dot("vqgrd,vkgd->vgrqk", grouped, keys) * HD**-0.5
-    scores = jnp.where(allowed[:, None, None], scores, -1e30)
-    probs = jnp.exp(scores - jnp.max(scores, axis=-1, keepdims=True))
-    probs = probs / jnp.sum(probs, axis=-1, keepdims=True)
-    attended = dot("vgrqk,vkgd->vqgrd", probs.astype(bf16), values).astype(bf16)
-    attended = own_halves(core, attended.reshape(sequences, count, heads * HD))
+    base = (here * count).astype(jnp.int32)
+    query_rot = query_rot.reshape(sequences, count, heads * HD)
+    (attended,) = attend_call(
+        attend_kernel, base, order, [query_rot, slots], [jax.ShapeDtypeStruct((sequences, count, heads * HD), bf16)]
+    )
+    attended = own_halves(core, attended)
     out, sent = project_out(team, "tc,dc->td", attended, weights[:, inner:])
     stored = (
         inverse,
@@ -373,10 +454,10 @@
         key_normed,
         cosines,
         sines,
-        grouped,
-        keys,
-        values,
-        probs,
+        query_rot,
+        slots,
+        base,
+        order,
         attended,
     )
     return hidden + out, stored, mixed
@@ -393,34 +474,30 @@
         key_normed,
         cosines,
         sines,
-        grouped,
-        keys,
-        values,
-        probs,
+        query_rot,
+        slots,
+        base,
+        order,
         attended,
     ) = stored
-    sequences, count, groups, repeat = grouped.shape[:4]
-    heads = groups * repeat
+    sequences, count = query_rot.shape[:2]
+    heads, groups = query_rot.shape[2] // HD, slots.shape[2] // (2 * HD)
     inner = (heads + 2 * groups) * HD
     back_tokens = gather_tokens(team, back_out.astype(bf16))
     back_attended = true_order(core, team.size, project("td,dc->tc", back_tokens, held(weights[:, inner:], before[0]))).astype(bf16)
-    back_grouped = back_attended.reshape(sequences, count, groups, repeat, HD)
-    back_probs = dot("vqgrd,vkgd->vgrqk", back_grouped, values)
-    row_dot = jnp.sum(probs * back_probs, axis=-1, keepdims=True)
-    back_scores = (probs * (back_probs - row_dot)).astype(bf16)
-    back_query_rot = dot("vgrqk,vkgd->vqgrd", back_scores, keys) * HD**-0.5
-    back_keys = dot("vgrqk,vqgrd->vkgd", back_scores, grouped) * HD**-0.5
-    back_values = dot("vgrqk,vqgrd->vkgd", probs.astype(bf16), back_grouped)
-    back_slots = jnp.concatenate(
+    back_query_rot, back_pair, rest = attend_call(
+        attend_back_kernel,
+        base,
+        order,
+        [query_rot, back_attended, slots],
         [
-            back_keys.reshape(sequences, -1, count, groups * HD),
-            back_values.reshape(sequences, -1, count, groups * HD),
+            jax.ShapeDtypeStruct((sequences, count, heads * HD), f32),
+            jax.ShapeDtypeStruct((sequences, count, 2 * HD), f32),
+            jax.ShapeDtypeStruct((sequences, slots.shape[1] - count, 2 * HD), bf16),
         ],
-        axis=-1,
-    )
-    back_pair = back_slots[:, 0]
-    for i in range(1, back_slots.shape[1]):
-        back_pair = back_pair + shift(back_slots[:, i].astype(bf16), -i).astype(f32)
+    )
+    for i in range(1, slots.shape[1] // count):
+        back_pair = back_pair + shift(rest[:, (i - 1) * count : i * count], -i).astype(f32)
     back_query_scaled = rotate(back_query_rot.reshape(sequences, count, heads, HD), cosines, -sines)
     query_scale_term = jnp.sum(back_query_scaled * query_normed, axis=(0, 1, 2))
     back_query = norm_back(back_query_scaled * query_gain, query_normed, query_inverse)
@@ -475,7 +552,7 @@
 ):
     core = lax.axis_index("mp")
     team = Team("dp")
-    first_team, second_team = Team(FIRST_AXIS), Team(SECOND_AXIS)
+    first_team = second_team = team
     rank = lax.axis_index("dp") * lax.axis_size("seq") + lax.axis_index("seq")
     model = hidden_in.shape[-1]
     share = hidden_in.shape[1] // 2
@@ -533,9 +610,10 @@
         team, core, hidden, token_halves, order, gains[0], mixer_weights, taps
     )
     mixed_done = zero(parts)
-    attend_weights = all_rows(team, got_attend, mixed_done)
+    beside = [jnp.concatenate(pair, axis=1) for pair in zip(got_attend, drop_of(got_second))]
+    shared = all_rows(team, beside, mixed_done)
+    attend_weights, second_drop_all = shared[:, : got_attend[0].shape[1]], shared[:, got_attend[0].shape[1] :]
     second_lift_all = all_rows(second_team, lift_of(got_second), mixed_done)
-    second_drop_all = all_rows(second_team, drop_of(got_second), mixed_done)
 
     first_stored = feed_forward(first_team, after_mixer, gains[1], first_lift_all, first_mask)
     out, sent = project_out(first_team, "tf,df->td", first_stored[-1], first_drop_all)
@@ -547,20 +625,23 @@
     signal_tokens = gather_tokens(second_team, signal_low)
     second_stored = feed_forward(second_team, after_attend, gains[3], second_lift_all, second_mask)
 
+    result_sums, result_sends = scatter_begin(
+        second_team, *project("tf,df->td", second_stored[-1], second_drop_all)
+    )
+    second_mask = held(second_mask, result_sends[-1][1])
+
     back, second_gain_term, *second_part = feed_backward(
-        second_team, signal, signal_tokens, second_stored, gains[3], second_lift_all, second_drop_all, second_mask, False
+        second_team, signal, signal_tokens, second_stored, gains[3], second_lift_all, second_drop_all, second_mask, None
     )
     back, attend_gain_term, attend_term, scale_terms, back_attended = attend_backward(
         team, core, back, attend_stored, gains[2], attend_weights, query_gain, key_gain, second_part
     )
     attend_part = summed_rows(team, attend_term)
-    late = zero(back_attended).astype(bf16)
-    out, sent = project_out(second_team, "tf,df->td", [half + late for half in second_stored[-1]], second_drop_all)
-    result = after_attend + out
+    result = after_attend + scatter_end(second_team, held(result_sums, back_attended), result_sends)
 
     first_back_tokens = gather_tokens(first_team, back.astype(bf16))
     back, first_gain_term, *first_part = feed_backward(
-        first_team, back, first_back_tokens, first_stored, gains[1], first_lift_all, first_drop_all, held(first_mask, attend_part), True
+        first_team, back, first_back_tokens, first_stored, gains[1], first_lift_all, first_drop_all, first_mask, attend_part
     )
     back, mixer_gain_term, mixer_term, tap_term, back_gated = mixer_backward(
         team, core, back, mixer_stored, gains[0], mixer_weights, taps

time: 1050 us -> 1020 us (0.971)
  matrix products: 200 us -> 167 us
  waiting for transfers between devices: 466 us -> 434 us
  Pallas kernels: 0 us -> 31 us
    dot_general x54 -> x48, matrix products: 200 us -> 167 us  [dot(): return jnp.einsum(pattern, first, second, preferred_element_type=f32)]
    pallas_call x0 -> x2, Pallas kernels: none -> 31 us  [attend_call(): pl.pallas_call(kernel, grid=(sequences,), in_specs=[pl.BlockSpec(memory_s...]
    ppermute x8, waiting for transfers between devices: 88.9 us -> 58.1 us  [shift(): lax.ppermute(array, 'seq', [(i, i + by) for i in range(count) if 0 <= i +...]
    unnamed x518 -> x471, local copies, waits for them, and re-layouts: 47.6 us -> 33 us
    reduce_scatter x6, waiting for transfers between devices: 20.8 us -> 33.2 us  [summed_rows(): lax.psum_scatter(split.reshape(-1, columns), team.across, scatter_dimensi...]
    all_gather x6 -> x5, waiting for transfers between devices: 32.8 us -> 24.9 us  [all_rows(): whole = lax.all_gather(near, team.across, axis=len(lead) + 1, tiled=True)]
  transfers between devices with their start and end apart: 122 -> 121, of which waited for: 68 -> 57; matrix products, arithmetic and copies ran while one was open for 36% -> 35% of each run, Pallas kernels for 0% -> 3%
where the time goes in v4:
time: 1020 us; the launch traced here: 1010 us
  waiting for transfers between devices  434 us (43%)
  matrix products  167 us (16%)
  local copies, waits for them, and re-layouts  143 us (14%)
  starting transfers between devices  123 us (12%)
  other arithmetic  88.8 us (9%)
  Pallas kernels  31 us (3%)
  between operations  25.6 us (3%)
    ppermute x102, waiting for transfers between devices, swap(): lax.ppermute(array, axis, [(i, i ^ mask) for i in range(lax.axis_size(axi...  318 us
    dot_general x48, matrix products, dot(): return jnp.einsum(pattern, first, second, preferred_element_type=f32)  167 us
    ppermute x102, starting transfers between devices, swap(): lax.ppermute(array, axis, [(i, i ^ mask) for i in range(lax.axis_size(axi...  106 us
    ppermute x8, waiting for transfers between devices, shift(): lax.ppermute(array, 'seq', [(i, i + by) for i in range(count) if 0 <= i +...  58.1 us
    reduce_scatter x6, waiting for transfers between devices, summed_rows(): lax.psum_scatter(split.reshape(-1, columns), team.across, scatter_dimensi...  33.2 us
    unnamed x471, local copies, waits for them, and re-layouts  33 us
    pallas_call x2, Pallas kernels, attend_call(): pl.pallas_call(kernel, grid=(sequences,), in_specs=[pl.BlockSpec(memory_s...  31 us
    all_gather x5, waiting for transfers between devices, all_rows(): whole = lax.all_gather(near, team.across, axis=len(lead) + 1, tiled=True)  24.9 us
  transfers between devices with their start and end apart: 121, of which 57 were waited for; matrix products, arithmetic and copies ran while one was open for 35% of the time, Pallas kernels for 3%

profile of v4, /device:TPU:0, one launch (start us, length us, event | category | flops | bytes accessed | tf_op | source)
XLA Modules:
  0.0 1012.7 jit_solution(12982825383082865480)
XLA Ops:
  40.1 20.4 %collective-permute-done.23 = bf16[96,2688]{1,0:T(8,128)(2,1)S(1)} collective-permute-done((bf16[96,2688]{1,0:T(8,128)(2,1)S(1)}, bf16[96,2688]{1,0:T(8,128)(2,1)S(1)}, u32[]{:S(2)}, u32[]{:S(2)}) %collective-permute-start.23) | collective-permute-done | bytes 516128 | tf_op jit(solution)/shard_map/ppermute | solution.py:52
  77.4 7.4 collective-permute-done.1
  158.3 7.9 collective-permute-done.19
  185.0 18.3 %collective-permute-done.36 = bf16[96,2688]{1,0:T(8,128)(2,1)} collective-permute-done((bf16[96,2688]{1,0:T(8,128)(2,1)}, bf16[96,2688]{1,0:T(8,128)(2,1)}, u32[]{:S(2)}, u32[]{:S(2)}) %collective-permute-start.36) | collective-permute-done | bytes 516128 | tf_op jit(solution)/shard_map/ppermute | solution.py:52
  251.0 7.4 collective-permute-done.29
  258.3 8.8 collective-permute-done.28
  274.9 8.1 collective-permute-done.32
  296.8 22.2 %all-gather.12.cloned.1.call-done = bf16[4,384,1408]{2,1,0:T(8,128)(2,1)} async-done(((bf16[4,96,1408]{2,1,0:T(8,128)(2,1)}), bf16[4,384,1408]{2,1,0:T(8,128)(2,1)}) %all-gather.12.cloned.1.call-update) | async-done | bytes 4325392 | tf_op jit(solution)/shard_map/all_gather | solution.py:129
  345.5 11.2 %collective-permute-done.41 = bf16[4,256,128]{2,1,0:T(8,128)(2,1)} collective-permute-done((bf16[4,256,128]{2,1,0:T(8,128)(2,1)}, bf16[4,256,128]{2,1,0:T(8,128)(2,1)}, u32[]{:S(2)}, u32[]{:S(2)}) %collective-permute-start.41) | collective-permute-done | bytes 262176 | tf_op jit(solution)/shard_map/ppermute | solution.py:61
  356.8 10.9 %collective-permute-done.40 = bf16[4,256,128]{2,1,0:T(8,128)(2,1)} collective-permute-done((bf16[4,256,128]{2,1,0:T(8,128)(2,1)}, bf16[4,256,128]{2,1,0:T(8,128)(2,1)}, u32[]{:S(2)}, u32[]{:S(2)}) %collective-permute-start.40) | collective-permute-done | bytes 262176 | tf_op jit(solution)/shard_map/ppermute | solution.py:61
  370.2 12.1 %shard_map.322 = bf16[4,256,192]{2,1,0:T(8,128)(2,1)} custom-call(s32[1]{0:T(128)} %bitcast.50.base_ref, s32[4,1,256]{2,1,0:T(1,128)} %reshape.721.order_ref, bf16[4,256,192]{2,1,0:T(8,128)(2,1)} %copy.190.query_ref, bf16[4,1024,128]{2,1,0:T(8,128)(2,1)} %pad_maximum_fusion.34.slots_ref), custom_call_target="tpu_custom_call" | custom-call | flops 2013265920 | bytes 1441792 | tf_op jit(solution)/shard_map/pallas_call | solution.py:400
  394.7 8.5 collective-permute-done.46
  403.1 9.1 collective-permute-done.45
  417.5 8.3 collective-permute-done.49
  437.4 9.4 collective-permute-done.54
  446.8 8.0 collective-permute-done.53
  498.1 9.0 fusion.29
  534.8 8.5 collective-permute-done.59
  543.3 8.8 collective-permute-done.58
  557.8 9.5 collective-permute-done.62
  588.3 18.9 %shard_map.323 = (f32[4,256,192]{2,1,0:T(8,128)}, f32[4,256,128]{2,1,0:T(8,128)}, bf16[4,768,128]{2,1,0:T(8,128)(2,1)}) custom-call(s32[1]{0:T(128)} %bitcast.50.base_ref, s32[4,1,256]{2,1,0:T(1,128)} %reshape.721.order_ref, bf16[4,256,192]{2,1,0:T(8,128)(2,1)} %copy.190.query_ref, bf16[4,256,192]{2,1,0:T(8,128)(2,1)} %fusion.34.back_ref, ...), custom_call_target="tpu_custom_call" | custom-call | flops 2013265920 | bytes 1835008 | tf_op jit(solution)/shard_map/pallas_call | solution.py:400
  627.8 30.6 %collective-permute-done.69 = bf16[4,256,128]{2,1,0:T(8,128)(2,1)} collective-permute-done((bf16[4,256,128]{2,1,0:T(8,128)(2,1)}, bf16[4,256,128]{2,1,0:T(8,128)(2,1)}, u32[]{:S(2)}, u32[]{:S(2)}) %collective-permute-start.69) | collective-permute-done | bytes 262176 | tf_op jit(solution)/shard_map/ppermute | solution.py:61
  695.3 15.3 %collective-permute-done.73 = bf16[128,1536]{1,0:T(8,128)(2,1)S(1)} collective-permute-done((bf16[128,1536]{1,0:T(8,128)(2,1)S(1)}, bf16[128,1536]{1,0:T(8,128)(2,1)S(1)}, u32[]{:S(2)}, u32[]{:S(2)}) %collective-permute-start.73) | collective-permute-done | bytes 393248 | tf_op jit(solution)/shard_map/ppermute | solution.py:52
  756.8 7.6 fusion.27
  764.4 7.7 add_convert_fusion
  775.5 8.0 fusion.206
  789.0 29.3 %reduce-scatter.11.cloned.1.call-done = bf16[384,896]{1,0:T(8,128)(2,1)} async-done(((bf16[1536,896]{1,0:T(8,128)(2,1)}), bf16[384,896]{1,0:T(8,128)(2,1)}) %reduce-scatter.11.cloned.1.call-update) | async-done | bytes 688144 | tf_op jit(solution)/shard_map/reduce_scatter | solution.py:144
  827.8 9.5 collective-permute-done.85
  897.4 8.0 collective-permute-done.107
  917.0 8.5 collective-permute-done.91
  967.9 9.3 collective-permute-done.103
  977.2 9.6 collective-permute-done.102
  (1013 shorter events, 611.3 us)
Async XLA Ops:
  7.2 110.6 %all-gather.6.cloned.1.call-start = ((), (), s32[]{:S(2)}) async-start(), calls=%async_computation.6 | async-start | bytes 2949120 | tf_op jit(solution)/shard_map/all_gather | solution.py:129
  22.5 195.4 %all-gather.8.cloned.1.call-start = ((), (), s32[]{:S(2)}) async-start(), calls=%async_computation.7 | async-start | bytes 6881280 | tf_op jit(solution)/shard_map/all_gather | solution.py:129
  63.5 171.8 %all-gather.10.cloned.1.call-start = ((), (), s32[]{:S(2)}) async-start(), calls=%async_computation.8 | async-start | bytes 3440640 | tf_op jit(solution)/shard_map/all_gather | solution.py:129
  85.7 31.6 %collective-permute-start.11 = (bf16[512,1536]{1,0:T(8,128)(2,1)S(1)}, bf16[512,1536]{1,0:T(8,128)(2,1)S(1)}, u32[]{:S(2)}, u32[]{:S(2)}) collective-permute-start(bf16[512,1536]{1,0:T(8,128)(2,1)S(1)} %get-tuple-element.156), channel_id=1, source_target_pairs={{0,1},{1,0},{2,3},{3,2},{4,5},{5,4},{6,7},{7,6},{8,9},{9,8},{10,11... | collective-permute-start | bytes 4718600 | tf_op jit(solution)/shard_map/ppermute | solution.py:52
  143.0 37.0 %collective-permute-start.34 = (bf16[96,2688]{1,0:T(8,128)(2,1)}, bf16[96,2688]{1,0:T(8,128)(2,1)}, u32[]{:S(2)}, u32[]{:S(2)}) collective-permute-start(bf16[96,2688]{1,0:T(8,128)(2,1)} %pad_maximum_fusion.43), channel_id=1, source_target_pairs={{0,8},{8,0},{16,24},{24,16},{1,9},{9,1},{17,25},{25,17},{2,10},{10... | collective-permute-start | bytes 1548296 | tf_op jit(solution)/shard_map/ppermute | solution.py:52
  148.9 170.2 %all-gather.12.cloned.1.call-start = ((), (), s32[]{:S(2)}) async-start(), calls=%async_computation.9 | async-start | bytes 5406720 | tf_op jit(solution)/shard_map/all_gather | solution.py:129
  156.0 47.3 %collective-permute-start.36 = (bf16[96,2688]{1,0:T(8,128)(2,1)}, bf16[96,2688]{1,0:T(8,128)(2,1)}, u32[]{:S(2)}, u32[]{:S(2)}) collective-permute-start(bf16[96,2688]{1,0:T(8,128)(2,1)} %pad_maximum_fusion.44), channel_id=1, source_target_pairs={{0,16},{8,24},{16,0},{24,8},{1,17},{9,25},{17,1},{25,9},{2,18},{10... | collective-permute-start | bytes 1548296 | tf_op jit(solution)/shard_map/ppermute | solution.py:52
  166.2 40.1 %collective-permute-start.38 = (bf16[96,2688]{1,0:T(8,128)(2,1)}, bf16[96,2688]{1,0:T(8,128)(2,1)}, u32[]{:S(2)}, u32[]{:S(2)}) collective-permute-start(bf16[96,2688]{1,0:T(8,128)(2,1)} %pad_maximum_fusion.45), channel_id=1, source_target_pairs={{0,24},{8,16},{16,8},{24,0},{1,25},{9,17},{17,9},{25,1},{2,26},{10... | collective-permute-start | bytes 1548296 | tf_op jit(solution)/shard_map/ppermute | solution.py:52
  177.1 33.5 %collective-permute-start.22 = (bf16[128,1536]{1,0:T(8,128)(2,1)}, bf16[128,1536]{1,0:T(8,128)(2,1)}, u32[]{:S(2)}, u32[]{:S(2)}) collective-permute-start(bf16[128,1536]{1,0:T(8,128)(2,1)} %multiply_convert_fusion.20), channel_id=1, source_target_pairs={{0,24},{8,16},{16,8},{24,0},{1,25},{9,17},{17,9},{25,1},{2,26},{10... | collective-permute-start | bytes 1179656 | tf_op jit(solution)/shard_map/ppermute | solution.py:52
  178.6 33.2 %collective-permute-start.21 = (bf16[128,1536]{1,0:T(8,128)(2,1)}, bf16[128,1536]{1,0:T(8,128)(2,1)}, u32[]{:S(2)}, u32[]{:S(2)}) collective-permute-start(bf16[128,1536]{1,0:T(8,128)(2,1)} %multiply_convert_fusion.20), channel_id=1, source_target_pairs={{0,16},{8,24},{16,0},{24,8},{1,17},{9,25},{17,1},{25,9},{2,18},{10... | collective-permute-start | bytes 1179656 | tf_op jit(solution)/shard_map/ppermute | solution.py:52
  180.0 31.7 %collective-permute-start.20 = (bf16[128,1536]{1,0:T(8,128)(2,1)}, bf16[128,1536]{1,0:T(8,128)(2,1)}, u32[]{:S(2)}, u32[]{:S(2)}) collective-permute-start(bf16[128,1536]{1,0:T(8,128)(2,1)} %multiply_convert_fusion.20), channel_id=1, source_target_pairs={{0,8},{8,0},{16,24},{24,16},{1,9},{9,1},{17,25},{25,17},{2,10},{10... | collective-permute-start | bytes 1179656 | tf_op jit(solution)/shard_map/ppermute | solution.py:52
  217.5 238.8 %all-gather.14.cloned.1.call-start = ((), (), s32[]{:S(2)}) async-start(), calls=%async_computation.10 | async-start | bytes 6881280 | tf_op jit(solution)/shard_map/all_gather | solution.py:129
  292.3 29.4 %collective-permute-start.39 = (bf16[512,1536]{1,0:T(8,128)(2,1)}, bf16[512,1536]{1,0:T(8,128)(2,1)S(1)}, u32[]{:S(2)}, u32[]{:S(2)}) collective-permute-start(bf16[512,1536]{1,0:T(8,128)(2,1)} %pad_maximum_fusion.11), channel_id=1, source_target_pairs={{0,1},{1,0},{2,3},{3,2},{4,5},{5,4},{6,7},{7,6},{8,9},{9,8},{10,11... | collective-permute-start | bytes 4718600 | tf_op jit(solution)/shard_map/ppermute | solution.py:52
  296.6 283.9 %reduce-scatter.7.cloned.1.call-start = ((), (), s32[]{:S(2)}) async-start(), calls=%async_computation.11 | async-start | bytes 3440640 | tf_op jit(solution)/shard_map/reduce_scatter | solution.py:144
  335.7 32.0 %collective-permute-start.40 = (bf16[4,256,128]{2,1,0:T(8,128)(2,1)}, bf16[4,256,128]{2,1,0:T(8,128)(2,1)}, u32[]{:S(2)}, u32[]{:S(2)}) collective-permute-start(bf16[4,256,128]{2,1,0:T(8,128)(2,1)} %pad_maximum_fusion.52), channel_id=1, source_target_pairs={{0,2},{2,4},{4,6},{1,3},{3,5},{5,7},{8,10},{10,12},{12,14},{9,11},... | collective-permute-start | bytes 786440 | tf_op jit(solution)/shard_map/ppermute | solution.py:61
  433.7 28.8 %collective-permute-start.50 = (bf16[512,1536]{1,0:T(8,128)(2,1)}, bf16[512,1536]{1,0:T(8,128)(2,1)}, u32[]{:S(2)}, u32[]{:S(2)}) collective-permute-start(bf16[512,1536]{1,0:T(8,128)(2,1)} %pad_maximum_fusion.12), channel_id=1, source_target_pairs={{0,1},{1,0},{2,3},{3,2},{4,5},{5,4},{6,7},{7,6},{8,9},{9,8},{10,11... | collective-permute-start | bytes 4718600 | tf_op jit(solution)/shard_map/ppermute | solution.py:52
  478.2 189.9 %reduce-scatter.9.cloned.1.call-start = ((), (), s32[]{:S(2)}) async-start(), calls=%async_computation.12 | async-start | bytes 6881280 | tf_op jit(solution)/shard_map/reduce_scatter | solution.py:144
  516.0 271.2 %reduce-scatter.13.cloned.1.call-start = ((), (), s32[]{:S(2)}) async-start(), calls=%async_computation.14 | async-start | bytes 1966080 | tf_op jit(solution)/shard_map/reduce_scatter | solution.py:144
  610.5 48.0 %collective-permute-start.69 = (bf16[4,256,128]{2,1,0:T(8,128)(2,1)}, bf16[4,256,128]{2,1,0:T(8,128)(2,1)}, u32[]{:S(2)}, u32[]{:S(2)}) collective-permute-start(bf16[4,256,128]{2,1,0:T(8,128)(2,1)} %get-tuple-element.281), channel_id=1, source_target_pairs={{4,0},{6,2},{5,1},{7,3},{12,8},{14,10},{13,9},{15,11},{20,16},{22,... | collective-permute-start | bytes 786440 | tf_op jit(solution)/shard_map/ppermute | solution.py:61
  611.8 46.7 %collective-permute-start.68 = (bf16[4,256,128]{2,1,0:T(8,128)(2,1)}, bf16[4,256,128]{2,1,0:T(8,128)(2,1)}, u32[]{:S(2)}, u32[]{:S(2)}) collective-permute-start(bf16[4,256,128]{2,1,0:T(8,128)(2,1)} %get-tuple-element.279), channel_id=1, source_target_pairs={{2,0},{4,2},{6,4},{3,1},{5,3},{7,5},{10,8},{12,10},{14,12},{11,9},... | collective-permute-start | bytes 786440 | tf_op jit(solution)/shard_map/ppermute | solution.py:61
  672.5 39.0 %collective-permute-start.66 = (bf16[128,1536]{1,0:T(8,128)(2,1)S(1)}, bf16[128,1536]{1,0:T(8,128)(2,1)S(1)}, u32[]{:S(2)}, u32[]{:S(2)}) collective-permute-start(bf16[128,1536]{1,0:T(8,128)(2,1)S(1)} %get-tuple-element.222), channel_id=1, source_target_pairs={{0,8},{8,0},{16,24},{24,16},{1,9},{9,1},{17,25},{25,17},{2,10},{10... | collective-permute-start | bytes 1179656 | tf_op jit(solution)/shard_map/ppermute | solution.py:52
  674.0 37.5 %collective-permute-start.65 = (bf16[128,1536]{1,0:T(8,128)(2,1)S(1)}, bf16[128,1536]{1,0:T(8,128)(2,1)S(1)}, u32[]{:S(2)}, u32[]{:S(2)}) collective-permute-start(bf16[128,1536]{1,0:T(8,128)(2,1)S(1)} %get-tuple-element.223), channel_id=1, source_target_pairs={{0,16},{8,24},{16,0},{24,8},{1,17},{9,25},{17,1},{25,9},{2,18},{10... | collective-permute-start | bytes 1179656 | tf_op jit(solution)/shard_map/ppermute | solution.py:52
  682.9 27.6 %collective-permute-start.73 = (bf16[128,1536]{1,0:T(8,128)(2,1)S(1)}, bf16[128,1536]{1,0:T(8,128)(2,1)S(1)}, u32[]{:S(2)}, u32[]{:S(2)}) collective-permute-start(bf16[128,1536]{1,0:T(8,128)(2,1)S(1)} %get-tuple-element.217), channel_id=1, source_target_pairs={{0,16},{8,24},{16,0},{24,8},{1,17},{9,25},{17,1},{25,9},{2,18},{10... | collective-permute-start | bytes 1179656 | tf_op jit(solution)/shard_map/ppermute | solution.py:52
  683.5 27.1 %collective-permute-start.72 = (bf16[128,1536]{1,0:T(8,128)(2,1)S(1)}, bf16[128,1536]{1,0:T(8,128)(2,1)S(1)}, u32[]{:S(2)}, u32[]{:S(2)}) collective-permute-start(bf16[128,1536]{1,0:T(8,128)(2,1)S(1)} %get-tuple-element.215), channel_id=1, source_target_pairs={{0,24},{8,16},{16,8},{24,0},{1,25},{9,17},{17,9},{25,1},{2,26},{10... | collective-permute-start | bytes 1179656 | tf_op jit(solution)/shard_map/ppermute | solution.py:52
  719.9 98.3 %reduce-scatter.11.cloned.1.call-start = ((), (), s32[]{:S(2)}) async-start(), calls=%async_computation.13 | async-start | bytes 3440640 | tf_op jit(solution)/shard_map/reduce_scatter | solution.py:144
  744.6 214.4 %reduce-scatter.17.cloned.1.call-start = ((), (), s32[]{:S(2)}) async-start(), calls=%async_computation.16 | async-start | bytes 6881280 | tf_op jit(solution)/shard_map/reduce_scatter | solution.py:144
  775.0 216.9 %reduce-scatter.15.cloned.1.call-start = ((), (), s32[]{:S(2)}) async-start(), calls=%async_computation.15 | async-start | bytes 2949120 | tf_op jit(solution)/shard_map/reduce_scatter | solution.py:144
  783.6 37.3 %collective-permute-start.82 = (bf16[128,1536]{1,0:T(8,128)(2,1)S(1)}, bf16[128,1536]{1,0:T(8,128)(2,1)S(1)}, u32[]{:S(2)}, u32[]{:S(2)}) collective-permute-start(bf16[128,1536]{1,0:T(8,128)(2,1)S(1)} %get-tuple-element.213), channel_id=1, source_target_pairs={{0,8},{8,0},{16,24},{24,16},{1,9},{9,1},{17,25},{25,17},{2,10},{10... | collective-permute-start | bytes 1179656 | tf_op jit(solution)/shard_map/ppermute | solution.py:52
  785.1 35.8 %collective-permute-start.81 = (bf16[128,1536]{1,0:T(8,128)(2,1)S(1)}, bf16[128,1536]{1,0:T(8,128)(2,1)S(1)}, u32[]{:S(2)}, u32[]{:S(2)}) collective-permute-start(bf16[128,1536]{1,0:T(8,128)(2,1)S(1)} %get-tuple-element.214), channel_id=1, source_target_pairs={{0,16},{8,24},{16,0},{24,8},{1,17},{9,25},{17,1},{25,9},{2,18},{10... | collective-permute-start | bytes 1179656 | tf_op jit(solution)/shard_map/ppermute | solution.py:52
  786.1 34.8 %collective-permute-start.80 = (bf16[128,1536]{1,0:T(8,128)(2,1)S(1)}, bf16[128,1536]{1,0:T(8,128)(2,1)}, u32[]{:S(2)}, u32[]{:S(2)}) collective-permute-start(bf16[128,1536]{1,0:T(8,128)(2,1)S(1)} %get-tuple-element.212), channel_id=1, source_target_pairs={{0,24},{8,16},{16,8},{24,0},{1,25},{9,17},{17,9},{25,1},{2,26},{10... | collective-permute-start | bytes 1179656 | tf_op jit(solution)/shard_map/ppermute | solution.py:52
  864.9 27.2 %collective-permute-start.106 = (bf16[96,512]{1,0:T(8,128)(2,1)}, bf16[96,512]{1,0:T(8,128)(2,1)}, u32[]{:S(2)}, u32[]{:S(2)}) collective-permute-start(bf16[96,512]{1,0:T(8,128)(2,1)} %get-tuple-element.309), channel_id=1, source_target_pairs={{0,24},{8,16},{16,8},{24,0},{1,25},{9,17},{17,9},{25,1},{2,26},{10... | collective-permute-start | bytes 294920 | tf_op jit(solution)/shard_map/ppermute | solution.py:52
  866.6 26.5 %collective-permute-start.105 = (bf16[96,512]{1,0:T(8,128)(2,1)}, bf16[96,512]{1,0:T(8,128)(2,1)}, u32[]{:S(2)}, u32[]{:S(2)}) collective-permute-start(bf16[96,512]{1,0:T(8,128)(2,1)} %get-tuple-element.310), channel_id=1, source_target_pairs={{0,16},{8,24},{16,0},{24,8},{1,17},{9,25},{17,1},{25,9},{2,18},{10... | collective-permute-start | bytes 294920 | tf_op jit(solution)/shard_map/ppermute | solution.py:52
  (312 other events, 3870.5 us)
Sparse Core Ops, SparseCore 0:
  22.6 50.7 all-gather.5
  75.6 102.2 all-gather.7
  180.0 55.2 all-gather.9
  237.3 81.6 all-gather.11
  320.5 113.5 all-gather.13
  478.3 72.7 reduce-scatter.6
  553.4 114.5 reduce-scatter.8
  720.0 42.6 reduce-scatter.12
  765.1 53.1 reduce-scatter.10
  820.4 97.9 reduce-scatter.16
  921.3 49.9 reduce-scatter.14

commit v5 on v4

--- a/solution.py
+++ b/solution.py
@@ -271,6 +271,8 @@
     back_pair = [feed_back(back_tokens[i], gate[i], up[i], drop, mask) for i in range(2)]
     back_normed, sent = project_out(team, "tf,df->td", back_pair, lift)
     drop_part = summed_rows(team, outer(back_tokens, active))
+    if hold is None:
+        back_pair = [held(half, sent) for half in back_pair]
     lift_part = summed_rows(team, outer(tokens, back_pair))
     if hold is not None:
         gain = held(held(gain, drop_part), hold)

time: 1020 us -> 1030 us (level)
    unnamed x471 -> x463, local copies, waits for them, and re-layouts: 33 us -> 33 us
  transfers between devices with their start and end apart: 121 -> 121, of which waited for: 57 -> 56; matrix products, arithmetic and copies ran while one was open for 35% -> 36% of each run, Pallas kernels for 3% -> 3%
where the time goes in v5:
time: 1030 us; the launch traced here: 1020 us
  waiting for transfers between devices  439 us (43%)
  matrix products  164 us (16%)
  local copies, waits for them, and re-layouts  145 us (14%)
  starting transfers between devices  122 us (12%)
  other arithmetic  89.9 us (9%)
  Pallas kernels  31 us (3%)
  between operations  26.2 us (3%)
    ppermute x102, waiting for transfers between devices, swap(): lax.ppermute(array, axis, [(i, i ^ mask) for i in range(lax.axis_size(axi...  318 us
    dot_general x48, matrix products, dot(): return jnp.einsum(pattern, first, second, preferred_element_type=f32)  164 us
    ppermute x102, starting transfers between devices, swap(): lax.ppermute(array, axis, [(i, i ^ mask) for i in range(lax.axis_size(axi...  106 us
    ppermute x8, waiting for transfers between devices, shift(): lax.ppermute(array, 'seq', [(i, i + by) for i in range(count) if 0 <= i +...  54.2 us
    reduce_scatter x6, waiting for transfers between devices, summed_rows(): lax.psum_scatter(split.reshape(-1, columns), team.across, scatter_dimensi...  40.8 us
    unnamed x463, local copies, waits for them, and re-layouts  33 us
    pallas_call x2, Pallas kernels, attend_call(): pl.pallas_call(kernel, grid=(sequences,), in_specs=[pl.BlockSpec(memory_s...  31 us
    all_gather x5, waiting for transfers between devices, all_rows(): whole = lax.all_gather(near, team.across, axis=len(lead) + 1, tiled=True)  24.9 us
  transfers between devices with their start and end apart: 121, of which 56 were waited for; matrix products, arithmetic and copies ran while one was open for 36% of the time, Pallas kernels for 3%

profile of v5, /device:TPU:0, one launch (start us, length us, event | category | flops | bytes accessed | tf_op | source)
XLA Modules:
  0.0 1016.7 jit_solution(16910497561180776739)
XLA Ops:
  40.1 20.4 %collective-permute-done.23 = bf16[96,2688]{1,0:T(8,128)(2,1)S(1)} collective-permute-done((bf16[96,2688]{1,0:T(8,128)(2,1)S(1)}, bf16[96,2688]{1,0:T(8,128)(2,1)S(1)}, u32[]{:S(2)}, u32[]{:S(2)}) %collective-permute-start.23) | collective-permute-done | bytes 516128 | tf_op jit(solution)/shard_map/ppermute | solution.py:52
  77.3 7.4 collective-permute-done.1
  158.3 7.9 collective-permute-done.19
  184.9 18.3 %collective-permute-done.36 = bf16[96,2688]{1,0:T(8,128)(2,1)} collective-permute-done((bf16[96,2688]{1,0:T(8,128)(2,1)}, bf16[96,2688]{1,0:T(8,128)(2,1)}, u32[]{:S(2)}, u32[]{:S(2)}) %collective-permute-start.36) | collective-permute-done | bytes 516128 | tf_op jit(solution)/shard_map/ppermute | solution.py:52
  258.4 8.8 collective-permute-done.28
  275.0 8.1 collective-permute-done.32
  296.8 22.2 %all-gather.12.cloned.1.call-done = bf16[4,384,1408]{2,1,0:T(8,128)(2,1)} async-done(((bf16[4,96,1408]{2,1,0:T(8,128)(2,1)}), bf16[4,384,1408]{2,1,0:T(8,128)(2,1)}) %all-gather.12.cloned.1.call-update) | async-done | bytes 4325392 | tf_op jit(solution)/shard_map/all_gather | solution.py:129
  345.6 11.2 %collective-permute-done.41 = bf16[4,256,128]{2,1,0:T(8,128)(2,1)} collective-permute-done((bf16[4,256,128]{2,1,0:T(8,128)(2,1)}, bf16[4,256,128]{2,1,0:T(8,128)(2,1)}, u32[]{:S(2)}, u32[]{:S(2)}) %collective-permute-start.41) | collective-permute-done | bytes 262176 | tf_op jit(solution)/shard_map/ppermute | solution.py:61
  356.8 10.9 %collective-permute-done.40 = bf16[4,256,128]{2,1,0:T(8,128)(2,1)} collective-permute-done((bf16[4,256,128]{2,1,0:T(8,128)(2,1)}, bf16[4,256,128]{2,1,0:T(8,128)(2,1)}, u32[]{:S(2)}, u32[]{:S(2)}) %collective-permute-start.40) | collective-permute-done | bytes 262176 | tf_op jit(solution)/shard_map/ppermute | solution.py:61
  370.2 12.1 %shard_map.322 = bf16[4,256,192]{2,1,0:T(8,128)(2,1)} custom-call(s32[1]{0:T(128)} %bitcast.50.base_ref, s32[4,1,256]{2,1,0:T(1,128)} %reshape.726.order_ref, bf16[4,256,192]{2,1,0:T(8,128)(2,1)} %copy.190.query_ref, bf16[4,1024,128]{2,1,0:T(8,128)(2,1)} %pad_maximum_fusion.34.slots_ref), custom_call_target="tpu_custom_call" | custom-call | flops 2013265920 | bytes 1441792 | tf_op jit(solution)/shard_map/pallas_call | solution.py:402
  394.7 8.5 collective-permute-done.46
  403.1 9.1 collective-permute-done.45
  417.5 8.3 collective-permute-done.49
  437.4 9.4 collective-permute-done.54
  446.8 8.0 collective-permute-done.53
  511.3 8.0 fusion.9
  533.1 8.5 collective-permute-done.59
  541.6 8.8 collective-permute-done.58
  557.3 9.5 collective-permute-done.62
  588.0 18.9 %shard_map.323 = (f32[4,256,192]{2,1,0:T(8,128)}, f32[4,256,128]{2,1,0:T(8,128)}, bf16[4,768,128]{2,1,0:T(8,128)(2,1)}) custom-call(s32[1]{0:T(128)} %bitcast.50.base_ref, s32[4,1,256]{2,1,0:T(1,128)} %reshape.726.order_ref, bf16[4,256,192]{2,1,0:T(8,128)(2,1)} %copy.190.query_ref, bf16[4,256,192]{2,1,0:T(8,128)(2,1)} %fusion.36.back_ref, ...), custom_call_target="tpu_custom_call" | custom-call | flops 2013265920 | bytes 1835008 | tf_op jit(solution)/shard_map/pallas_call | solution.py:402
  627.5 26.7 %collective-permute-done.69 = bf16[4,256,128]{2,1,0:T(8,128)(2,1)} collective-permute-done((bf16[4,256,128]{2,1,0:T(8,128)(2,1)}, bf16[4,256,128]{2,1,0:T(8,128)(2,1)}, u32[]{:S(2)}, u32[]{:S(2)}) %collective-permute-start.69) | collective-permute-done | bytes 262176 | tf_op jit(solution)/shard_map/ppermute | solution.py:61
  659.9 15.5 %reduce-scatter.9.cloned.1.call-done = bf16[384,1792]{1,0:T(8,128)(2,1)} async-done(((bf16[1536,1792]{1,0:T(8,128)(2,1)}), bf16[384,1792]{1,0:T(8,128)(2,1)}) %reduce-scatter.9.cloned.1.call-update) | async-done | bytes 1376272 | tf_op jit(solution)/shard_map/reduce_scatter | solution.py:144
  702.7 15.2 %collective-permute-done.73 = bf16[128,1536]{1,0:T(8,128)(2,1)S(1)} collective-permute-done((bf16[128,1536]{1,0:T(8,128)(2,1)S(1)}, bf16[128,1536]{1,0:T(8,128)(2,1)S(1)}, u32[]{:S(2)}, u32[]{:S(2)}) %collective-permute-start.73) | collective-permute-done | bytes 393248 | tf_op jit(solution)/shard_map/ppermute | solution.py:52
  764.0 7.7 fusion.30
  771.6 8.2 add_convert_fusion
  783.2 8.0 fusion.210
  796.7 25.3 %reduce-scatter.11.cloned.1.call-done = bf16[384,896]{1,0:T(8,128)(2,1)} async-done(((bf16[1536,896]{1,0:T(8,128)(2,1)}), bf16[384,896]{1,0:T(8,128)(2,1)}) %reduce-scatter.11.cloned.1.call-update) | async-done | bytes 688144 | tf_op jit(solution)/shard_map/reduce_scatter | solution.py:144
  831.5 9.5 collective-permute-done.85
  901.2 7.9 collective-permute-done.107
  920.8 8.5 collective-permute-done.91
  971.6 9.4 collective-permute-done.103
  981.0 9.8 collective-permute-done.102
  (1007 shorter events, 614.6 us)
Async XLA Ops:
  7.2 110.6 %all-gather.6.cloned.1.call-start = ((), (), s32[]{:S(2)}) async-start(), calls=%async_computation.6 | async-start | bytes 2949120 | tf_op jit(solution)/shard_map/all_gather | solution.py:129
  22.5 195.4 %all-gather.8.cloned.1.call-start = ((), (), s32[]{:S(2)}) async-start(), calls=%async_computation.7 | async-start | bytes 6881280 | tf_op jit(solution)/shard_map/all_gather | solution.py:129
  63.5 171.9 %all-gather.10.cloned.1.call-start = ((), (), s32[]{:S(2)}) async-start(), calls=%async_computation.8 | async-start | bytes 3440640 | tf_op jit(solution)/shard_map/all_gather | solution.py:129
  85.7 31.6 %collective-permute-start.11 = (bf16[512,1536]{1,0:T(8,128)(2,1)S(1)}, bf16[512,1536]{1,0:T(8,128)(2,1)S(1)}, u32[]{:S(2)}, u32[]{:S(2)}) collective-permute-start(bf16[512,1536]{1,0:T(8,128)(2,1)S(1)} %get-tuple-element.156), channel_id=1, source_target_pairs={{0,1},{1,0},{2,3},{3,2},{4,5},{5,4},{6,7},{7,6},{8,9},{9,8},{10,11... | collective-permute-start | bytes 4718600 | tf_op jit(solution)/shard_map/ppermute | solution.py:52
  143.0 37.0 %collective-permute-start.34 = (bf16[96,2688]{1,0:T(8,128)(2,1)}, bf16[96,2688]{1,0:T(8,128)(2,1)}, u32[]{:S(2)}, u32[]{:S(2)}) collective-permute-start(bf16[96,2688]{1,0:T(8,128)(2,1)} %pad_maximum_fusion.43), channel_id=1, source_target_pairs={{0,8},{8,0},{16,24},{24,16},{1,9},{9,1},{17,25},{25,17},{2,10},{10... | collective-permute-start | bytes 1548296 | tf_op jit(solution)/shard_map/ppermute | solution.py:52
  148.9 170.2 %all-gather.12.cloned.1.call-start = ((), (), s32[]{:S(2)}) async-start(), calls=%async_computation.9 | async-start | bytes 5406720 | tf_op jit(solution)/shard_map/all_gather | solution.py:129
  155.9 47.3 %collective-permute-start.36 = (bf16[96,2688]{1,0:T(8,128)(2,1)}, bf16[96,2688]{1,0:T(8,128)(2,1)}, u32[]{:S(2)}, u32[]{:S(2)}) collective-permute-start(bf16[96,2688]{1,0:T(8,128)(2,1)} %pad_maximum_fusion.44), channel_id=1, source_target_pairs={{0,16},{8,24},{16,0},{24,8},{1,17},{9,25},{17,1},{25,9},{2,18},{10... | collective-permute-start | bytes 1548296 | tf_op jit(solution)/shard_map/ppermute | solution.py:52
  166.2 40.2 %collective-permute-start.38 = (bf16[96,2688]{1,0:T(8,128)(2,1)}, bf16[96,2688]{1,0:T(8,128)(2,1)}, u32[]{:S(2)}, u32[]{:S(2)}) collective-permute-start(bf16[96,2688]{1,0:T(8,128)(2,1)} %pad_maximum_fusion.45), channel_id=1, source_target_pairs={{0,24},{8,16},{16,8},{24,0},{1,25},{9,17},{17,9},{25,1},{2,26},{10... | collective-permute-start | bytes 1548296 | tf_op jit(solution)/shard_map/ppermute | solution.py:52
  177.1 33.5 %collective-permute-start.22 = (bf16[128,1536]{1,0:T(8,128)(2,1)}, bf16[128,1536]{1,0:T(8,128)(2,1)}, u32[]{:S(2)}, u32[]{:S(2)}) collective-permute-start(bf16[128,1536]{1,0:T(8,128)(2,1)} %multiply_convert_fusion.20), channel_id=1, source_target_pairs={{0,24},{8,16},{16,8},{24,0},{1,25},{9,17},{17,9},{25,1},{2,26},{10... | collective-permute-start | bytes 1179656 | tf_op jit(solution)/shard_map/ppermute | solution.py:52
  178.5 33.2 %collective-permute-start.21 = (bf16[128,1536]{1,0:T(8,128)(2,1)}, bf16[128,1536]{1,0:T(8,128)(2,1)}, u32[]{:S(2)}, u32[]{:S(2)}) collective-permute-start(bf16[128,1536]{1,0:T(8,128)(2,1)} %multiply_convert_fusion.20), channel_id=1, source_target_pairs={{0,16},{8,24},{16,0},{24,8},{1,17},{9,25},{17,1},{25,9},{2,18},{10... | collective-permute-start | bytes 1179656 | tf_op jit(solution)/shard_map/ppermute | solution.py:52
  180.0 31.7 %collective-permute-start.20 = (bf16[128,1536]{1,0:T(8,128)(2,1)}, bf16[128,1536]{1,0:T(8,128)(2,1)}, u32[]{:S(2)}, u32[]{:S(2)}) collective-permute-start(bf16[128,1536]{1,0:T(8,128)(2,1)} %multiply_convert_fusion.20), channel_id=1, source_target_pairs={{0,8},{8,0},{16,24},{24,16},{1,9},{9,1},{17,25},{25,17},{2,10},{10... | collective-permute-start | bytes 1179656 | tf_op jit(solution)/shard_map/ppermute | solution.py:52
  217.4 238.8 %all-gather.14.cloned.1.call-start = ((), (), s32[]{:S(2)}) async-start(), calls=%async_computation.10 | async-start | bytes 6881280 | tf_op jit(solution)/shard_map/all_gather | solution.py:129
  292.3 29.3 %collective-permute-start.39 = (bf16[512,1536]{1,0:T(8,128)(2,1)}, bf16[512,1536]{1,0:T(8,128)(2,1)S(1)}, u32[]{:S(2)}, u32[]{:S(2)}) collective-permute-start(bf16[512,1536]{1,0:T(8,128)(2,1)} %pad_maximum_fusion.11), channel_id=1, source_target_pairs={{0,1},{1,0},{2,3},{3,2},{4,5},{5,4},{6,7},{7,6},{8,9},{9,8},{10,11... | collective-permute-start | bytes 4718600 | tf_op jit(solution)/shard_map/ppermute | solution.py:52
  296.6 283.5 %reduce-scatter.7.cloned.1.call-start = ((), (), s32[]{:S(2)}) async-start(), calls=%async_computation.11 | async-start | bytes 3440640 | tf_op jit(solution)/shard_map/reduce_scatter | solution.py:144
  335.7 32.1 %collective-permute-start.40 = (bf16[4,256,128]{2,1,0:T(8,128)(2,1)}, bf16[4,256,128]{2,1,0:T(8,128)(2,1)}, u32[]{:S(2)}, u32[]{:S(2)}) collective-permute-start(bf16[4,256,128]{2,1,0:T(8,128)(2,1)} %pad_maximum_fusion.52), channel_id=1, source_target_pairs={{0,2},{2,4},{4,6},{1,3},{3,5},{5,7},{8,10},{10,12},{12,14},{9,11},... | collective-permute-start | bytes 786440 | tf_op jit(solution)/shard_map/ppermute | solution.py:61
  433.7 28.8 %collective-permute-start.50 = (bf16[512,1536]{1,0:T(8,128)(2,1)}, bf16[512,1536]{1,0:T(8,128)(2,1)}, u32[]{:S(2)}, u32[]{:S(2)}) collective-permute-start(bf16[512,1536]{1,0:T(8,128)(2,1)} %pad_maximum_fusion.12), channel_id=1, source_target_pairs={{0,1},{1,0},{2,3},{3,2},{4,5},{5,4},{6,7},{7,6},{8,9},{9,8},{10,11... | collective-permute-start | bytes 4718600 | tf_op jit(solution)/shard_map/ppermute | solution.py:52
  485.6 189.8 %reduce-scatter.9.cloned.1.call-start = ((), (), s32[]{:S(2)}) async-start(), calls=%async_computation.12 | async-start | bytes 6881280 | tf_op jit(solution)/shard_map/reduce_scatter | solution.py:144
  528.2 266.7 %reduce-scatter.13.cloned.1.call-start = ((), (), s32[]{:S(2)}) async-start(), calls=%async_computation.14 | async-start | bytes 1966080 | tf_op jit(solution)/shard_map/reduce_scatter | solution.py:144
  610.2 44.0 %collective-permute-start.69 = (bf16[4,256,128]{2,1,0:T(8,128)(2,1)}, bf16[4,256,128]{2,1,0:T(8,128)(2,1)}, u32[]{:S(2)}, u32[]{:S(2)}) collective-permute-start(bf16[4,256,128]{2,1,0:T(8,128)(2,1)} %get-tuple-element.281), channel_id=1, source_target_pairs={{4,0},{6,2},{5,1},{7,3},{12,8},{14,10},{13,9},{15,11},{20,16},{22,... | collective-permute-start | bytes 786440 | tf_op jit(solution)/shard_map/ppermute | solution.py:61
  611.5 42.7 %collective-permute-start.68 = (bf16[4,256,128]{2,1,0:T(8,128)(2,1)}, bf16[4,256,128]{2,1,0:T(8,128)(2,1)}, u32[]{:S(2)}, u32[]{:S(2)}) collective-permute-start(bf16[4,256,128]{2,1,0:T(8,128)(2,1)} %get-tuple-element.279), channel_id=1, source_target_pairs={{2,0},{4,2},{6,4},{3,1},{5,3},{7,5},{10,8},{12,10},{14,12},{11,9},... | collective-permute-start | bytes 786440 | tf_op jit(solution)/shard_map/ppermute | solution.py:61
  679.9 39.0 %collective-permute-start.66 = (bf16[128,1536]{1,0:T(8,128)(2,1)S(1)}, bf16[128,1536]{1,0:T(8,128)(2,1)S(1)}, u32[]{:S(2)}, u32[]{:S(2)}) collective-permute-start(bf16[128,1536]{1,0:T(8,128)(2,1)S(1)} %get-tuple-element.222), channel_id=1, source_target_pairs={{0,8},{8,0},{16,24},{24,16},{1,9},{9,1},{17,25},{25,17},{2,10},{10... | collective-permute-start | bytes 1179656 | tf_op jit(solution)/shard_map/ppermute | solution.py:52
  681.4 37.5 %collective-permute-start.65 = (bf16[128,1536]{1,0:T(8,128)(2,1)S(1)}, bf16[128,1536]{1,0:T(8,128)(2,1)S(1)}, u32[]{:S(2)}, u32[]{:S(2)}) collective-permute-start(bf16[128,1536]{1,0:T(8,128)(2,1)S(1)} %get-tuple-element.223), channel_id=1, source_target_pairs={{0,16},{8,24},{16,0},{24,8},{1,17},{9,25},{17,1},{25,9},{2,18},{10... | collective-permute-start | bytes 1179656 | tf_op jit(solution)/shard_map/ppermute | solution.py:52
  690.3 27.6 %collective-permute-start.73 = (bf16[128,1536]{1,0:T(8,128)(2,1)S(1)}, bf16[128,1536]{1,0:T(8,128)(2,1)S(1)}, u32[]{:S(2)}, u32[]{:S(2)}) collective-permute-start(bf16[128,1536]{1,0:T(8,128)(2,1)S(1)} %get-tuple-element.217), channel_id=1, source_target_pairs={{0,16},{8,24},{16,0},{24,8},{1,17},{9,25},{17,1},{25,9},{2,18},{10... | collective-permute-start | bytes 1179656 | tf_op jit(solution)/shard_map/ppermute | solution.py:52
  690.8 27.1 %collective-permute-start.72 = (bf16[128,1536]{1,0:T(8,128)(2,1)S(1)}, bf16[128,1536]{1,0:T(8,128)(2,1)S(1)}, u32[]{:S(2)}, u32[]{:S(2)}) collective-permute-start(bf16[128,1536]{1,0:T(8,128)(2,1)S(1)} %get-tuple-element.215), channel_id=1, source_target_pairs={{0,24},{8,16},{16,8},{24,0},{1,25},{9,17},{17,9},{25,1},{2,26},{10... | collective-permute-start | bytes 1179656 | tf_op jit(solution)/shard_map/ppermute | solution.py:52
  727.3 94.7 %reduce-scatter.11.cloned.1.call-start = ((), (), s32[]{:S(2)}) async-start(), calls=%async_computation.13 | async-start | bytes 3440640 | tf_op jit(solution)/shard_map/reduce_scatter | solution.py:144
  751.8 210.9 %reduce-scatter.17.cloned.1.call-start = ((), (), s32[]{:S(2)}) async-start(), calls=%async_computation.16 | async-start | bytes 6881280 | tf_op jit(solution)/shard_map/reduce_scatter | solution.py:144
  782.7 213.1 %reduce-scatter.15.cloned.1.call-start = ((), (), s32[]{:S(2)}) async-start(), calls=%async_computation.15 | async-start | bytes 2949120 | tf_op jit(solution)/shard_map/reduce_scatter | solution.py:144
  791.3 33.3 %collective-permute-start.82 = (bf16[128,1536]{1,0:T(8,128)(2,1)S(1)}, bf16[128,1536]{1,0:T(8,128)(2,1)S(1)}, u32[]{:S(2)}, u32[]{:S(2)}) collective-permute-start(bf16[128,1536]{1,0:T(8,128)(2,1)S(1)} %get-tuple-element.213), channel_id=1, source_target_pairs={{0,8},{8,0},{16,24},{24,16},{1,9},{9,1},{17,25},{25,17},{2,10},{10... | collective-permute-start | bytes 1179656 | tf_op jit(solution)/shard_map/ppermute | solution.py:52
  792.9 31.8 %collective-permute-start.81 = (bf16[128,1536]{1,0:T(8,128)(2,1)S(1)}, bf16[128,1536]{1,0:T(8,128)(2,1)S(1)}, u32[]{:S(2)}, u32[]{:S(2)}) collective-permute-start(bf16[128,1536]{1,0:T(8,128)(2,1)S(1)} %get-tuple-element.214), channel_id=1, source_target_pairs={{0,16},{8,24},{16,0},{24,8},{1,17},{9,25},{17,1},{25,9},{2,18},{10... | collective-permute-start | bytes 1179656 | tf_op jit(solution)/shard_map/ppermute | solution.py:52
  794.0 30.7 %collective-permute-start.80 = (bf16[128,1536]{1,0:T(8,128)(2,1)S(1)}, bf16[128,1536]{1,0:T(8,128)(2,1)}, u32[]{:S(2)}, u32[]{:S(2)}) collective-permute-start(bf16[128,1536]{1,0:T(8,128)(2,1)S(1)} %get-tuple-element.212), channel_id=1, source_target_pairs={{0,24},{8,16},{16,8},{24,0},{1,25},{9,17},{17,9},{25,1},{2,26},{10... | collective-permute-start | bytes 1179656 | tf_op jit(solution)/shard_map/ppermute | solution.py:52
  868.7 27.3 %collective-permute-start.106 = (bf16[96,512]{1,0:T(8,128)(2,1)}, bf16[96,512]{1,0:T(8,128)(2,1)}, u32[]{:S(2)}, u32[]{:S(2)}) collective-permute-start(bf16[96,512]{1,0:T(8,128)(2,1)} %get-tuple-element.309), channel_id=1, source_target_pairs={{0,24},{8,16},{16,8},{24,0},{1,25},{9,17},{17,9},{25,1},{2,26},{10... | collective-permute-start | bytes 294920 | tf_op jit(solution)/shard_map/ppermute | solution.py:52
  870.4 26.5 %collective-permute-start.105 = (bf16[96,512]{1,0:T(8,128)(2,1)}, bf16[96,512]{1,0:T(8,128)(2,1)}, u32[]{:S(2)}, u32[]{:S(2)}) collective-permute-start(bf16[96,512]{1,0:T(8,128)(2,1)} %get-tuple-element.310), channel_id=1, source_target_pairs={{0,16},{8,24},{16,0},{24,8},{1,17},{9,25},{17,1},{25,9},{2,18},{10... | collective-permute-start | bytes 294920 | tf_op jit(solution)/shard_map/ppermute | solution.py:52
  (308 other events, 3835.7 us)
Sparse Core Ops, SparseCore 0:
  22.6 50.7 all-gather.5
  75.6 102.2 all-gather.7
  180.0 55.2 all-gather.9
  237.3 81.6 all-gather.11
  320.5 113.5 all-gather.13
  485.8 72.6 reduce-scatter.6
  560.8 114.6 reduce-scatter.8
  727.4 39.0 reduce-scatter.12
  768.8 53.1 reduce-scatter.10
  824.1 97.9 reduce-scatter.16
  925.0 49.9 reduce-scatter.14

commit v6 on v4

--- a/solution.py
+++ b/solution.py
@@ -299,7 +299,7 @@
     return hidden + out, stored, parts
 
 
-def mixer_backward(team, core, back_out, stored, gain, weights, taps):
+def mixer_backward(team, core, back_out, stored, gain, weights, taps, before):
     inverse, normed, tokens, gate_in, gate_out, value, padded, convolved, gated, one_back, two_back = stored
     channels = taps.shape[1]
     back_tokens = gather_tokens(team, back_out.astype(bf16))
@@ -327,7 +327,7 @@
         ]
     )
     term = jnp.concatenate([outer(tokens, back_parts), outer(back_tokens, gated)], axis=-1)
-    back_hidden, gain_term = after_norm(back_out, back_normed, normed, inverse, gain)
+    back_hidden, gain_term = after_norm(back_out, back_normed, normed, inverse, held(gain, before))
     return back_hidden, gain_term, term, tap_term, back_gated
 
 
@@ -643,14 +643,14 @@
     back, first_gain_term, *first_part = feed_backward(
         first_team, back, first_back_tokens, first_stored, gains[1], first_lift_all, first_drop_all, first_mask, attend_part
     )
+    first_total = every_seat(first_team, jnp.concatenate(first_part[::-1], axis=-1))
     back, mixer_gain_term, mixer_term, tap_term, back_gated = mixer_backward(
-        team, core, back, mixer_stored, gains[0], mixer_weights, taps
+        team, core, back, mixer_stored, gains[0], mixer_weights, taps, first_total
     )
     mixer_part = summed_rows(team, mixer_term)
     gated_done = zero(back_gated)
     second_total = every_seat(second_team, jnp.concatenate(second_part[::-1], axis=-1), gated_done)
     attend_total = every_seat(team, attend_part, gated_done)
-    first_total = every_seat(first_team, jnp.concatenate(first_part[::-1], axis=-1))
     mixer_total = every_seat(team, mixer_part)
 
     small = jnp.concatenate(

time: 1020 us -> 1120 us (1.098)
  waiting for transfers between devices: 434 us -> 545 us
    reduce_scatter x6, waiting for transfers between devices: 33.2 us -> 143 us  [summed_rows(): lax.psum_scatter(split.reshape(-1, columns), team.across, scatter_dimensi...]
    unnamed x471 -> x467, local copies, waits for them, and re-layouts: 33 us -> 33.5 us
  transfers between devices with their start and end apart: 121 -> 121, of which waited for: 57 -> 64; matrix products, arithmetic and copies ran while one was open for 35% -> 30% of each run, Pallas kernels for 3% -> 3%
where the time goes in v6:
time: 1120 us; the launch traced here: 1110 us
  waiting for transfers between devices  545 us (49%)
  matrix products  160 us (14%)
  local copies, waits for them, and re-layouts  142 us (13%)
  starting transfers between devices  125 us (11%)
  other arithmetic  81.2 us (7%)
  Pallas kernels  31.2 us (3%)
  between operations  26.2 us (2%)
    ppermute x102, waiting for transfers between devices, swap(): lax.ppermute(array, axis, [(i, i ^ mask) for i in range(lax.axis_size(axi...  319 us
    dot_general x48, matrix products, dot(): return jnp.einsum(pattern, first, second, preferred_element_type=f32)  160 us
    reduce_scatter x6, waiting for transfers between devices, summed_rows(): lax.psum_scatter(split.reshape(-1, columns), team.across, scatter_dimensi...  143 us
    ppermute x102, starting transfers between devices, swap(): lax.ppermute(array, axis, [(i, i ^ mask) for i in range(lax.axis_size(axi...  108 us
    ppermute x8, waiting for transfers between devices, shift(): lax.ppermute(array, 'seq', [(i, i + by) for i in range(count) if 0 <= i +...  57.8 us
    unnamed x467, local copies, waits for them, and re-layouts  33.5 us
    pallas_call x2, Pallas kernels, attend_call(): pl.pallas_call(kernel, grid=(sequences,), in_specs=[pl.BlockSpec(memory_s...  31.2 us
    all_gather x5, waiting for transfers between devices, all_rows(): whole = lax.all_gather(near, team.across, axis=len(lead) + 1, tiled=True)  25.1 us
  transfers between devices with their start and end apart: 121, of which 64 were waited for; matrix products, arithmetic and copies ran while one was open for 30% of the time, Pallas kernels for 3%

profile of v6, /device:TPU:0, one launch (start us, length us, event | category | flops | bytes accessed | tf_op | source)
XLA Modules:
  0.0 1110.8 jit_solution(10942280292270644205)
XLA Ops:
  40.1 20.4 %collective-permute-done.23 = bf16[96,2688]{1,0:T(8,128)(2,1)S(1)} collective-permute-done((bf16[96,2688]{1,0:T(8,128)(2,1)S(1)}, bf16[96,2688]{1,0:T(8,128)(2,1)S(1)}, u32[]{:S(2)}, u32[]{:S(2)}) %collective-permute-start.23) | collective-permute-done | bytes 516128 | tf_op jit(solution)/shard_map/ppermute | solution.py:52
  77.4 7.4 collective-permute-done.1
  158.3 7.9 collective-permute-done.19
  168.5 7.1 collective-permute-done.17
  185.0 18.3 %collective-permute-done.36 = bf16[96,2688]{1,0:T(8,128)(2,1)} collective-permute-done((bf16[96,2688]{1,0:T(8,128)(2,1)}, bf16[96,2688]{1,0:T(8,128)(2,1)}, u32[]{:S(2)}, u32[]{:S(2)}) %collective-permute-start.36) | collective-permute-done | bytes 516128 | tf_op jit(solution)/shard_map/ppermute | solution.py:52
  250.9 7.3 collective-permute-done.29
  258.3 8.8 collective-permute-done.28
  274.9 8.1 collective-permute-done.32
  296.8 22.2 %all-gather.12.cloned.1.call-done = bf16[4,384,1408]{2,1,0:T(8,128)(2,1)} async-done(((bf16[4,96,1408]{2,1,0:T(8,128)(2,1)}), bf16[4,384,1408]{2,1,0:T(8,128)(2,1)}) %all-gather.12.cloned.1.call-update) | async-done | bytes 4325392 | tf_op jit(solution)/shard_map/all_gather | solution.py:129
  345.5 11.2 %collective-permute-done.41 = bf16[4,256,128]{2,1,0:T(8,128)(2,1)} collective-permute-done((bf16[4,256,128]{2,1,0:T(8,128)(2,1)}, bf16[4,256,128]{2,1,0:T(8,128)(2,1)}, u32[]{:S(2)}, u32[]{:S(2)}) %collective-permute-start.41) | collective-permute-done | bytes 262176 | tf_op jit(solution)/shard_map/ppermute | solution.py:61
  356.8 10.9 collective-permute-done.40
  370.2 12.3 %shard_map.322 = bf16[4,256,192]{2,1,0:T(8,128)(2,1)} custom-call(s32[1]{0:T(128)} %bitcast.50.base_ref, s32[4,1,256]{2,1,0:T(1,128)} %reshape.725.order_ref, bf16[4,256,192]{2,1,0:T(8,128)(2,1)} %copy.190.query_ref, bf16[4,1024,128]{2,1,0:T(8,128)(2,1)} %pad_maximum_fusion.34.slots_ref), custom_call_target="tpu_custom_call" | custom-call | flops 2013265920 | bytes 1441792 | tf_op jit(solution)/shard_map/pallas_call | solution.py:400
  394.8 8.5 collective-permute-done.46
  403.3 9.0 collective-permute-done.45
  417.7 8.3 collective-permute-done.49
  437.6 9.4 collective-permute-done.54
  446.9 8.0 collective-permute-done.53
  498.1 9.0 fusion.29
  534.8 8.5 collective-permute-done.59
  543.3 8.8 collective-permute-done.58
  557.8 9.5 collective-permute-done.62
  588.3 18.9 %shard_map.323 = (f32[4,256,192]{2,1,0:T(8,128)}, f32[4,256,128]{2,1,0:T(8,128)}, bf16[4,768,128]{2,1,0:T(8,128)(2,1)}) custom-call(s32[1]{0:T(128)} %bitcast.50.base_ref, s32[4,1,256]{2,1,0:T(1,128)} %reshape.725.order_ref, bf16[4,256,192]{2,1,0:T(8,128)(2,1)} %copy.190.query_ref, bf16[4,256,192]{2,1,0:T(8,128)(2,1)} %fusion.34.back_ref, ...), custom_call_target="tpu_custom_call" | custom-call | flops 2013265920 | bytes 1835008 | tf_op jit(solution)/shard_map/pallas_call | solution.py:400
  627.9 30.6 %collective-permute-done.69 = bf16[4,256,128]{2,1,0:T(8,128)(2,1)} collective-permute-done((bf16[4,256,128]{2,1,0:T(8,128)(2,1)}, bf16[4,256,128]{2,1,0:T(8,128)(2,1)}, u32[]{:S(2)}, u32[]{:S(2)}) %collective-permute-start.69) | collective-permute-done | bytes 262176 | tf_op jit(solution)/shard_map/ppermute | solution.py:61
  687.5 6.9 collective-permute-done.74
  695.3 15.2 %collective-permute-done.73 = bf16[128,1536]{1,0:T(8,128)(2,1)S(1)} collective-permute-done((bf16[128,1536]{1,0:T(8,128)(2,1)S(1)}, bf16[128,1536]{1,0:T(8,128)(2,1)S(1)}, u32[]{:S(2)}, u32[]{:S(2)}) %collective-permute-start.73) | collective-permute-done | bytes 393248 | tf_op jit(solution)/shard_map/ppermute | solution.py:52
  720.1 7.2 collective-permute-done.77
  778.9 39.1 %reduce-scatter.11.cloned.1.call-done = bf16[384,896]{1,0:T(8,128)(2,1)} async-done(((bf16[1536,896]{1,0:T(8,128)(2,1)}), bf16[384,896]{1,0:T(8,128)(2,1)}) %reduce-scatter.11.cloned.1.call-update) | async-done | bytes 688144 | tf_op jit(solution)/shard_map/reduce_scatter | solution.py:144
  818.0 100.0 %reduce-scatter.15.cloned.1.call-done = bf16[384,1792]{1,0:T(8,128)(2,1)} async-done(((bf16[1536,1792]{1,0:T(8,128)(2,1)}), bf16[384,1792]{1,0:T(8,128)(2,1)}) %reduce-scatter.15.cloned.1.call-update) | async-done | bytes 1376272 | tf_op jit(solution)/shard_map/reduce_scatter | solution.py:144
  937.6 7.7 collective-permute-done.93
  954.8 7.4 collective-permute-done.80
  968.2 9.0 collective-permute-done.85
  1051.0 8.5 collective-permute-done.91
  (1009 shorter events, 613.2 us)
Async XLA Ops:
  7.2 110.6 %all-gather.6.cloned.1.call-start = ((), (), s32[]{:S(2)}) async-start(), calls=%async_computation.6 | async-start | bytes 2949120 | tf_op jit(solution)/shard_map/all_gather | solution.py:129
  22.5 195.1 %all-gather.8.cloned.1.call-start = ((), (), s32[]{:S(2)}) async-start(), calls=%async_computation.7 | async-start | bytes 6881280 | tf_op jit(solution)/shard_map/all_gather | solution.py:129
  63.5 171.8 %all-gather.10.cloned.1.call-start = ((), (), s32[]{:S(2)}) async-start(), calls=%async_computation.8 | async-start | bytes 3440640 | tf_op jit(solution)/shard_map/all_gather | solution.py:129
  85.8 31.6 %collective-permute-start.11 = (bf16[512,1536]{1,0:T(8,128)(2,1)S(1)}, bf16[512,1536]{1,0:T(8,128)(2,1)S(1)}, u32[]{:S(2)}, u32[]{:S(2)}) collective-permute-start(bf16[512,1536]{1,0:T(8,128)(2,1)S(1)} %get-tuple-element.158), channel_id=1, source_target_pairs={{0,1},{1,0},{2,3},{3,2},{4,5},{5,4},{6,7},{7,6},{8,9},{9,8},{10,11... | collective-permute-start | bytes 4718600 | tf_op jit(solution)/shard_map/ppermute | solution.py:52
  143.0 37.0 %collective-permute-start.34 = (bf16[96,2688]{1,0:T(8,128)(2,1)}, bf16[96,2688]{1,0:T(8,128)(2,1)}, u32[]{:S(2)}, u32[]{:S(2)}) collective-permute-start(bf16[96,2688]{1,0:T(8,128)(2,1)} %pad_maximum_fusion.43), channel_id=1, source_target_pairs={{0,8},{8,0},{16,24},{24,16},{1,9},{9,1},{17,25},{25,17},{2,10},{10... | collective-permute-start | bytes 1548296 | tf_op jit(solution)/shard_map/ppermute | solution.py:52
  148.9 170.2 %all-gather.12.cloned.1.call-start = ((), (), s32[]{:S(2)}) async-start(), calls=%async_computation.9 | async-start | bytes 5406720 | tf_op jit(solution)/shard_map/all_gather | solution.py:129
  155.9 47.3 %collective-permute-start.36 = (bf16[96,2688]{1,0:T(8,128)(2,1)}, bf16[96,2688]{1,0:T(8,128)(2,1)}, u32[]{:S(2)}, u32[]{:S(2)}) collective-permute-start(bf16[96,2688]{1,0:T(8,128)(2,1)} %pad_maximum_fusion.44), channel_id=1, source_target_pairs={{0,16},{8,24},{16,0},{24,8},{1,17},{9,25},{17,1},{25,9},{2,18},{10... | collective-permute-start | bytes 1548296 | tf_op jit(solution)/shard_map/ppermute | solution.py:52
  166.1 40.2 %collective-permute-start.38 = (bf16[96,2688]{1,0:T(8,128)(2,1)}, bf16[96,2688]{1,0:T(8,128)(2,1)}, u32[]{:S(2)}, u32[]{:S(2)}) collective-permute-start(bf16[96,2688]{1,0:T(8,128)(2,1)} %pad_maximum_fusion.45), channel_id=1, source_target_pairs={{0,24},{8,16},{16,8},{24,0},{1,25},{9,17},{17,9},{25,1},{2,26},{10... | collective-permute-start | bytes 1548296 | tf_op jit(solution)/shard_map/ppermute | solution.py:52
  177.1 33.4 %collective-permute-start.22 = (bf16[128,1536]{1,0:T(8,128)(2,1)}, bf16[128,1536]{1,0:T(8,128)(2,1)}, u32[]{:S(2)}, u32[]{:S(2)}) collective-permute-start(bf16[128,1536]{1,0:T(8,128)(2,1)} %multiply_convert_fusion.20), channel_id=1, source_target_pairs={{0,24},{8,16},{16,8},{24,0},{1,25},{9,17},{17,9},{25,1},{2,26},{10... | collective-permute-start | bytes 1179656 | tf_op jit(solution)/shard_map/ppermute | solution.py:52
  178.5 33.2 %collective-permute-start.21 = (bf16[128,1536]{1,0:T(8,128)(2,1)}, bf16[128,1536]{1,0:T(8,128)(2,1)}, u32[]{:S(2)}, u32[]{:S(2)}) collective-permute-start(bf16[128,1536]{1,0:T(8,128)(2,1)} %multiply_convert_fusion.20), channel_id=1, source_target_pairs={{0,16},{8,24},{16,0},{24,8},{1,17},{9,25},{17,1},{25,9},{2,18},{10... | collective-permute-start | bytes 1179656 | tf_op jit(solution)/shard_map/ppermute | solution.py:52
  180.0 31.7 %collective-permute-start.20 = (bf16[128,1536]{1,0:T(8,128)(2,1)}, bf16[128,1536]{1,0:T(8,128)(2,1)}, u32[]{:S(2)}, u32[]{:S(2)}) collective-permute-start(bf16[128,1536]{1,0:T(8,128)(2,1)} %multiply_convert_fusion.20), channel_id=1, source_target_pairs={{0,8},{8,0},{16,24},{24,16},{1,9},{9,1},{17,25},{25,17},{2,10},{10... | collective-permute-start | bytes 1179656 | tf_op jit(solution)/shard_map/ppermute | solution.py:52
  217.4 239.0 %all-gather.14.cloned.1.call-start = ((), (), s32[]{:S(2)}) async-start(), calls=%async_computation.10 | async-start | bytes 6881280 | tf_op jit(solution)/shard_map/all_gather | solution.py:129
  292.3 29.4 %collective-permute-start.39 = (bf16[512,1536]{1,0:T(8,128)(2,1)}, bf16[512,1536]{1,0:T(8,128)(2,1)S(1)}, u32[]{:S(2)}, u32[]{:S(2)}) collective-permute-start(bf16[512,1536]{1,0:T(8,128)(2,1)} %pad_maximum_fusion.11), channel_id=1, source_target_pairs={{0,1},{1,0},{2,3},{3,2},{4,5},{5,4},{6,7},{7,6},{8,9},{9,8},{10,11... | collective-permute-start | bytes 4718600 | tf_op jit(solution)/shard_map/ppermute | solution.py:52
  296.6 283.9 %reduce-scatter.7.cloned.1.call-start = ((), (), s32[]{:S(2)}) async-start(), calls=%async_computation.11 | async-start | bytes 3440640 | tf_op jit(solution)/shard_map/reduce_scatter | solution.py:144
  335.7 32.0 %collective-permute-start.40 = (bf16[4,256,128]{2,1,0:T(8,128)(2,1)}, bf16[4,256,128]{2,1,0:T(8,128)(2,1)}, u32[]{:S(2)}, u32[]{:S(2)}) collective-permute-start(bf16[4,256,128]{2,1,0:T(8,128)(2,1)} %pad_maximum_fusion.52), channel_id=1, source_target_pairs={{0,2},{2,4},{4,6},{1,3},{3,5},{5,7},{8,10},{10,12},{12,14},{9,11},... | collective-permute-start | bytes 786440 | tf_op jit(solution)/shard_map/ppermute | solution.py:61
  433.9 28.8 %collective-permute-start.50 = (bf16[512,1536]{1,0:T(8,128)(2,1)}, bf16[512,1536]{1,0:T(8,128)(2,1)}, u32[]{:S(2)}, u32[]{:S(2)}) collective-permute-start(bf16[512,1536]{1,0:T(8,128)(2,1)} %pad_maximum_fusion.12), channel_id=1, source_target_pairs={{0,1},{1,0},{2,3},{3,2},{4,5},{5,4},{6,7},{7,6},{8,9},{9,8},{10,11... | collective-permute-start | bytes 4718600 | tf_op jit(solution)/shard_map/ppermute | solution.py:52
  478.1 189.9 %reduce-scatter.9.cloned.1.call-start = ((), (), s32[]{:S(2)}) async-start(), calls=%async_computation.12 | async-start | bytes 6881280 | tf_op jit(solution)/shard_map/reduce_scatter | solution.py:144
  516.0 259.8 %reduce-scatter.13.cloned.1.call-start = ((), (), s32[]{:S(2)}) async-start(), calls=%async_computation.14 | async-start | bytes 1966080 | tf_op jit(solution)/shard_map/reduce_scatter | solution.py:144
  610.5 48.0 %collective-permute-start.69 = (bf16[4,256,128]{2,1,0:T(8,128)(2,1)}, bf16[4,256,128]{2,1,0:T(8,128)(2,1)}, u32[]{:S(2)}, u32[]{:S(2)}) collective-permute-start(bf16[4,256,128]{2,1,0:T(8,128)(2,1)} %get-tuple-element.283), channel_id=1, source_target_pairs={{4,0},{6,2},{5,1},{7,3},{12,8},{14,10},{13,9},{15,11},{20,16},{22,... | collective-permute-start | bytes 786440 | tf_op jit(solution)/shard_map/ppermute | solution.py:61
  611.8 46.7 %collective-permute-start.68 = (bf16[4,256,128]{2,1,0:T(8,128)(2,1)}, bf16[4,256,128]{2,1,0:T(8,128)(2,1)}, u32[]{:S(2)}, u32[]{:S(2)}) collective-permute-start(bf16[4,256,128]{2,1,0:T(8,128)(2,1)} %get-tuple-element.281), channel_id=1, source_target_pairs={{2,0},{4,2},{6,4},{3,1},{5,3},{7,5},{10,8},{12,10},{14,12},{11,9},... | collective-permute-start | bytes 786440 | tf_op jit(solution)/shard_map/ppermute | solution.py:61
  672.5 39.0 %collective-permute-start.66 = (bf16[128,1536]{1,0:T(8,128)(2,1)S(1)}, bf16[128,1536]{1,0:T(8,128)(2,1)S(1)}, u32[]{:S(2)}, u32[]{:S(2)}) collective-permute-start(bf16[128,1536]{1,0:T(8,128)(2,1)S(1)} %get-tuple-element.224), channel_id=1, source_target_pairs={{0,8},{8,0},{16,24},{24,16},{1,9},{9,1},{17,25},{25,17},{2,10},{10... | collective-permute-start | bytes 1179656 | tf_op jit(solution)/shard_map/ppermute | solution.py:52
  674.0 37.5 %collective-permute-start.65 = (bf16[128,1536]{1,0:T(8,128)(2,1)S(1)}, bf16[128,1536]{1,0:T(8,128)(2,1)S(1)}, u32[]{:S(2)}, u32[]{:S(2)}) collective-permute-start(bf16[128,1536]{1,0:T(8,128)(2,1)S(1)} %get-tuple-element.225), channel_id=1, source_target_pairs={{0,16},{8,24},{16,0},{24,8},{1,17},{9,25},{17,1},{25,9},{2,18},{10... | collective-permute-start | bytes 1179656 | tf_op jit(solution)/shard_map/ppermute | solution.py:52
  682.9 27.6 %collective-permute-start.73 = (bf16[128,1536]{1,0:T(8,128)(2,1)S(1)}, bf16[128,1536]{1,0:T(8,128)(2,1)S(1)}, u32[]{:S(2)}, u32[]{:S(2)}) collective-permute-start(bf16[128,1536]{1,0:T(8,128)(2,1)S(1)} %get-tuple-element.219), channel_id=1, source_target_pairs={{0,16},{8,24},{16,0},{24,8},{1,17},{9,25},{17,1},{25,9},{2,18},{10... | collective-permute-start | bytes 1179656 | tf_op jit(solution)/shard_map/ppermute | solution.py:52
  683.5 27.1 %collective-permute-start.72 = (bf16[128,1536]{1,0:T(8,128)(2,1)S(1)}, bf16[128,1536]{1,0:T(8,128)(2,1)S(1)}, u32[]{:S(2)}, u32[]{:S(2)}) collective-permute-start(bf16[128,1536]{1,0:T(8,128)(2,1)S(1)} %get-tuple-element.217), channel_id=1, source_target_pairs={{0,24},{8,16},{16,8},{24,0},{1,25},{9,17},{17,9},{25,1},{2,26},{10... | collective-permute-start | bytes 1179656 | tf_op jit(solution)/shard_map/ppermute | solution.py:52
  719.9 98.0 %reduce-scatter.11.cloned.1.call-start = ((), (), s32[]{:S(2)}) async-start(), calls=%async_computation.13 | async-start | bytes 3440640 | tf_op jit(solution)/shard_map/reduce_scatter | solution.py:144
  744.5 173.4 %reduce-scatter.15.cloned.1.call-start = ((), (), s32[]{:S(2)}) async-start(), calls=%async_computation.15 | async-start | bytes 6881280 | tf_op jit(solution)/shard_map/reduce_scatter | solution.py:144
  767.0 324.4 %reduce-scatter.17.cloned.1.call-start = ((), (), s32[]{:S(2)}) async-start(), calls=%async_computation.16 | async-start | bytes 2949120 | tf_op jit(solution)/shard_map/reduce_scatter | solution.py:144
  774.1 149.1 %collective-permute-start.79 = (bf16[512,1536]{1,0:T(8,128)(2,1)}, bf16[512,1536]{1,0:T(8,128)(2,1)S(1)}, u32[]{:S(2)}, u32[]{:S(2)}) collective-permute-start(bf16[512,1536]{1,0:T(8,128)(2,1)} %convolution_convert_fusion.1), channel_id=1, source_target_pairs={{0,1},{1,0},{2,3},{3,2},{4,5},{5,4},{6,7},{7,6},{8,9},{9,8},{10,11... | collective-permute-start | bytes 4718600 | tf_op jit(solution)/shard_map/ppermute | solution.py:52
  928.4 26.4 %collective-permute-start.82 = (bf16[128,1536]{1,0:T(8,128)(2,1)S(1)}, bf16[128,1536]{1,0:T(8,128)(2,1)S(1)}, u32[]{:S(2)}, u32[]{:S(2)}) collective-permute-start(bf16[128,1536]{1,0:T(8,128)(2,1)S(1)} %get-tuple-element.215), channel_id=1, source_target_pairs={{0,8},{8,0},{16,24},{24,16},{1,9},{9,1},{17,25},{25,17},{2,10},{10... | collective-permute-start | bytes 1179656 | tf_op jit(solution)/shard_map/ppermute | solution.py:52
  929.9 24.8 %collective-permute-start.81 = (bf16[128,1536]{1,0:T(8,128)(2,1)S(1)}, bf16[128,1536]{1,0:T(8,128)(2,1)S(1)}, u32[]{:S(2)}, u32[]{:S(2)}) collective-permute-start(bf16[128,1536]{1,0:T(8,128)(2,1)S(1)} %get-tuple-element.216), channel_id=1, source_target_pairs={{0,16},{8,24},{16,0},{24,8},{1,17},{9,25},{17,1},{25,9},{2,18},{10... | collective-permute-start | bytes 1179656 | tf_op jit(solution)/shard_map/ppermute | solution.py:52
  935.3 26.9 %collective-permute-start.80 = (bf16[128,1536]{1,0:T(8,128)(2,1)S(1)}, bf16[128,1536]{1,0:T(8,128)(2,1)S(1)}, u32[]{:S(2)}, u32[]{:S(2)}) collective-permute-start(bf16[128,1536]{1,0:T(8,128)(2,1)S(1)} %get-tuple-element.214), channel_id=1, source_target_pairs={{0,24},{8,16},{16,8},{24,0},{1,25},{9,17},{17,9},{25,1},{2,26},{10... | collective-permute-start | bytes 1179656 | tf_op jit(solution)/shard_map/ppermute | solution.py:52
  1005.7 25.8 %collective-permute-start.109 = (bf16[96,2688]{1,0:T(8,128)(2,1)}, bf16[96,2688]{1,0:T(8,128)(2,1)}, u32[]{:S(2)}, u32[]{:S(2)}) collective-permute-start(bf16[96,2688]{1,0:T(8,128)(2,1)} %get-tuple-element.198), channel_id=1, source_target_pairs={{0,24},{8,16},{16,8},{24,0},{1,25},{9,17},{17,9},{25,1},{2,26},{10... | collective-permute-start | bytes 1548296 | tf_op jit(solution)/shard_map/ppermute | solution.py:52
  (310 other events, 3780.0 us)
Sparse Core Ops, SparseCore 0:
  22.6 50.7 all-gather.5
  75.6 102.2 all-gather.7
  180.0 55.2 all-gather.9
  237.3 81.6 all-gather.11
  320.5 113.5 all-gather.13
  478.3 72.7 reduce-scatter.6
  553.4 114.5 reduce-scatter.8
  720.0 42.4 reduce-scatter.12
  764.8 53.0 reduce-scatter.10
  820.1 97.7 reduce-scatter.14
  1026.4 49.4 reduce-scatter.16
